TPU v7x, 32 devices: a whole 2x2x4 slice. The times are simulated.
32 devices in a mesh: gx: 8 (over z, x), trait: 4 (over y, core).
Axes of the slice: x: 2, y: 2, z: 4, core: 2. Of those that a mesh axis runs over, the one named last changes fastest.
Arguments:
- initial: float32 [64, 128, 1024], P('gx', None, 'trait'), may hold values from 0.2 to 2
- section_one: float32 [64, 128, 1024], P('gx', None, 'trait'), may hold values from 0.2 to 2
- section_two: float32 [64, 128, 1024], P('gx', None, 'trait'), may hold values from 0.2 to 2
- kernels: bfloat16 [2, 1024, 1024], P(None, None, 'trait'), may hold values from -0.1875 to 0.1875
- growth: float32 [1024], P('trait'), may hold values from -3 to 3
- death_rate: float32 [1024], P('trait'), may hold values from 0.5 to 8
Outputs:
- new_one: float32 [64, 128, 1024], P('gx', None, 'trait')
- new_two: float32 [64, 128, 1024], P('gx', None, 'trait')
All inputs are finite; a program needn't handle non-finite values.
Results may differ from a plain program's by a relative error of at most 0.002.
Values may be sent and summed in bfloat16 or wider, within the bound.
No kernel may reach another device: no remote copies, remote signals or barrier semaphores. Data moves between devices by JAX's collectives and lax.ppermute only.
A program may use at most 64 MiB of HBM per device.

v0:
```python
import jax
import jax.numpy as jnp
from jax import lax
from jax.sharding import PartitionSpec as P

DIFFUSION = 0.25
STEP_SIZE = 0.5


def with_halo(cells, sides, width):
    for axis, dim in sides:
        count = lax.axis_size(axis)
        head = lax.slice_in_dim(cells, 0, width, axis=dim)
        tail = lax.slice_in_dim(cells, cells.shape[dim] - width, cells.shape[dim], axis=dim)
        cells = jnp.concatenate(
            [
                lax.ppermute(tail, axis, [(i, (i + 1) % count) for i in range(count)]),
                cells,
                lax.ppermute(head, axis, [((i + 1) % count, i) for i in range(count)]),
            ],
            axis=dim,
        )
    return cells


def local(initial, section_one, section_two, kernels, growth, death_rate):
    first_dt = STEP_SIZE / 3.0
    second_dt = 2.0 * STEP_SIZE / 3.0

    def products(core):
        xcount, ycount, owned = core.shape
        flat = core.astype(jnp.bfloat16).reshape(xcount * ycount, owned)
        piece = lax.all_gather(flat, "trait", axis=1, tiled=True)
        compete = jnp.dot(piece, kernels[0], preferred_element_type=jnp.float32)
        mutate = jnp.dot(piece, kernels[1], preferred_element_type=jnp.float32)
        compete = compete.astype(jnp.bfloat16)
        mutate = mutate.astype(jnp.bfloat16)
        return (
            compete.astype(jnp.float32).reshape(xcount, ycount, owned),
            mutate.astype(jnp.float32).reshape(xcount, ycount, owned),
        )

    def explicit(padded):
        core = padded[1:-1]
        lapl = padded[2:] + padded[:-2] + jnp.roll(core, 1, 1) + jnp.roll(core, -1, 1) - 4.0 * core
        compete, mutate = products(core)
        return DIFFUSION * lapl + core * (growth - compete) + mutate - core

    padded_pair = with_halo(jnp.stack([section_one, section_two]), (("gx", 1),), 1)
    expl_one = explicit(padded_pair[0])
    expl_two = explicit(padded_pair[1])
    full_one = expl_one - death_rate * section_one
    full_two = expl_two - death_rate * section_two
    result = (
        initial
        + first_dt * death_rate * section_one
        + STEP_SIZE * (5.0 / 12.0 * full_one - 1.0 / 12.0 * full_two)
    ) / (1.0 + first_dt * death_rate)
    new_one, full_one, full_two = (result, full_one, full_two)
    padded_new = with_halo(new_one, (("gx", 0),), 1)
    expl_new = explicit(padded_new)
    new_two = (
        new_one
        + second_dt * (expl_new - expl_one)
        + second_dt * death_rate * section_two
        + STEP_SIZE / 3.0 * (full_one + full_two)
    ) / (1.0 + second_dt * death_rate)
    return (new_one, new_two)


def solution(mesh):
    in_specs = (
        P("gx", None, "trait"),
        P("gx", None, "trait"),
        P("gx", None, "trait"),
        P(None, None, "trait"),
        P("trait"),
        P("trait"),
    )
    out_specs = (P("gx", None, "trait"), P("gx", None, "trait"))
    return jax.shard_map(local, mesh=mesh, in_specs=in_specs, out_specs=out_specs, check_vma=False)
```

profile of v0, /device:TPU:0, one launch (start us, length us, event | category | flops | bytes accessed | tf_op | source)
XLA Modules:
  0.0 105.0 jit_solution(6749250892413294128)
XLA Ops:
  7.2 0.0 all-gather.4.cloned.1.call-start
  7.2 2.2 %convert_element_type.41 = bf16[8,128,256]{2,1,0:T(8,128)(2,1)} convert(f32[8,128,256]{2,1,0:T(8,128)} %param.7) | non-fusion elementwise | flops 262144 | bytes 1572864 | tf_op jit(solution)/shard_map/convert_element_type | solution.py:32
  9.4 0.0 all-gather.4.cloned.1.call-update
  9.5 0.0 copy-start.15
  9.5 0.0 all-gather.6.cloned.1.call-start
  9.5 0.8 convert_element_type.45
  10.4 0.0 all-gather.6.cloned.1.call-update
  10.4 0.0 all-gather.8.cloned.1.call-start
  10.5 6.0 %collective-permute-start = (f32[2,1,128,256]{3,2,1,0:T(8,128)S(1)}, f32[2,1,128,256]{3,2,1,0:T(8,128)S(1)}, u32[]{:S(2)}, u32[]{:S(2)}) collective-permute-start(f32[2,1,128,256]{3,2,1,0:T(8,128)S(1)} %get-tuple-element.6), channel_id=1, source_target_pairs={{4,0},{8,4},{12,8},{16,12},{20,16},{24,20},{28,24},{0,28},{5,1},{9... | collective-permute-start | bytes 786440 | tf_op jit(solution)/shard_map/ppermute | solution.py:19
  16.6 0.0 collective-permute-start.1
  16.6 0.6 broadcast_multiply_fusion
  17.2 2.2 %fusion.54 = (f32[8,127,256]{2,1,0:T(8,128)}, f32[8,127,256]{2,1,0:T(8,128)}, f32[8,127,256]{2,1,0:T(8,128)}, f32[8,127,256]{2,1,0:T(8,128)}) fusion(f32[8,128,256]{2,1,0:T(8,128)S(1)} %copy-done.1, f32[8,128,256]{2,1,0:T(8,128)S(1)} %copy-done), kind=kLoop, calls=%fused_computation.76 | loop fusion | bytes 8323072 | tf_op jit(solution)/shard_map/jit(_roll_static)/slice | solution.py:45
  19.4 15.8 %all-gather.4.cloned.1.call-done = bf16[1024,1024]{1,0:T(8,128)(2,1)} async-done(((bf16[1024,256]{1,0:T(8,128)(2,1)}), bf16[1024,1024]{1,0:T(8,128)(2,1)}) %all-gather.4.cloned.1.call-update) | async-done | bytes 2097168 | tf_op jit(solution)/shard_map/all_gather | solution.py:33
  35.2 3.3 %convolution_convert_fusion.4 = bf16[1024,256]{1,0:T(8,128)(2,1)} fusion(bf16[1024,1024]{1,0:T(8,128)(2,1)} %all-gather.4.cloned.1.call-done, bf16[2,1024,256]{2,1,0:T(8,128)(2,1)} %param.9), kind=kOutput, calls=%fused_computation.4 | convolution fusion | flops 537133056 | bytes 3145728 | tf_op jit(solution)/shard_map/dot_general | solution.py:35
  38.5 1.5 %convolution_convert_fusion.5 = bf16[1024,256]{1,0:T(8,128)(2,1)} fusion(bf16[1024,1024]{1,0:T(8,128)(2,1)S(1)} %copy-done.21, bf16[2,1024,256]{2,1,0:T(8,128)(2,1)S(1)} %copy-done.24), kind=kOutput, calls=%fused_computation.5 | convolution fusion | flops 537133056 | bytes 3145728 | tf_op jit(solution)/shard_map/dot_general | solution.py:34
  40.0 19.6 %all-gather.6.cloned.1.call-done = bf16[1024,1024]{1,0:T(8,128)(2,1)} async-done(((bf16[1024,256]{1,0:T(8,128)(2,1)}), bf16[1024,1024]{1,0:T(8,128)(2,1)}) %all-gather.6.cloned.1.call-update) | async-done | bytes 2097168 | tf_op jit(solution)/shard_map/all_gather | solution.py:33
  59.6 2.5 %convolution_convert_fusion.2 = bf16[1024,256]{1,0:T(8,128)(2,1)S(1)} fusion(bf16[1024,1024]{1,0:T(8,128)(2,1)} %all-gather.6.cloned.1.call-done, bf16[2,1024,256]{2,1,0:T(8,128)(2,1)} %param.9), kind=kOutput, calls=%fused_computation.2 | convolution fusion | flops 537133056 | bytes 3145728 | tf_op jit(solution)/shard_map/dot_general | solution.py:35
  62.1 0.1 copy-done.25
  62.3 0.0 copy-start.11
  62.3 0.0 copy-start.17
  62.3 0.7 convolution_convert_fusion.3
  63.0 0.0 collective-permute-done
  63.0 0.0 collective-permute-done.1
  63.0 0.7 copy-done.14
  63.7 0.0 copy-done.8
  63.8 0.4 copy-done.9
  64.2 0.3 copy-done.10
  64.5 0.3 copy-done.11
  64.8 0.1 copy-done.12
  64.9 0.2 copy-done.13
  65.1 3.5 %fusion.47 = (bf16[8,128,256]{2,1,0:T(8,128)(2,1)}, f32[8,128,256]{2,1,0:T(8,128)S(1)}, f32[8,128,256]{2,1,0:T(8,128)}, f32[8,128,256]{2,1,0:T(8,128)}) fusion(f32[256]{0:T(256)S(1)} %get-tuple-element.23, f32[8,128,256]{2,1,0:T(8,128)S(1)} %copy-done, f32[256]{0:T(256)S(1)} %copy-done.15, f32[8,128,256]{2,1,0:T(8,128)S(1)} %copy-done.11, ...), kind=kLoop, calls=%fused_computation.71 | loop fusion | flops 13369344 | bytes 15732736 | tf_op jit(solution)/shard_map/convert_element_type | solution.py:32
  68.6 0.0 all-gather.8.cloned.1.call-update
  68.7 0.7 fusion.52
  69.4 4.2 %collective-permute-start.2 = (f32[1,128,256]{2,1,0:T(8,128)}, f32[1,128,256]{2,1,0:T(8,128)S(1)}, u32[]{:S(2)}, u32[]{:S(2)}) collective-permute-start(f32[1,128,256]{2,1,0:T(8,128)} %get-tuple-element.12), channel_id=1, source_target_pairs={{4,0},{8,4},{12,8},{16,12},{20,16},{24,20},{28,24},{0,28},{5,1},{9... | collective-permute-start | bytes 393224 | tf_op jit(solution)/shard_map/ppermute | solution.py:19
  73.7 1.5 %fusion.50 = (f32[8,127,256]{2,1,0:T(8,128)}, f32[8,127,256]{2,1,0:T(8,128)}) fusion(f32[8,128,256]{2,1,0:T(8,128)S(1)} %get-tuple-element.3), kind=kLoop, calls=%fused_computation.72 | loop fusion | bytes 4161536 | tf_op jit(solution)/shard_map/jit(_roll_static)/slice | solution.py:45
  75.2 16.5 %all-gather.8.cloned.1.call-done = bf16[1024,1024]{1,0:T(8,128)(2,1)} async-done(((bf16[1024,256]{1,0:T(8,128)(2,1)}), bf16[1024,1024]{1,0:T(8,128)(2,1)}) %all-gather.8.cloned.1.call-update) | async-done | bytes 2097168 | tf_op jit(solution)/shard_map/all_gather | solution.py:33
  91.7 2.5 %convolution_convert_fusion = bf16[1024,256]{1,0:T(8,128)(2,1)S(1)} fusion(bf16[1024,1024]{1,0:T(8,128)(2,1)} %all-gather.8.cloned.1.call-done, bf16[2,1024,256]{2,1,0:T(8,128)(2,1)} %param.9), kind=kOutput, calls=%fused_computation | convolution fusion | flops 537133056 | bytes 3145728 | tf_op jit(solution)/shard_map/dot_general | solution.py:35
  94.2 0.1 copy-done.26
  94.3 0.0 copy-start.16
  94.3 0.0 copy-start.18
  94.4 0.7 convolution_convert_fusion.1
  95.1 0.0 collective-permute-done.2
  95.1 0.0 collective-permute-done.3
  95.1 0.4 copy-done.3
  95.5 0.3 copy-done.4
  95.9 0.3 copy-done.5
  96.2 0.3 copy-done.6
  96.5 2.0 %fusion.13 = f32[8,128,256]{2,1,0:T(8,128)} fusion(f32[8,128,256]{2,1,0:T(8,128)S(1)} %get-tuple-element.3, f32[8,128,256]{2,1,0:T(8,128)S(1)} %copy-done.3, f32[1,128,256]{2,1,0:T(8,128)S(1)} %collective-permute-done.3, f32[1,128,256]{2,1,0:T(8,128)S(1)} %collective-permute-done.2, f32[8,127,256]{2,1,0:T(8,128)S(1)} %copy-done.6, ...), kind=kLoop, calls=%fused_computation.20 | loop fusion | flops 7340032 | bytes 9703424 | tf_op jit(solution)/shard_map/div | solution.py:62
  (40 shorter events, 0.1 us)
Async XLA Ops:
  7.2 3.3 %copy-start = (f32[8,128,256]{2,1,0:T(8,128)S(1)}, f32[8,128,256]{2,1,0:T(8,128)}, u32[]{:S(2)}) copy-start(f32[8,128,256]{2,1,0:T(8,128)} %param.7) | copy-start | bytes 3145732
  7.2 2.4 %copy-start.1 = (f32[8,128,256]{2,1,0:T(8,128)S(1)}, f32[8,128,256]{2,1,0:T(8,128)}, u32[]{:S(2)}) copy-start(f32[8,128,256]{2,1,0:T(8,128)} %param.8) | copy-start | bytes 3145732
  7.2 28.0 %all-gather.4.cloned.1.call-start = ((), (), s32[]{:S(2)}) async-start(), calls=%async_computation | async-start | bytes 2621440 | tf_op jit(solution)/shard_map/all_gather | solution.py:33
  9.5 7.1 %copy-start.15 = (f32[256]{0:T(256)S(1)}, f32[256]{0:T(256)}, u32[]{:S(2)}) copy-start(f32[256]{0:T(256)} %param.11) | copy-start | bytes 3076
  9.5 50.1 %all-gather.6.cloned.1.call-start = ((), (), s32[]{:S(2)}) async-start(), calls=%async_computation.1 | async-start | bytes 2621440 | tf_op jit(solution)/shard_map/all_gather | solution.py:33
  10.4 81.2 %all-gather.8.cloned.1.call-start = ((), (), s32[]{:S(2)}) async-start(), calls=%async_computation.2 | async-start | bytes 2621440 | tf_op jit(solution)/shard_map/all_gather | solution.py:33
  10.5 52.5 %collective-permute-start = (f32[2,1,128,256]{3,2,1,0:T(8,128)S(1)}, f32[2,1,128,256]{3,2,1,0:T(8,128)S(1)}, u32[]{:S(2)}, u32[]{:S(2)}) collective-permute-start(f32[2,1,128,256]{3,2,1,0:T(8,128)S(1)} %get-tuple-element.6), channel_id=1, source_target_pairs={{4,0},{8,4},{12,8},{16,12},{20,16},{24,20},{28,24},{0,28},{5,1},{9... | collective-permute-start | bytes 786440 | tf_op jit(solution)/shard_map/ppermute | solution.py:19
  16.6 46.5 %collective-permute-start.1 = (f32[2,1,128,256]{3,2,1,0:T(8,128)S(1)}, f32[2,1,128,256]{3,2,1,0:T(8,128)S(1)}, u32[]{:S(2)}, u32[]{:S(2)}) collective-permute-start(f32[2,1,128,256]{3,2,1,0:T(8,128)S(1)} %get-tuple-element.7), channel_id=1, source_target_pairs={{0,4},{4,8},{8,12},{12,16},{16,20},{20,24},{24,28},{28,0},{1,5},{5... | collective-permute-start | bytes 786440 | tf_op jit(solution)/shard_map/ppermute | solution.py:17
  35.2 3.3 %copy-start.21 = (bf16[1024,1024]{1,0:T(8,128)(2,1)S(1)}, bf16[1024,1024]{1,0:T(8,128)(2,1)}, u32[]{:S(2)}) copy-start(bf16[1024,1024]{1,0:T(8,128)(2,1)} %all-gather.4.cloned.1.call-done) | copy-start | bytes 6291460
  35.2 3.3 %copy-start.24 = (bf16[2,1024,256]{2,1,0:T(8,128)(2,1)S(1)}, bf16[2,1024,256]{2,1,0:T(8,128)(2,1)}, u32[]{:S(2)}) copy-start(bf16[2,1024,256]{2,1,0:T(8,128)(2,1)} %param.9) | copy-start | bytes 3145732
  59.6 2.5 %copy-start.22 = (bf16[1024,1024]{1,0:T(8,128)(2,1)S(1)}, bf16[1024,1024]{1,0:T(8,128)(2,1)}, u32[]{:S(2)}) copy-start(bf16[1024,1024]{1,0:T(8,128)(2,1)} %all-gather.6.cloned.1.call-done) | copy-start | bytes 6291460
  59.6 2.6 %copy-start.25 = (bf16[2,1024,256]{2,1,0:T(8,128)(2,1)S(1)}, bf16[2,1024,256]{2,1,0:T(8,128)(2,1)}, u32[]{:S(2)}) copy-start(bf16[2,1024,256]{2,1,0:T(8,128)(2,1)} %param.9) | copy-start | bytes 3145732
  62.2 1.5 %copy-start.7 = (f32[8,127,256]{2,1,0:T(8,128)S(1)}, f32[8,127,256]{2,1,0:T(8,128)}, u32[]{:S(2)}) copy-start(f32[8,127,256]{2,1,0:T(8,128)} %get-tuple-element.16) | copy-start | bytes 3121156
  62.2 1.5 %copy-start.8 = (f32[8,127,256]{2,1,0:T(8,128)S(1)}, f32[8,127,256]{2,1,0:T(8,128)}, u32[]{:S(2)}) copy-start(f32[8,127,256]{2,1,0:T(8,128)} %get-tuple-element.17) | copy-start | bytes 3121156
  62.2 1.9 %copy-start.9 = (f32[8,127,256]{2,1,0:T(8,128)S(1)}, f32[8,127,256]{2,1,0:T(8,128)}, u32[]{:S(2)}) copy-start(f32[8,127,256]{2,1,0:T(8,128)} %get-tuple-element.28) | copy-start | bytes 3121156
  62.2 2.3 %copy-start.10 = (f32[8,127,256]{2,1,0:T(8,128)S(1)}, f32[8,127,256]{2,1,0:T(8,128)}, u32[]{:S(2)}) copy-start(f32[8,127,256]{2,1,0:T(8,128)} %get-tuple-element.29) | copy-start | bytes 3121156
  62.3 2.6 %copy-start.11 = (f32[8,128,256]{2,1,0:T(8,128)S(1)}, f32[8,128,256]{2,1,0:T(8,128)}, u32[]{:S(2)}) copy-start(f32[8,128,256]{2,1,0:T(8,128)} %param.6) | copy-start | bytes 3145732
  62.3 2.7 %copy-start.12 = (bf16[1024,256]{1,0:T(8,128)(2,1)S(1)}, bf16[1024,256]{1,0:T(8,128)(2,1)}, u32[]{:S(2)}) copy-start(bf16[1024,256]{1,0:T(8,128)(2,1)} %convolution_convert_fusion.4) | copy-start | bytes 1572868
  62.3 2.8 %copy-start.13 = (bf16[1024,256]{1,0:T(8,128)(2,1)S(1)}, bf16[1024,256]{1,0:T(8,128)(2,1)}, u32[]{:S(2)}) copy-start(bf16[1024,256]{1,0:T(8,128)(2,1)} %convolution_convert_fusion.5) | copy-start | bytes 1572868
  62.3 2.8 %copy-start.17 = (f32[256]{0:T(256)S(1)}, f32[256]{0:T(256)}, u32[]{:S(2)}) copy-start(f32[256]{0:T(256)} %param.10) | copy-start | bytes 3076
  63.0 0.7 copy-start.14
  68.6 26.5 %copy-start.2 = (f32[8,128,256]{2,1,0:T(8,128)}, f32[8,128,256]{2,1,0:T(8,128)S(1)}, u32[]{:S(2)}) copy-start(f32[8,128,256]{2,1,0:T(8,128)S(1)} %get-tuple-element.3) | copy-start | bytes 3145732
  69.4 25.7 %collective-permute-start.2 = (f32[1,128,256]{2,1,0:T(8,128)}, f32[1,128,256]{2,1,0:T(8,128)S(1)}, u32[]{:S(2)}, u32[]{:S(2)}) collective-permute-start(f32[1,128,256]{2,1,0:T(8,128)} %get-tuple-element.12), channel_id=1, source_target_pairs={{4,0},{8,4},{12,8},{16,12},{20,16},{24,20},{28,24},{0,28},{5,1},{9... | collective-permute-start | bytes 393224 | tf_op jit(solution)/shard_map/ppermute | solution.py:19
  73.6 21.4 %collective-permute-start.3 = (f32[1,128,256]{2,1,0:T(8,128)S(1)}, f32[1,128,256]{2,1,0:T(8,128)S(1)}, u32[]{:S(2)}, u32[]{:S(2)}) collective-permute-start(f32[1,128,256]{2,1,0:T(8,128)S(1)} %get-tuple-element.13), channel_id=1, source_target_pairs={{0,4},{4,8},{8,12},{12,16},{16,20},{20,24},{24,28},{28,0},{1,5},{5... | collective-permute-start | bytes 393224 | tf_op jit(solution)/shard_map/ppermute | solution.py:17
  91.7 2.5 %copy-start.23 = (bf16[1024,1024]{1,0:T(8,128)(2,1)S(1)}, bf16[1024,1024]{1,0:T(8,128)(2,1)}, u32[]{:S(2)}) copy-start(bf16[1024,1024]{1,0:T(8,128)(2,1)} %all-gather.8.cloned.1.call-done) | copy-start | bytes 6291460
  91.7 2.6 %copy-start.26 = (bf16[2,1024,256]{2,1,0:T(8,128)(2,1)S(1)}, bf16[2,1024,256]{2,1,0:T(8,128)(2,1)}, u32[]{:S(2)}) copy-start(bf16[2,1024,256]{2,1,0:T(8,128)(2,1)} %param.9) | copy-start | bytes 3145732
  94.3 1.2 %copy-start.3 = (f32[8,128,256]{2,1,0:T(8,128)S(1)}, f32[8,128,256]{2,1,0:T(8,128)}, u32[]{:S(2)}) copy-start(f32[8,128,256]{2,1,0:T(8,128)} %get-tuple-element.4) | copy-start | bytes 3145732
  94.3 1.5 %copy-start.4 = (f32[8,128,256]{2,1,0:T(8,128)S(1)}, f32[8,128,256]{2,1,0:T(8,128)}, u32[]{:S(2)}) copy-start(f32[8,128,256]{2,1,0:T(8,128)} %get-tuple-element.5) | copy-start | bytes 3145732
  94.3 1.9 %copy-start.5 = (f32[8,127,256]{2,1,0:T(8,128)S(1)}, f32[8,127,256]{2,1,0:T(8,128)}, u32[]{:S(2)}) copy-start(f32[8,127,256]{2,1,0:T(8,128)} %get-tuple-element.8) | copy-start | bytes 3121156
  94.3 2.2 %copy-start.6 = (f32[8,127,256]{2,1,0:T(8,128)S(1)}, f32[8,127,256]{2,1,0:T(8,128)}, u32[]{:S(2)}) copy-start(f32[8,127,256]{2,1,0:T(8,128)} %get-tuple-element.9) | copy-start | bytes 3121156
  94.3 2.2 %copy-start.16 = (f32[256]{0:T(256)S(1)}, f32[256]{0:T(256)}, u32[]{:S(2)}) copy-start(f32[256]{0:T(256)} %param.11) | copy-start | bytes 3076
  94.3 2.2 %copy-start.18 = (f32[256]{0:T(256)S(1)}, f32[256]{0:T(256)}, u32[]{:S(2)}) copy-start(f32[256]{0:T(256)} %param.10) | copy-start | bytes 3076
  94.3 2.1 %copy-start.19 = (f32[256]{0:T(256)S(1)}, f32[256]{0:T(256)}, u32[]{:S(2)}) copy-start(f32[256]{0:T(256)} %get-tuple-element.22) | copy-start | bytes 3076
  94.4 2.1 %copy-start.20 = (f32[256]{0:T(256)S(1)}, f32[256]{0:T(256)}, u32[]{:S(2)}) copy-start(f32[256]{0:T(256)} %get-tuple-element.24) | copy-start | bytes 3076
Sparse Core Ops, SparseCore 0:
  9.6 25.5 all-gather.3
  36.7 22.8 all-gather.5
  68.8 22.8 all-gather.7
where the time goes:
time: 105 us
  waiting for transfers between devices  51.9 us (49%)
  between operations  14 us (13%)
  matrix products  11.3 us (11%)
  starting transfers between devices  10.4 us (10%)
  other arithmetic  9.25 us (9%)
  local copies, waits for them, and re-layouts  8.14 us (8%)
    all_gather x3, waiting for transfers between devices, products(): piece = lax.all_gather(flat, 'trait', axis=1, tiled=True)  51.9 us
    ppermute x2, starting transfers between devices, with_halo(): lax.ppermute(head, axis, [((i + 1) % count, i) for i in range(count)])  10.3 us
    dot_general x3, matrix products, products(): mutate = jnp.dot(piece, kernels[1], preferred_element_type=jnp.float32)  8.39 us
    convert_element_type x3, other arithmetic, products(): flat = core.astype(jnp.bfloat16).reshape(xcount * ycount, owned)  6.6 us
    unnamed x54, local copies, waits for them, and re-layouts  3.71 us
    dot_general x3, matrix products, products(): compete = jnp.dot(piece, kernels[0], preferred_element_type=jnp.float32)  2.94 us
    slice x2, local copies, waits for them, and re-layouts, explicit(): jnp.roll(core, 1, 1)  2.2 us
  transfers between devices with their start and end apart: 7, of which 3 were waited for; matrix products, arithmetic and copies ran while one was open for 16% of the time, Pallas kernels for 0%

commit v1 on v0

v1 whole, which is shorter than its diff:
```python
import jax
import jax.numpy as jnp
from jax import lax
from jax.experimental import pallas as pl
from jax.experimental.pallas import tpu as pltpu
from jax.sharding import PartitionSpec as P

DIFFUSION = 0.25
STEP_SIZE = 0.5
FIRST = STEP_SIZE / 3.0
SECOND = 2.0 * STEP_SIZE / 3.0
F32 = jnp.float32
BF16 = jnp.bfloat16
VMEM_LIMIT = 28 * 1024 * 1024
SPEC = pl.BlockSpec(memory_space=pltpu.VMEM)
ANYWHERE = pl.BlockSpec(memory_space=pl.ANY)
FROM_HBM = pl.BlockSpec(memory_space=pltpu.HBM)


def chunks_of(xcount):
    last = max(1, 3 * xcount // 8)
    start = (xcount - last + 1) // 2
    middle = list(range(start, start + last))
    return [x for x in range(xcount) if x not in middle], middle


def after(value, *others):
    return lax.optimization_barrier((value, *others))[0]


def call(body, name, args, outs, scratch=(), specs=None, out_specs=None, gflop=0.0):
    specs = specs or [SPEC] * len(args)
    space = {id(SPEC): pltpu.VMEM, id(FROM_HBM): pltpu.HBM}
    args = [
        pltpu.with_memory_space_constraint(a, space[id(s)]) if id(s) in space else a for a, s in zip(args, specs)
    ]
    return pl.pallas_call(
        body,
        out_shape=outs,
        in_specs=specs,
        out_specs=out_specs or [SPEC] * len(outs),
        scratch_shapes=list(scratch),
        compiler_params=pltpu.CompilerParams(vmem_limit_bytes=VMEM_LIMIT),
        cost_estimate=pl.CostEstimate(flops=int(gflop * 1e9), bytes_accessed=0, transcendentals=0),
        name=name,
    )(*args)


def rows_of(refs, owned):
    return jnp.concatenate([r[...].reshape(-1, owned) for r in refs], axis=0)


def round_chunk(fields, cells, with_faces):
    xcount, ycount, owned = fields[0].shape
    count = len(fields)

    def body(*refs):
        field_refs = refs[:count]
        out = refs[count]
        held, sems = refs[-2:]
        copies = []
        for f in range(count):
            for i, x in enumerate(cells):
                copies.append(pltpu.make_async_copy(field_refs[f].at[x], held.at[f, i], sems.at[f, i]))
                copies[-1].start()
        for f in range(count):
            for i, x in enumerate(cells):
                copies[f * len(cells) + i].wait()
                value = held[f, i].astype(BF16)
                out[f, i * ycount:(i + 1) * ycount, :] = value
                if with_faces and x == 0:
                    refs[count + 1][f] = value
                if with_faces and x == xcount - 1:
                    refs[count + 2][f] = value

    outs = [pltpu.VMEM((count, len(cells) * ycount, owned), BF16)]
    if with_faces:
        outs += [pltpu.VMEM((count, ycount, owned), BF16)] * 2
    return call(
        body, "round_chunk", fields, outs,
        scratch=[pltpu.VMEM((count, len(cells), ycount, owned), F32), pltpu.SemaphoreType.DMA((count, len(cells)))],
        specs=[FROM_HBM] * count, gflop=0.0,
    )


def half_dot(near, other, kernels_ref, k, first, second):
    depth = near.shape[-1]
    lhs = jnp.concatenate([near, other], axis=-1)
    rhs = jnp.concatenate(
        [kernels_ref[k, pl.ds(pl.multiple_of(b * depth, depth), depth), :] for b in (first, second)], axis=0
    )
    return jnp.dot(lhs, rhs, preferred_element_type=F32)


def stencil(get, faces, x, xcount):
    core = get(x)
    before = get(x - 1) if x > 0 else faces[0]().astype(F32)
    behind = get(x + 1) if x < xcount - 1 else faces[1]().astype(F32)
    around = before + behind + pltpu.roll(core, 1, 0) + pltpu.roll(core, core.shape[0] - 1, 0)
    return DIFFUSION * around - 2.0 * core, core


def before_first(me, owns, sibs, one, two, lo, hi, kernels, growth, chunks):
    xcount, ycount, owned = one.shape
    count = len(chunks)

    def body(me_ref, *refs):
        own_refs, sib_refs = refs[:count], refs[count:2 * count]
        one_ref, two_ref, lo_ref, hi_ref, k_ref, g_ref = refs[2 * count:2 * count + 6]
        outs = refs[2 * count + 6:]
        me = me_ref[0]
        growth = g_ref[...]
        for c, cells in enumerate(chunks):
            part_ref, base_ref = outs[2 * c:2 * c + 2]
            rows = len(cells) * ycount
            near = own_refs[c][...].reshape(2 * rows, owned)
            other = sib_refs[c][...].reshape(2 * rows, owned)
            for k in range(2):
                part_ref[k] = half_dot(near, other, k_ref, k, me, me ^ 1)
            for f, ref in enumerate((one_ref, two_ref)):
                for i, x in enumerate(cells):
                    base, core = stencil(lambda x: ref[x], (lambda: lo_ref[f], lambda: hi_ref[f]), x, xcount)
                    base_ref[f, i] = base + core * growth

    outs = []
    for cells in chunks:
        outs.append(pltpu.VMEM((2, 2 * len(cells) * ycount, owned), F32))
        outs.append(pltpu.VMEM((2, len(cells), ycount, owned), F32))
    args = [me, *owns, *sibs, one, two, lo, hi, kernels, growth]
    flat = call(body, "before_first", args, outs, specs=[pl.BlockSpec(memory_space=pltpu.SMEM)] + [SPEC] * (len(args) - 1), gflop=20.0)
    return [flat[2 * c:2 * c + 2] for c in range(count)]


def first_node(me, far, farsib, part, base, one, two, initial, kernels, death, cells, with_faces):
    xcount, ycount, owned = one.shape
    rows = len(cells) * ycount

    def body(me_ref, far_ref, farsib_ref, part_ref, base_ref, one_ref, two_ref, init_ref, k_ref, d_ref, *refs):
        new_ref, rounded_ref, rest_ref = refs[:3]
        sums = refs[-1]
        me = me_ref[0]
        near = far_ref[...].reshape(2 * rows, owned)
        other = farsib_ref[...].reshape(2 * rows, owned)
        for k in range(2):
            sums[k] = (part_ref[k] + half_dot(near, other, k_ref, k, me ^ 2, me ^ 3)).astype(BF16)
        death = d_ref[...]
        inv_one = 1.0 / (1.0 + FIRST * death)
        inv_two = 1.0 / (1.0 + SECOND * death)
        for i, x in enumerate(cells):
            cores = (one_ref[x], two_ref[x])
            e = []
            for f in range(2):
                at = pl.ds(f * rows + i * ycount, ycount)
                e.append(base_ref[f, i] - cores[f] * sums[0, at, :].astype(F32) + sums[1, at, :].astype(F32))
            full_one = e[0] - death * cores[0]
            full_two = e[1] - death * cores[1]
            new = (
                init_ref[x]
                + FIRST * death * cores[0]
                + STEP_SIZE * (5.0 / 12.0 * full_one - 1.0 / 12.0 * full_two)
            ) * inv_one
            new_ref[i] = new
            rounded = new.astype(BF16)
            rounded_ref[0, i * ycount:(i + 1) * ycount, :] = rounded
            if with_faces and x == 0:
                refs[3][0] = rounded
            if with_faces and x == xcount - 1:
                refs[4][0] = rounded
            rest_ref[i] = (
                new - SECOND * e[0] + SECOND * death * cores[1] + STEP_SIZE / 3.0 * (full_one + full_two)
            ) * inv_two

    outs = [
        pltpu.VMEM((len(cells), ycount, owned), F32),
        pltpu.VMEM((1, rows, owned), BF16),
        pltpu.VMEM((len(cells), ycount, owned), F32),
    ]
    if with_faces:
        outs += [pltpu.VMEM((1, ycount, owned), BF16)] * 2
    args = [me, far, farsib, part, base, one, two, initial, kernels, death]
    return call(
        body, "first_node", args, outs, scratch=[pltpu.VMEM((2, 2 * rows, owned), BF16)],
        specs=[pl.BlockSpec(memory_space=pltpu.SMEM)] + [SPEC] * (len(args) - 1), gflop=0.0,
    )


def near_part(me, own, sib, kernels):
    rows, owned = own.shape[1:]

    def body(me_ref, own_ref, sib_ref, k_ref, part_ref):
        me = me_ref[0]
        near, other = rows_of([own_ref], owned), rows_of([sib_ref], owned)
        for k in range(2):
            part_ref[k] = half_dot(near, other, k_ref, k, me, me ^ 1)

    return call(
        body, "near_part", [me, own, sib, kernels], [pltpu.VMEM((2, rows, owned), F32)],
        specs=[pl.BlockSpec(memory_space=pltpu.SMEM)] + [SPEC] * 3, gflop=20.0,
    )[0]


def before_second(me, own, sib, news, rests, lo, hi, kernels, growth, death, chunks):
    _, ycount, owned = news[0].shape
    xcount = sum(len(cells) for cells in chunks)
    count = len(chunks)
    rows = own.shape[1]
    place = {x: (c, i) for c, cells in enumerate(chunks) for i, x in enumerate(cells)}

    def body(me_ref, own_ref, sib_ref, *refs):
        new_refs, rest_refs = refs[:count], refs[count:2 * count]
        lo_ref, hi_ref, k_ref, g_ref, d_ref, whole_ref, part_ref = refs[2 * count:2 * count + 7]
        base_refs, sems = refs[2 * count + 7:-1], refs[-1]
        copies = [
            pltpu.make_async_copy(new_refs[c].at[i], whole_ref.at[x], sems.at[x]) for x, (c, i) in place.items()
        ]
        for copy in copies:
            copy.start()
        me = me_ref[0]
        growth = g_ref[...]
        factor = SECOND / (1.0 + SECOND * d_ref[...])

        def get(x):
            c, i = place[x]
            return new_refs[c][i]

        near, other = rows_of([own_ref], owned), rows_of([sib_ref], owned)
        for k in range(2):
            part_ref[k] = half_dot(near, other, k_ref, k, me, me ^ 1)
        for c, cells in enumerate(chunks):
            for i, x in enumerate(cells):
                base, core = stencil(get, (lambda: lo_ref[0], lambda: hi_ref[0]), x, xcount)
                base_refs[c][i] = rest_refs[c][i] + factor * (base + core * growth)
        for copy in copies:
            copy.wait()

    outs = [jax.ShapeDtypeStruct((xcount, ycount, owned), F32), pltpu.VMEM((2, rows, owned), F32)]
    outs += [pltpu.VMEM((len(cells), ycount, owned), F32) for cells in chunks]
    args = [me, own, sib, *news, *rests, lo, hi, kernels, growth, death]
    return call(
        body, "before_second", args, outs, scratch=[pltpu.SemaphoreType.DMA((xcount,))],
        specs=[pl.BlockSpec(memory_space=pltpu.SMEM)] + [SPEC] * (len(args) - 1),
        out_specs=[ANYWHERE] + [SPEC] * (len(outs) - 1), gflop=20.0,
    )


def second_node(me, far, farsib, part, base, new, kernels, death, cells, xcount, previous=None):
    _, ycount, owned = new.shape
    rows = len(cells) * ycount
    others = previous[1] if previous else []

    def body(me_ref, far_ref, farsib_ref, part_ref, base_ref, new_ref, k_ref, d_ref, *refs):
        if previous:
            prev_ref, out_ref, sums, held, sems = refs
            copies = [pltpu.make_async_copy(prev_ref.at[i], out_ref.at[x], sems.at[x]) for i, x in enumerate(others)]
            for copy in copies:
                copy.start()
        else:
            out_ref, sums = refs
        me = me_ref[0]
        near = far_ref[...].reshape(rows, owned)
        other = farsib_ref[...].reshape(rows, owned)
        for k in range(2):
            sums[k] = (part_ref[k] + half_dot(near, other, k_ref, k, me ^ 2, me ^ 3)).astype(BF16)
        factor = SECOND / (1.0 + SECOND * d_ref[...])
        for i, x in enumerate(cells):
            at = pl.ds(i * ycount, ycount)
            value = base_ref[i] + factor * (sums[1, at, :].astype(F32) - new_ref[i] * sums[0, at, :].astype(F32))
            if previous:
                held[i] = value
                copies.append(pltpu.make_async_copy(held.at[i], out_ref.at[x], sems.at[x]))
                copies[-1].start()
            else:
                out_ref[i] = value
        if previous:
            for copy in copies:
                copy.wait()

    args = [me, far, farsib, part, base, new, kernels, death]
    specs = [pl.BlockSpec(memory_space=pltpu.SMEM)] + [SPEC] * (len(args) - 1)
    scratch = [pltpu.VMEM((2, rows, owned), BF16)]
    if previous:
        args.append(previous[0])
        specs.append(SPEC)
        outs = [jax.ShapeDtypeStruct((xcount, ycount, owned), F32)]
        scratch += [pltpu.VMEM((len(cells), ycount, owned), F32), pltpu.SemaphoreType.DMA((xcount,))]
    else:
        outs = [pltpu.VMEM((len(cells), ycount, owned), F32)]
    return call(
        body, "second_node", args, outs, scratch=scratch, specs=specs,
        out_specs=[ANYWHERE] if previous else None, gflop=0.0,
    )[0]


def local(initial, section_one, section_two, kernels, growth, death_rate):
    xcount, ycount, owned = section_one.shape
    traits = lax.axis_size("trait")
    gcount = lax.axis_size("gx")
    me = lax.axis_index("trait").reshape(1)
    growth = growth.reshape(1, owned)
    death = death_rate.reshape(1, owned)
    chunks = chunks_of(xcount)

    def to_sibling(v):
        return lax.ppermute(v, "trait", [(i, i ^ 1) for i in range(traits)])

    def to_far(v):
        return lax.ppermute(v, "trait", [(i, i ^ 2) for i in range(traits)])

    def faces(head, tail):
        lo = lax.ppermute(tail, "gx", [(i, (i + 1) % gcount) for i in range(gcount)])
        hi = lax.ppermute(head, "gx", [((i + 1) % gcount, i) for i in range(gcount)])
        return lo, hi

    own_a, head, tail = round_chunk((section_one, section_two), chunks[0], True)
    far_a = to_far(own_a)
    own_b = round_chunk((after(section_one, own_a), section_two), chunks[1], False)[0]
    far_b = to_far(own_b)
    head, tail, near_a, near_b = lax.optimization_barrier((head, tail, own_a, own_b))
    lo, hi = faces(head, tail)
    sib_a = to_sibling(near_a)
    sib_b = to_sibling(after(near_b, lo))
    (part_a, base_a), (part_b, base_b) = before_first(
        me, (own_a, own_b), (sib_a, sib_b), section_one, section_two, lo, hi, kernels, growth, chunks
    )

    farsib_a = to_sibling(far_a)
    new_a, rounded_a, rest_a, new_head, new_tail = first_node(
        me, far_a, farsib_a, part_a, base_a, section_one, section_two, initial, kernels, death, chunks[0], True
    )
    nfar_a = to_far(rounded_a)
    new_lo, new_hi = faces(new_head, new_tail)
    nsib_a = to_sibling(rounded_a)
    npart_a = near_part(me, after(rounded_a, new_lo, new_hi), nsib_a, kernels)

    far_b = after(far_b, rounded_a)
    farsib_b = to_sibling(far_b)
    new_b, rounded_b, rest_b = first_node(
        me, far_b, farsib_b, after(part_b, npart_a), base_b, section_one, section_two, initial, kernels, death,
        chunks[1], False,
    )
    nfar_b = to_far(rounded_b)
    nsib_b = to_sibling(rounded_b)
    nfar_a = after(nfar_a, rounded_b)
    nfarsib_a = to_sibling(nfar_a)
    new_one, npart_b, nbase_a, nbase_b = before_second(
        me, rounded_b, nsib_b, (new_a, new_b), (rest_a, rest_b), new_lo, new_hi, kernels, growth, death, chunks
    )
    two_a = second_node(me, nfar_a, nfarsib_a, npart_a, nbase_a, new_a, kernels, death, chunks[0], xcount)
    nfar_b = after(nfar_b, two_a)
    nfarsib_b = to_sibling(nfar_b)
    new_two = second_node(
        me, nfar_b, nfarsib_b, npart_b, nbase_b, new_b, kernels, death, chunks[1], xcount, (two_a, chunks[0])
    )
    return new_one, new_two


def solution(mesh):
    in_specs = (
        P("gx", None, "trait"),
        P("gx", None, "trait"),
        P("gx", None, "trait"),
        P(None, None, "trait"),
        P("trait"),
        P("trait"),
    )
    out_specs = (P("gx", None, "trait"), P("gx", None, "trait"))
    return jax.shard_map(local, mesh=mesh, in_specs=in_specs, out_specs=out_specs, check_vma=False)
```

time: 105 us -> 51.5 us (0.49)
  waiting for transfers between devices: 51.9 us -> 19.3 us
  Pallas kernels: 0 us -> 15 us
  between operations: 14 us -> 0.81 us
  matrix products: 11.3 us -> 0 us
  other arithmetic: 9.25 us -> 0 us
  local copies, waits for them, and re-layouts: 8.14 us -> 1.59 us
  starting transfers between devices: 10.4 us -> 14.4 us
    all_gather x3 -> x0, waiting for transfers between devices: 51.9 us -> none  [products(): piece = lax.all_gather(flat, 'trait', axis=1, tiled=True)]
    ppermute x4 -> x16, waiting for transfers between devices: 0.01 us -> 19.3 us  [the longest x2 8.28 us: faces(): lax.ppermute(tail, 'gx', [(i, (i + 1) % gcount) for i in range(gcount)])]
    pallas_call x0 -> x9, Pallas kernels: none -> 15 us  [call(): pl.pallas_call(body, out_shape=outs, in_specs=specs, out_specs=out_specs...]
    dot_general x6 -> x0, matrix products: 11.3 us -> none  [the longest x3 8.39 us: products(): mutate = jnp.dot(piece, kernels[1], preferred_element_type=jnp.float32)]
    convert_element_type x3 -> x0, other arithmetic: 6.6 us -> none  [products(): flat = core.astype(jnp.bfloat16).reshape(xcount * ycount, owned)]
    slice x5 -> x0, local copies, waits for them, and re-layouts: 4.43 us -> none  [the longest x2 2.2 us: explicit(): jnp.roll(core, 1, 1)]
    ppermute x4 -> x16, starting transfers between devices: 10.3 us -> 14.4 us  [the longest x4 6.01 us: to_far(): return lax.ppermute(v, 'trait', [(i, i ^ 2) for i in range(traits)])]
    unnamed x54 -> x16, local copies, waits for them, and re-layouts: 3.71 us -> 1.59 us
  transfers between devices with their start and end apart: 7 -> 16, of which waited for: 3 -> 9; matrix products, arithmetic and copies ran while one was open for 16% -> 0% of each run, Pallas kernels for 0% -> 22%
where the time goes in v1:
time: 51.5 us; the launch traced here: 51.2 us
  waiting for transfers between devices  19.3 us (37%)
  Pallas kernels  15 us (29%)
  starting transfers between devices  14.4 us (28%)
  local copies, waits for them, and re-layouts  1.59 us (3%)
  between operations  0.81 us (2%)
    pallas_call x9, Pallas kernels, call(): pl.pallas_call(body, out_shape=outs, in_specs=specs, out_specs=out_specs...  15 us
    ppermute x2, waiting for transfers between devices, faces(): lax.ppermute(tail, 'gx', [(i, (i + 1) % gcount) for i in range(gcount)])  8.28 us
    ppermute x4, waiting for transfers between devices, to_far(): return lax.ppermute(v, 'trait', [(i, i ^ 2) for i in range(traits)])  7.15 us
    ppermute x4, starting transfers between devices, to_far(): return lax.ppermute(v, 'trait', [(i, i ^ 2) for i in range(traits)])  6.01 us
    ppermute x2, starting transfers between devices, faces(): lax.ppermute(head, 'gx', [((i + 1) % gcount, i) for i in range(gcount)])  5.14 us
    ppermute x2, starting transfers between devices, faces(): lax.ppermute(tail, 'gx', [(i, (i + 1) % gcount) for i in range(gcount)])  2.92 us
    ppermute x8, waiting for transfers between devices, to_sibling(): return lax.ppermute(v, 'trait', [(i, i ^ 1) for i in range(traits)])  2.1 us
    ppermute x2, waiting for transfers between devices, faces(): lax.ppermute(head, 'gx', [((i + 1) % gcount, i) for i in range(gcount)])  1.8 us
  transfers between devices with their start and end apart: 16, of which 9 were waited for; matrix products, arithmetic and copies ran while one was open for 0% of the time, Pallas kernels for 22%

profile of v1, /device:TPU:0, one launch (start us, length us, event | category | flops | bytes accessed | tf_op | source)
XLA Modules:
  0.0 51.2 jit_solution(11176257555345439151)
XLA Ops:
  0.6 2.4 %round_chunk.2 = (bf16[2,640,256]{2,1,0:T(8,128)(2,1)}, bf16[2,128,256]{2,1,0:T(8,128)(2,1)}, bf16[2,128,256]{2,1,0:T(8,128)(2,1)S(1)}) custom-call(f32[8,128,256]{2,1,0:T(8,128)} %one_ref.3, f32[8,128,256]{2,1,0:T(8,128)} %two_ref.3), custom_call_target="tpu_custom_call" | custom-call | tf_op jit(solution)/shard_map/round_chunk/pallas_call | solution.py:37
  3.1 0.0 copy-start
  3.1 0.0 copy-start.1
  3.1 0.0 copy-start.7
  3.1 3.0 %collective-permute-start.1 = (bf16[2,640,256]{2,1,0:T(8,128)(2,1)}, bf16[2,640,256]{2,1,0:T(8,128)(2,1)}, u32[]{:S(2)}, u32[]{:S(2)}) collective-permute-start(bf16[2,640,256]{2,1,0:T(8,128)(2,1)} %get-tuple-element.36.refs_0_), channel_id=1, source_target_pairs={{0,2},{1,3},{2,0},{3,1},{4,6},{5,7},{6,4},{7,5},{8,10},{9,11},{10,... | collective-permute-start | bytes 1966088 | tf_op jit(solution)/shard_map/ppermute | solution.py:307
  6.1 1.3 %round_chunk.3.refs_1_ = bf16[2,384,256]{2,1,0:T(8,128)(2,1)S(1)} custom-call(f32[8,128,256]{2,1,0:T(8,128)} %one_ref.3, f32[8,128,256]{2,1,0:T(8,128)} %two_ref.3), custom_call_target="tpu_custom_call" | custom-call | tf_op jit(solution)/shard_map/round_chunk/pallas_call | solution.py:37
  7.4 0.1 collective-permute-start.3
  7.5 1.5 %collective-permute-start.4 = (bf16[2,128,256]{2,1,0:T(8,128)(2,1)S(1)}, bf16[2,128,256]{2,1,0:T(8,128)(2,1)S(1)}, u32[]{:S(2)}, u32[]{:S(2)}) collective-permute-start(bf16[2,128,256]{2,1,0:T(8,128)(2,1)S(1)} %get-tuple-element.38), channel_id=1, source_target_pairs={{0,4},{4,8},{8,12},{12,16},{16,20},{20,24},{24,28},{28,0},{1,5},{5... | collective-permute-start | bytes 393224 | tf_op jit(solution)/shard_map/ppermute | solution.py:310
  9.0 7.1 %collective-permute-done.4.refs_6_ = bf16[2,128,256]{2,1,0:T(8,128)(2,1)S(1)} collective-permute-done((bf16[2,128,256]{2,1,0:T(8,128)(2,1)S(1)}, bf16[2,128,256]{2,1,0:T(8,128)(2,1)S(1)}, u32[]{:S(2)}, u32[]{:S(2)}) %collective-permute-start.4) | collective-permute-done | bytes 131104 | tf_op jit(solution)/shard_map/ppermute | solution.py:310
  16.2 0.7 %copy-done.5 = bf16[2,128,256]{2,1,0:T(8,128)(2,1)} copy-done((bf16[2,128,256]{2,1,0:T(8,128)(2,1)}, bf16[2,128,256]{2,1,0:T(8,128)(2,1)S(1)}, u32[]{:S(2)}) %copy-start.5) | copy-done | bytes 131096
  16.8 0.0 collective-permute-start.5
  16.8 1.7 %collective-permute-start.6 = (bf16[2,128,256]{2,1,0:T(8,128)(2,1)}, bf16[2,128,256]{2,1,0:T(8,128)(2,1)}, u32[]{:S(2)}, u32[]{:S(2)}) collective-permute-start(bf16[2,128,256]{2,1,0:T(8,128)(2,1)} %get-tuple-element.40), channel_id=1, source_target_pairs={{4,0},{8,4},{12,8},{16,12},{20,16},{24,20},{28,24},{0,28},{5,1},{9... | collective-permute-start | bytes 393224 | tf_op jit(solution)/shard_map/ppermute | solution.py:311
  18.6 0.5 %collective-permute-start = (bf16[2,384,256]{2,1,0:T(8,128)(2,1)S(1)}, bf16[2,384,256]{2,1,0:T(8,128)(2,1)}, u32[]{:S(2)}, u32[]{:S(2)}) collective-permute-start(bf16[2,384,256]{2,1,0:T(8,128)(2,1)S(1)} %round_chunk.3.refs_1_), channel_id=1, source_target_pairs={{0,2},{1,3},{2,0},{3,1},{4,6},{5,7},{6,4},{7,5},{8,10},{9,11},{10,... | collective-permute-start | bytes 1179656 | tf_op jit(solution)/shard_map/ppermute | solution.py:307
  19.1 2.1 %collective-permute-done.1.far_ref = bf16[2,640,256]{2,1,0:T(8,128)(2,1)} collective-permute-done((bf16[2,640,256]{2,1,0:T(8,128)(2,1)}, bf16[2,640,256]{2,1,0:T(8,128)(2,1)}, u32[]{:S(2)}, u32[]{:S(2)}) %collective-permute-start.1) | collective-permute-done | bytes 655392 | tf_op jit(solution)/shard_map/ppermute | solution.py:307
  21.2 0.0 collective-permute-start.2
  21.2 1.8 %collective-permute-done.6.refs_7_ = bf16[2,128,256]{2,1,0:T(8,128)(2,1)} collective-permute-done((bf16[2,128,256]{2,1,0:T(8,128)(2,1)}, bf16[2,128,256]{2,1,0:T(8,128)(2,1)}, u32[]{:S(2)}, u32[]{:S(2)}) %collective-permute-start.6) | collective-permute-done | bytes 131104 | tf_op jit(solution)/shard_map/ppermute | solution.py:311
  23.0 0.0 collective-permute-done.5.refs_3_
  23.0 0.0 collective-permute-done.3.refs_2_
  23.1 0.9 %copy-done.6 = bf16[2,128,256]{2,1,0:T(8,128)(2,1)S(1)} copy-done((bf16[2,128,256]{2,1,0:T(8,128)(2,1)S(1)}, bf16[2,128,256]{2,1,0:T(8,128)(2,1)}, u32[]{:S(2)}) %copy-start.6) | copy-done | bytes 131096
  24.0 3.5 %before_first.1 = (f32[2,1280,256]{2,1,0:T(8,128)S(1)}, f32[2,5,128,256]{3,2,1,0:T(8,128)S(1)}, f32[2,768,256]{2,1,0:T(8,128)S(1)}, f32[2,3,128,256]{3,2,1,0:T(8,128)S(1)}) custom-call(s32[1]{0:T(128)} %bitcast.me_ref, bf16[2,640,256]{2,1,0:T(8,128)(2,1)} %get-tuple-element.36.refs_0_, bf16[2,384,256]{2,1,0:T(8,128)(2,1)S(1)} %round_chunk.3.refs_1_, ...), custom_call_target="tpu_custom_call" | custom-call | flops 20000000000 | tf_op jit(solution)/shard_map/before_first/pallas_call | solution.py:37
  27.5 0.0 collective-permute-done.2.farsib_ref
  27.5 0.0 copy-done.3
  27.5 0.0 copy-done.4
  27.5 2.5 %first_node.2 = (f32[5,128,256]{2,1,0:T(8,128)S(1)}, bf16[1,640,256]{2,1,0:T(8,128)(2,1)S(1)}, f32[5,128,256]{2,1,0:T(8,128)S(1)}, bf16[1,128,256]{2,1,0:T(8,128)(2,1)S(1)}, bf16[1,128,256]{2,1,0:T(8,128)(2,1)S(1)}) custom-call(s32[1]{0:T(128)} %bitcast.me_ref, bf16[2,640,256]{2,1,0:T(8,128)(2,1)} %collective-permute-done.1.far_ref, ...), custom_call_target="tpu_custom_call" | custom-call | tf_op jit(solution)/shard_map/first_node/pallas_call | solution.py:37
  30.1 0.1 collective-permute-start.10
  30.1 1.4 %collective-permute-start.8 = (bf16[1,128,256]{2,1,0:T(8,128)(2,1)S(1)}, bf16[1,128,256]{2,1,0:T(8,128)(2,1)S(1)}, u32[]{:S(2)}, u32[]{:S(2)}) collective-permute-start(bf16[1,128,256]{2,1,0:T(8,128)(2,1)S(1)} %get-tuple-element.46), channel_id=1, source_target_pairs={{0,4},{4,8},{8,12},{12,16},{16,20},{20,24},{24,28},{28,0},{1,5},{5... | collective-permute-start | bytes 196616 | tf_op jit(solution)/shard_map/ppermute | solution.py:310
  31.5 3.4 %collective-permute-start.9 = (bf16[1,128,256]{2,1,0:T(8,128)(2,1)S(1)}, bf16[1,128,256]{2,1,0:T(8,128)(2,1)S(1)}, u32[]{:S(2)}, u32[]{:S(2)}) collective-permute-start(bf16[1,128,256]{2,1,0:T(8,128)(2,1)S(1)} %get-tuple-element.47), channel_id=1, source_target_pairs={{4,0},{8,4},{12,8},{16,12},{20,16},{24,20},{28,24},{0,28},{5,1},{9... | collective-permute-start | bytes 196616 | tf_op jit(solution)/shard_map/ppermute | solution.py:311
  34.9 1.3 %collective-permute-start.13 = (bf16[1,640,256]{2,1,0:T(8,128)(2,1)S(1)}, bf16[1,640,256]{2,1,0:T(8,128)(2,1)S(1)}, u32[]{:S(2)}, u32[]{:S(2)}) collective-permute-start(bf16[1,640,256]{2,1,0:T(8,128)(2,1)S(1)} %get-tuple-element.48.own_ref), channel_id=1, source_target_pairs={{0,2},{1,3},{2,0},{3,1},{4,6},{5,7},{6,4},{7,5},{8,10},{9,11},{10,... | collective-permute-start | bytes 983048 | tf_op jit(solution)/shard_map/ppermute | solution.py:307
  36.2 0.0 collective-permute-done.far_ref
  36.2 0.0 collective-permute-start.7
  36.2 1.1 %collective-permute-done.8.refs_4_ = bf16[1,128,256]{2,1,0:T(8,128)(2,1)S(1)} collective-permute-done((bf16[1,128,256]{2,1,0:T(8,128)(2,1)S(1)}, bf16[1,128,256]{2,1,0:T(8,128)(2,1)S(1)}, u32[]{:S(2)}, u32[]{:S(2)}) %collective-permute-start.8) | collective-permute-done | bytes 65568 | tf_op jit(solution)/shard_map/ppermute | solution.py:310
  37.3 0.0 collective-permute-done.9.refs_5_
  37.3 0.0 collective-permute-done.10.sib_ref
  37.3 0.5 near_part.1.part_ref
  37.8 0.3 collective-permute-done.7.farsib_ref
  38.1 1.9 %first_node.3 = (f32[3,128,256]{2,1,0:T(8,128)S(1)}, bf16[1,384,256]{2,1,0:T(8,128)(2,1)S(1)}, f32[3,128,256]{2,1,0:T(8,128)S(1)}) custom-call(s32[1]{0:T(128)} %bitcast.me_ref, bf16[2,384,256]{2,1,0:T(8,128)(2,1)} %collective-permute-done.far_ref, bf16[2,384,256]{2,1,0:T(8,128)(2,1)S(1)} %collective-permute-done.7.farsib_ref, ...), custom_call_target="tpu_custom_call" | custom-call | tf_op jit(solution)/shard_map/first_node/pallas_call | solution.py:37
  40.0 0.2 collective-permute-start.11
  40.2 1.2 %collective-permute-start.12 = (bf16[1,384,256]{2,1,0:T(8,128)(2,1)S(1)}, bf16[1,384,256]{2,1,0:T(8,128)(2,1)S(1)}, u32[]{:S(2)}, u32[]{:S(2)}) collective-permute-start(bf16[1,384,256]{2,1,0:T(8,128)(2,1)S(1)} %get-tuple-element.51.own_ref), channel_id=1, source_target_pairs={{0,2},{1,3},{2,0},{3,1},{4,6},{5,7},{6,4},{7,5},{8,10},{9,11},{10,... | collective-permute-start | bytes 589832 | tf_op jit(solution)/shard_map/ppermute | solution.py:307
  41.4 4.1 %collective-permute-done.13.far_ref = bf16[1,640,256]{2,1,0:T(8,128)(2,1)S(1)} collective-permute-done((bf16[1,640,256]{2,1,0:T(8,128)(2,1)S(1)}, bf16[1,640,256]{2,1,0:T(8,128)(2,1)S(1)}, u32[]{:S(2)}, u32[]{:S(2)}) %collective-permute-start.13) | collective-permute-done | bytes 327712 | tf_op jit(solution)/shard_map/ppermute | solution.py:307
  45.5 0.0 collective-permute-start.14
  45.5 0.0 collective-permute-done.11.sib_ref
  45.5 1.2 %before_second.1 = (f32[8,128,256]{2,1,0:T(8,128)}, f32[2,384,256]{2,1,0:T(8,128)S(1)}, f32[5,128,256]{2,1,0:T(8,128)S(1)}, f32[3,128,256]{2,1,0:T(8,128)S(1)}) custom-call(s32[1]{0:T(128)} %bitcast.me_ref, bf16[1,384,256]{2,1,0:T(8,128)(2,1)S(1)} %get-tuple-element.51.own_ref, bf16[1,384,256]{2,1,0:T(8,128)(2,1)S(1)} %collective-permute-done.11.sib_ref, ...), custom_call_target="tpu_custom_call" | custom-call | flops 20000000000 | tf_op jit(solution)/shard_map/before_second/pallas_call | solution.py:37
  46.7 0.4 collective-permute-done.14.farsib_ref
  47.1 0.6 %second_node.2.refs_0_ = f32[5,128,256]{2,1,0:T(8,128)S(1)} custom-call(s32[1]{0:T(128)} %bitcast.me_ref, bf16[1,640,256]{2,1,0:T(8,128)(2,1)S(1)} %collective-permute-done.13.far_ref, bf16[1,640,256]{2,1,0:T(8,128)(2,1)S(1)} %collective-permute-done.14.farsib_ref, f32[2,640,256]{2,1,0:T(8,128)S(1)} %near_part.1.part_ref, ...), custom_call_target="tpu_custom_call" | custom-call | tf_op jit(solution)/shard_map/second_node/pallas_call | solution.py:37
  47.7 0.9 %collective-permute-done.12.far_ref = bf16[1,384,256]{2,1,0:T(8,128)(2,1)S(1)} collective-permute-done((bf16[1,384,256]{2,1,0:T(8,128)(2,1)S(1)}, bf16[1,384,256]{2,1,0:T(8,128)(2,1)S(1)}, u32[]{:S(2)}, u32[]{:S(2)}) %collective-permute-start.12) | collective-permute-done | bytes 196640 | tf_op jit(solution)/shard_map/ppermute | solution.py:307
  48.6 0.0 collective-permute-start.15
  48.6 1.4 %collective-permute-done.15.farsib_ref = bf16[1,384,256]{2,1,0:T(8,128)(2,1)S(1)} collective-permute-done((bf16[1,384,256]{2,1,0:T(8,128)(2,1)S(1)}, bf16[1,384,256]{2,1,0:T(8,128)(2,1)S(1)}, u32[]{:S(2)}, u32[]{:S(2)}) %collective-permute-start.15) | collective-permute-done | bytes 196640 | tf_op jit(solution)/shard_map/ppermute | solution.py:304
  50.1 1.1 %second_node.3 = f32[8,128,256]{2,1,0:T(8,128)} custom-call(s32[1]{0:T(128)} %bitcast.me_ref, bf16[1,384,256]{2,1,0:T(8,128)(2,1)S(1)} %collective-permute-done.12.far_ref, bf16[1,384,256]{2,1,0:T(8,128)(2,1)S(1)} %collective-permute-done.15.farsib_ref, f32[2,384,256]{2,1,0:T(8,128)S(1)} %get-tuple-element.60.part_ref, ...), custom_call_target="tpu_custom_call" | custom-call | tf_op jit(solution)/shard_map/second_node/pallas_call | solution.py:37
  (9 shorter events, 0.0 us)
Async XLA Ops:
  0.6 22.4 %copy-start.2 = (bf16[2,1024,256]{2,1,0:T(8,128)(2,1)S(1)}, bf16[2,1024,256]{2,1,0:T(8,128)(2,1)}, u32[]{:S(2)}) copy-start(bf16[2,1024,256]{2,1,0:T(8,128)(2,1)} %k_ref.9) | copy-start | bytes 3145732
  3.1 20.0 %copy-start = (f32[8,128,256]{2,1,0:T(8,128)S(1)}, f32[8,128,256]{2,1,0:T(8,128)}, u32[]{:S(2)}) copy-start(f32[8,128,256]{2,1,0:T(8,128)} %one_ref.3) | copy-start | bytes 3145732
  3.1 20.0 %copy-start.1 = (f32[8,128,256]{2,1,0:T(8,128)S(1)}, f32[8,128,256]{2,1,0:T(8,128)}, u32[]{:S(2)}) copy-start(f32[8,128,256]{2,1,0:T(8,128)} %two_ref.3) | copy-start | bytes 3145732
  3.1 20.0 %copy-start.7 = (f32[256]{0:T(256)S(1)}, f32[256]{0:T(256)}, u32[]{:S(2)}) copy-start(f32[256]{0:T(256)} %param.10) | copy-start | bytes 3076
  3.1 18.2 %collective-permute-start.1 = (bf16[2,640,256]{2,1,0:T(8,128)(2,1)}, bf16[2,640,256]{2,1,0:T(8,128)(2,1)}, u32[]{:S(2)}, u32[]{:S(2)}) collective-permute-start(bf16[2,640,256]{2,1,0:T(8,128)(2,1)} %get-tuple-element.36.refs_0_), channel_id=1, source_target_pairs={{0,2},{1,3},{2,0},{3,1},{4,6},{5,7},{6,4},{7,5},{8,10},{9,11},{10,... | collective-permute-start | bytes 1966088 | tf_op jit(solution)/shard_map/ppermute | solution.py:307
  7.4 15.7 %collective-permute-start.3 = (bf16[2,640,256]{2,1,0:T(8,128)(2,1)}, bf16[2,640,256]{2,1,0:T(8,128)(2,1)}, u32[]{:S(2)}, u32[]{:S(2)}) collective-permute-start(bf16[2,640,256]{2,1,0:T(8,128)(2,1)} %get-tuple-element.36.refs_0_), channel_id=1, source_target_pairs={{0,1},{1,0},{2,3},{3,2},{4,5},{5,4},{6,7},{7,6},{8,9},{9,8},{10,11... | collective-permute-start | bytes 1966088 | tf_op jit(solution)/shard_map/ppermute | solution.py:304
  7.5 8.7 %collective-permute-start.4 = (bf16[2,128,256]{2,1,0:T(8,128)(2,1)S(1)}, bf16[2,128,256]{2,1,0:T(8,128)(2,1)S(1)}, u32[]{:S(2)}, u32[]{:S(2)}) collective-permute-start(bf16[2,128,256]{2,1,0:T(8,128)(2,1)S(1)} %get-tuple-element.38), channel_id=1, source_target_pairs={{0,4},{4,8},{8,12},{12,16},{16,20},{20,24},{24,28},{28,0},{1,5},{5... | collective-permute-start | bytes 393224 | tf_op jit(solution)/shard_map/ppermute | solution.py:310
  16.2 0.7 %copy-start.5 = (bf16[2,128,256]{2,1,0:T(8,128)(2,1)}, bf16[2,128,256]{2,1,0:T(8,128)(2,1)S(1)}, u32[]{:S(2)}) copy-start(bf16[2,128,256]{2,1,0:T(8,128)(2,1)S(1)} %collective-permute-done.4.refs_6_) | copy-start | bytes 393220
  16.8 6.2 %collective-permute-start.5 = (bf16[2,384,256]{2,1,0:T(8,128)(2,1)S(1)}, bf16[2,384,256]{2,1,0:T(8,128)(2,1)}, u32[]{:S(2)}, u32[]{:S(2)}) collective-permute-start(bf16[2,384,256]{2,1,0:T(8,128)(2,1)S(1)} %round_chunk.3.refs_1_), channel_id=1, source_target_pairs={{0,1},{1,0},{2,3},{3,2},{4,5},{5,4},{6,7},{7,6},{8,9},{9,8},{10,11... | collective-permute-start | bytes 1179656 | tf_op jit(solution)/shard_map/ppermute | solution.py:304
  16.8 6.2 %collective-permute-start.6 = (bf16[2,128,256]{2,1,0:T(8,128)(2,1)}, bf16[2,128,256]{2,1,0:T(8,128)(2,1)}, u32[]{:S(2)}, u32[]{:S(2)}) collective-permute-start(bf16[2,128,256]{2,1,0:T(8,128)(2,1)} %get-tuple-element.40), channel_id=1, source_target_pairs={{4,0},{8,4},{12,8},{16,12},{20,16},{24,20},{28,24},{0,28},{5,1},{9... | collective-permute-start | bytes 393224 | tf_op jit(solution)/shard_map/ppermute | solution.py:311
  18.6 17.6 %collective-permute-start = (bf16[2,384,256]{2,1,0:T(8,128)(2,1)S(1)}, bf16[2,384,256]{2,1,0:T(8,128)(2,1)}, u32[]{:S(2)}, u32[]{:S(2)}) collective-permute-start(bf16[2,384,256]{2,1,0:T(8,128)(2,1)S(1)} %round_chunk.3.refs_1_), channel_id=1, source_target_pairs={{0,2},{1,3},{2,0},{3,1},{4,6},{5,7},{6,4},{7,5},{8,10},{9,11},{10,... | collective-permute-start | bytes 1179656 | tf_op jit(solution)/shard_map/ppermute | solution.py:307
  21.2 6.3 %collective-permute-start.2 = (bf16[2,640,256]{2,1,0:T(8,128)(2,1)}, bf16[2,640,256]{2,1,0:T(8,128)(2,1)S(1)}, u32[]{:S(2)}, u32[]{:S(2)}) collective-permute-start(bf16[2,640,256]{2,1,0:T(8,128)(2,1)} %collective-permute-done.1.far_ref), channel_id=1, source_target_pairs={{0,1},{1,0},{2,3},{3,2},{4,5},{5,4},{6,7},{7,6},{8,9},{9,8},{10,11... | collective-permute-start | bytes 1966088 | tf_op jit(solution)/shard_map/ppermute | solution.py:304
  23.1 0.9 %copy-start.6 = (bf16[2,128,256]{2,1,0:T(8,128)(2,1)S(1)}, bf16[2,128,256]{2,1,0:T(8,128)(2,1)}, u32[]{:S(2)}) copy-start(bf16[2,128,256]{2,1,0:T(8,128)(2,1)} %copy-done.5) | copy-start | bytes 393220
  24.0 3.5 %copy-start.3 = (f32[8,128,256]{2,1,0:T(8,128)S(1)}, f32[8,128,256]{2,1,0:T(8,128)}, u32[]{:S(2)}) copy-start(f32[8,128,256]{2,1,0:T(8,128)} %init_ref.3) | copy-start | bytes 3145732
  24.0 3.5 %copy-start.4 = (f32[256]{0:T(256)S(1)}, f32[256]{0:T(256)}, u32[]{:S(2)}) copy-start(f32[256]{0:T(256)} %param.11) | copy-start | bytes 3076
  30.1 7.3 %collective-permute-start.10 = (bf16[1,640,256]{2,1,0:T(8,128)(2,1)S(1)}, bf16[1,640,256]{2,1,0:T(8,128)(2,1)S(1)}, u32[]{:S(2)}, u32[]{:S(2)}) collective-permute-start(bf16[1,640,256]{2,1,0:T(8,128)(2,1)S(1)} %get-tuple-element.48.own_ref), channel_id=1, source_target_pairs={{0,1},{1,0},{2,3},{3,2},{4,5},{5,4},{6,7},{7,6},{8,9},{9,8},{10,11... | collective-permute-start | bytes 983048 | tf_op jit(solution)/shard_map/ppermute | solution.py:304
  30.1 7.2 %collective-permute-start.8 = (bf16[1,128,256]{2,1,0:T(8,128)(2,1)S(1)}, bf16[1,128,256]{2,1,0:T(8,128)(2,1)S(1)}, u32[]{:S(2)}, u32[]{:S(2)}) collective-permute-start(bf16[1,128,256]{2,1,0:T(8,128)(2,1)S(1)} %get-tuple-element.46), channel_id=1, source_target_pairs={{0,4},{4,8},{8,12},{12,16},{16,20},{20,24},{24,28},{28,0},{1,5},{5... | collective-permute-start | bytes 196616 | tf_op jit(solution)/shard_map/ppermute | solution.py:310
  31.5 5.8 %collective-permute-start.9 = (bf16[1,128,256]{2,1,0:T(8,128)(2,1)S(1)}, bf16[1,128,256]{2,1,0:T(8,128)(2,1)S(1)}, u32[]{:S(2)}, u32[]{:S(2)}) collective-permute-start(bf16[1,128,256]{2,1,0:T(8,128)(2,1)S(1)} %get-tuple-element.47), channel_id=1, source_target_pairs={{4,0},{8,4},{12,8},{16,12},{20,16},{24,20},{28,24},{0,28},{5,1},{9... | collective-permute-start | bytes 196616 | tf_op jit(solution)/shard_map/ppermute | solution.py:311
  34.9 10.6 %collective-permute-start.13 = (bf16[1,640,256]{2,1,0:T(8,128)(2,1)S(1)}, bf16[1,640,256]{2,1,0:T(8,128)(2,1)S(1)}, u32[]{:S(2)}, u32[]{:S(2)}) collective-permute-start(bf16[1,640,256]{2,1,0:T(8,128)(2,1)S(1)} %get-tuple-element.48.own_ref), channel_id=1, source_target_pairs={{0,2},{1,3},{2,0},{3,1},{4,6},{5,7},{6,4},{7,5},{8,10},{9,11},{10,... | collective-permute-start | bytes 983048 | tf_op jit(solution)/shard_map/ppermute | solution.py:307
  36.2 1.9 %collective-permute-start.7 = (bf16[2,384,256]{2,1,0:T(8,128)(2,1)}, bf16[2,384,256]{2,1,0:T(8,128)(2,1)S(1)}, u32[]{:S(2)}, u32[]{:S(2)}) collective-permute-start(bf16[2,384,256]{2,1,0:T(8,128)(2,1)} %collective-permute-done.far_ref), channel_id=1, source_target_pairs={{0,1},{1,0},{2,3},{3,2},{4,5},{5,4},{6,7},{7,6},{8,9},{9,8},{10,11... | collective-permute-start | bytes 1179656 | tf_op jit(solution)/shard_map/ppermute | solution.py:304
  40.0 5.5 %collective-permute-start.11 = (bf16[1,384,256]{2,1,0:T(8,128)(2,1)S(1)}, bf16[1,384,256]{2,1,0:T(8,128)(2,1)S(1)}, u32[]{:S(2)}, u32[]{:S(2)}) collective-permute-start(bf16[1,384,256]{2,1,0:T(8,128)(2,1)S(1)} %get-tuple-element.51.own_ref), channel_id=1, source_target_pairs={{0,1},{1,0},{2,3},{3,2},{4,5},{5,4},{6,7},{7,6},{8,9},{9,8},{10,11... | collective-permute-start | bytes 589832 | tf_op jit(solution)/shard_map/ppermute | solution.py:304
  40.2 8.4 %collective-permute-start.12 = (bf16[1,384,256]{2,1,0:T(8,128)(2,1)S(1)}, bf16[1,384,256]{2,1,0:T(8,128)(2,1)S(1)}, u32[]{:S(2)}, u32[]{:S(2)}) collective-permute-start(bf16[1,384,256]{2,1,0:T(8,128)(2,1)S(1)} %get-tuple-element.51.own_ref), channel_id=1, source_target_pairs={{0,2},{1,3},{2,0},{3,1},{4,6},{5,7},{6,4},{7,5},{8,10},{9,11},{10,... | collective-permute-start | bytes 589832 | tf_op jit(solution)/shard_map/ppermute | solution.py:307
  45.5 1.6 %collective-permute-start.14 = (bf16[1,640,256]{2,1,0:T(8,128)(2,1)S(1)}, bf16[1,640,256]{2,1,0:T(8,128)(2,1)S(1)}, u32[]{:S(2)}, u32[]{:S(2)}) collective-permute-start(bf16[1,640,256]{2,1,0:T(8,128)(2,1)S(1)} %collective-permute-done.13.far_ref), channel_id=1, source_target_pairs={{0,1},{1,0},{2,3},{3,2},{4,5},{5,4},{6,7},{7,6},{8,9},{9,8},{10,11... | collective-permute-start | bytes 983048 | tf_op jit(solution)/shard_map/ppermute | solution.py:304
  48.6 1.4 %collective-permute-start.15 = (bf16[1,384,256]{2,1,0:T(8,128)(2,1)S(1)}, bf16[1,384,256]{2,1,0:T(8,128)(2,1)S(1)}, u32[]{:S(2)}, u32[]{:S(2)}) collective-permute-start(bf16[1,384,256]{2,1,0:T(8,128)(2,1)S(1)} %collective-permute-done.12.far_ref), channel_id=1, source_target_pairs={{0,1},{1,0},{2,3},{3,2},{4,5},{5,4},{6,7},{7,6},{8,9},{9,8},{10,11... | collective-permute-start | bytes 589832 | tf_op jit(solution)/shard_map/ppermute | solution.py:304

commit v2 on v1

--- a/solution.py
+++ b/solution.py
@@ -11,7 +11,7 @@
 SECOND = 2.0 * STEP_SIZE / 3.0
 F32 = jnp.float32
 BF16 = jnp.bfloat16
-VMEM_LIMIT = 28 * 1024 * 1024
+VMEM_LIMIT = 20 * 1024 * 1024
 SPEC = pl.BlockSpec(memory_space=pltpu.VMEM)
 ANYWHERE = pl.BlockSpec(memory_space=pl.ANY)
 FROM_HBM = pl.BlockSpec(memory_space=pltpu.HBM)
@@ -83,11 +83,11 @@
     )
 
 
-def half_dot(near, other, kernels_ref, k, first, second):
-    depth = near.shape[-1]
-    lhs = jnp.concatenate([near, other], axis=-1)
+def blocks_dot(blocks, kernels_ref, k, owners):
+    depth = blocks[0].shape[-1]
+    lhs = jnp.concatenate(blocks, axis=-1)
     rhs = jnp.concatenate(
-        [kernels_ref[k, pl.ds(pl.multiple_of(b * depth, depth), depth), :] for b in (first, second)], axis=0
+        [kernels_ref[k, pl.ds(pl.multiple_of(o * depth, depth), depth), :] for o in owners], axis=0
     )
     return jnp.dot(lhs, rhs, preferred_element_type=F32)
 
@@ -100,49 +100,68 @@
     return DIFFUSION * around - 2.0 * core, core
 
 
-def before_first(me, owns, sibs, one, two, lo, hi, kernels, growth, chunks):
+def before_first(me, owns, one, two, lo, hi, kernels, growth, chunks):
     xcount, ycount, owned = one.shape
     count = len(chunks)
 
     def body(me_ref, *refs):
-        own_refs, sib_refs = refs[:count], refs[count:2 * count]
-        one_ref, two_ref, lo_ref, hi_ref, k_ref, g_ref = refs[2 * count:2 * count + 6]
-        outs = refs[2 * count + 6:]
+        own_refs = refs[:count]
+        one_ref, two_ref, lo_ref, hi_ref, k_ref, g_ref = refs[count:count + 6]
+        outs = refs[count + 6:]
         me = me_ref[0]
         growth = g_ref[...]
         for c, cells in enumerate(chunks):
-            part_ref, base_ref = outs[2 * c:2 * c + 2]
-            rows = len(cells) * ycount
-            near = own_refs[c][...].reshape(2 * rows, owned)
-            other = sib_refs[c][...].reshape(2 * rows, owned)
             for k in range(2):
-                part_ref[k] = half_dot(near, other, k_ref, k, me, me ^ 1)
+                outs[c][k] = blocks_dot([rows_of([own_refs[c]], owned)], k_ref, k, (me,))
             for f, ref in enumerate((one_ref, two_ref)):
                 for i, x in enumerate(cells):
                     base, core = stencil(lambda x: ref[x], (lambda: lo_ref[f], lambda: hi_ref[f]), x, xcount)
-                    base_ref[f, i] = base + core * growth
-
-    outs = []
-    for cells in chunks:
-        outs.append(pltpu.VMEM((2, 2 * len(cells) * ycount, owned), F32))
-        outs.append(pltpu.VMEM((2, len(cells), ycount, owned), F32))
-    args = [me, *owns, *sibs, one, two, lo, hi, kernels, growth]
-    flat = call(body, "before_first", args, outs, specs=[pl.BlockSpec(memory_space=pltpu.SMEM)] + [SPEC] * (len(args) - 1), gflop=20.0)
-    return [flat[2 * c:2 * c + 2] for c in range(count)]
+                    outs[count + c][f, i] = base + core * growth
+
+    outs = [pltpu.VMEM((2, 2 * len(cells) * ycount, owned), F32) for cells in chunks]
+    outs += [pltpu.VMEM((2, len(cells), ycount, owned), F32) for cells in chunks]
+    args = [me, *owns, one, two, lo, hi, kernels, growth]
+    flat = call(
+        body, "before_first", args, outs,
+        specs=[pl.BlockSpec(memory_space=pltpu.SMEM)] + [SPEC] * (len(args) - 1), gflop=0.0,
+    )
+    return flat[:count], flat[count:]
+
+
+def sibling_part(me, parts, sibs, kernels):
+    owned = sibs[0].shape[-1]
+    count = len(parts)
+
+    def body(me_ref, *refs):
+        part_refs, sib_refs, k_ref, outs = refs[:count], refs[count:2 * count], refs[2 * count], refs[2 * count + 1:]
+        me = me_ref[0]
+        for part_ref, sib_ref, out_ref in zip(part_refs, sib_refs, outs):
+            for k in range(2):
+                out_ref[k] = part_ref[k] + blocks_dot([rows_of([sib_ref], owned)], k_ref, k, (me ^ 1,))
+
+    args = [me, *parts, *sibs, kernels]
+    return call(
+        body, "sibling_part", args, [pltpu.VMEM(p.shape, F32) for p in parts],
+        specs=[pl.BlockSpec(memory_space=pltpu.SMEM)] + [SPEC] * (len(args) - 1), gflop=20.0,
+    )
 
 
 def first_node(me, far, farsib, part, base, one, two, initial, kernels, death, cells, with_faces):
     xcount, ycount, owned = one.shape
     rows = len(cells) * ycount
 
-    def body(me_ref, far_ref, farsib_ref, part_ref, base_ref, one_ref, two_ref, init_ref, k_ref, d_ref, *refs):
+    count = len(far)
+
+    def body(me_ref, *refs):
+        far_refs, farsib_refs = refs[:count], refs[count:2 * count]
+        part_ref, base_ref, one_ref, two_ref, init_ref, k_ref, d_ref = refs[2 * count:2 * count + 7]
+        refs = refs[2 * count + 7:]
         new_ref, rounded_ref, rest_ref = refs[:3]
         sums = refs[-1]
         me = me_ref[0]
-        near = far_ref[...].reshape(2 * rows, owned)
-        other = farsib_ref[...].reshape(2 * rows, owned)
+        blocks = [rows_of(far_refs, owned), rows_of(farsib_refs, owned)]
         for k in range(2):
-            sums[k] = (part_ref[k] + half_dot(near, other, k_ref, k, me ^ 2, me ^ 3)).astype(BF16)
+            sums[k] = (part_ref[k] + blocks_dot(blocks, k_ref, k, (me ^ 2, me ^ 3))).astype(BF16)
         death = d_ref[...]
         inv_one = 1.0 / (1.0 + FIRST * death)
         inv_two = 1.0 / (1.0 + SECOND * death)
@@ -177,39 +196,37 @@
     ]
     if with_faces:
         outs += [pltpu.VMEM((1, ycount, owned), BF16)] * 2
-    args = [me, far, farsib, part, base, one, two, initial, kernels, death]
+    args = [me, *far, *farsib, part, base, one, two, initial, kernels, death]
     return call(
         body, "first_node", args, outs, scratch=[pltpu.VMEM((2, 2 * rows, owned), BF16)],
         specs=[pl.BlockSpec(memory_space=pltpu.SMEM)] + [SPEC] * (len(args) - 1), gflop=0.0,
     )
 
 
-def near_part(me, own, sib, kernels):
+def own_part(me, own, kernels):
     rows, owned = own.shape[1:]
 
-    def body(me_ref, own_ref, sib_ref, k_ref, part_ref):
-        me = me_ref[0]
-        near, other = rows_of([own_ref], owned), rows_of([sib_ref], owned)
+    def body(me_ref, own_ref, k_ref, part_ref):
+        me = me_ref[0]
         for k in range(2):
-            part_ref[k] = half_dot(near, other, k_ref, k, me, me ^ 1)
-
-    return call(
-        body, "near_part", [me, own, sib, kernels], [pltpu.VMEM((2, rows, owned), F32)],
-        specs=[pl.BlockSpec(memory_space=pltpu.SMEM)] + [SPEC] * 3, gflop=20.0,
+            part_ref[k] = blocks_dot([rows_of([own_ref], owned)], k_ref, k, (me,))
+
+    return call(
+        body, "own_part", [me, own, kernels], [pltpu.VMEM((2, rows, owned), F32)],
+        specs=[pl.BlockSpec(memory_space=pltpu.SMEM)] + [SPEC] * 2, gflop=20.0,
     )[0]
 
 
-def before_second(me, own, sib, news, rests, lo, hi, kernels, growth, death, chunks):
+def before_second(me, owned_a, sib_a, own, sib, news, rests, lo, hi, kernels, growth, death, chunks):
     _, ycount, owned = news[0].shape
     xcount = sum(len(cells) for cells in chunks)
     count = len(chunks)
-    rows = own.shape[1]
     place = {x: (c, i) for c, cells in enumerate(chunks) for i, x in enumerate(cells)}
 
-    def body(me_ref, own_ref, sib_ref, *refs):
+    def body(me_ref, owned_ref, sib_a_ref, own_ref, sib_ref, *refs):
         new_refs, rest_refs = refs[:count], refs[count:2 * count]
-        lo_ref, hi_ref, k_ref, g_ref, d_ref, whole_ref, part_ref = refs[2 * count:2 * count + 7]
-        base_refs, sems = refs[2 * count + 7:-1], refs[-1]
+        lo_ref, hi_ref, k_ref, g_ref, d_ref, whole_ref, part_a_ref, part_b_ref = refs[2 * count:2 * count + 8]
+        base_refs, sems = refs[2 * count + 8:-1], refs[-1]
         copies = [
             pltpu.make_async_copy(new_refs[c].at[i], whole_ref.at[x], sems.at[x]) for x, (c, i) in place.items()
         ]
@@ -223,9 +240,10 @@
             c, i = place[x]
             return new_refs[c][i]
 
-        near, other = rows_of([own_ref], owned), rows_of([sib_ref], owned)
+        blocks = [rows_of([own_ref], owned), rows_of([sib_ref], owned)]
         for k in range(2):
-            part_ref[k] = half_dot(near, other, k_ref, k, me, me ^ 1)
+            part_a_ref[k] = owned_ref[k] + blocks_dot([rows_of([sib_a_ref], owned)], k_ref, k, (me ^ 1,))
+            part_b_ref[k] = blocks_dot(blocks, k_ref, k, (me, me ^ 1))
         for c, cells in enumerate(chunks):
             for i, x in enumerate(cells):
                 base, core = stencil(get, (lambda: lo_ref[0], lambda: hi_ref[0]), x, xcount)
@@ -233,9 +251,10 @@
         for copy in copies:
             copy.wait()
 
-    outs = [jax.ShapeDtypeStruct((xcount, ycount, owned), F32), pltpu.VMEM((2, rows, owned), F32)]
+    outs = [jax.ShapeDtypeStruct((xcount, ycount, owned), F32)]
+    outs += [pltpu.VMEM((2, len(cells) * ycount, owned), F32) for cells in chunks]
     outs += [pltpu.VMEM((len(cells), ycount, owned), F32) for cells in chunks]
-    args = [me, own, sib, *news, *rests, lo, hi, kernels, growth, death]
+    args = [me, owned_a, sib_a, own, sib, *news, *rests, lo, hi, kernels, growth, death]
     return call(
         body, "before_second", args, outs, scratch=[pltpu.SemaphoreType.DMA((xcount,))],
         specs=[pl.BlockSpec(memory_space=pltpu.SMEM)] + [SPEC] * (len(args) - 1),
@@ -257,10 +276,9 @@
         else:
             out_ref, sums = refs
         me = me_ref[0]
-        near = far_ref[...].reshape(rows, owned)
-        other = farsib_ref[...].reshape(rows, owned)
+        blocks = [rows_of([far_ref], owned), rows_of([farsib_ref], owned)]
         for k in range(2):
-            sums[k] = (part_ref[k] + half_dot(near, other, k_ref, k, me ^ 2, me ^ 3)).astype(BF16)
+            sums[k] = (part_ref[k] + blocks_dot(blocks, k_ref, k, (me ^ 2, me ^ 3))).astype(BF16)
         factor = SECOND / (1.0 + SECOND * d_ref[...])
         for i, x in enumerate(cells):
             at = pl.ds(i * ycount, ycount)
@@ -315,35 +333,37 @@
     far_a = to_far(own_a)
     own_b = round_chunk((after(section_one, own_a), section_two), chunks[1], False)[0]
     far_b = to_far(own_b)
-    head, tail, near_a, near_b = lax.optimization_barrier((head, tail, own_a, own_b))
+    head, tail = lax.optimization_barrier((head, tail, own_b))[:2]
     lo, hi = faces(head, tail)
-    sib_a = to_sibling(near_a)
-    sib_b = to_sibling(after(near_b, lo))
-    (part_a, base_a), (part_b, base_b) = before_first(
-        me, (own_a, own_b), (sib_a, sib_b), section_one, section_two, lo, hi, kernels, growth, chunks
-    )
-
+    (part_a, part_b), (base_a, base_b) = before_first(
+        me, (own_a, own_b), section_one, section_two, lo, hi, kernels, growth, chunks
+    )
+    sib_a = to_sibling(after(own_a, own_b))
+    sib_b = to_sibling(own_b)
+    far_a = after(far_a, part_a)
     farsib_a = to_sibling(far_a)
+    part_a, part_b = sibling_part(me, (part_a, part_b), (sib_a, sib_b), kernels)
     new_a, rounded_a, rest_a, new_head, new_tail = first_node(
-        me, far_a, farsib_a, part_a, base_a, section_one, section_two, initial, kernels, death, chunks[0], True
+        me, [far_a], [farsib_a], part_a, base_a, section_one, section_two, initial, kernels, death, chunks[0], True,
     )
     nfar_a = to_far(rounded_a)
     new_lo, new_hi = faces(new_head, new_tail)
     nsib_a = to_sibling(rounded_a)
-    npart_a = near_part(me, after(rounded_a, new_lo, new_hi), nsib_a, kernels)
+    npart_a = own_part(me, rounded_a, kernels)
 
     far_b = after(far_b, rounded_a)
     farsib_b = to_sibling(far_b)
     new_b, rounded_b, rest_b = first_node(
-        me, far_b, farsib_b, after(part_b, npart_a), base_b, section_one, section_two, initial, kernels, death,
+        me, [far_b], [farsib_b], after(part_b, npart_a, new_lo, new_hi), base_b, section_one, section_two, initial, kernels, death,
         chunks[1], False,
     )
     nfar_b = to_far(rounded_b)
     nsib_b = to_sibling(rounded_b)
     nfar_a = after(nfar_a, rounded_b)
     nfarsib_a = to_sibling(nfar_a)
-    new_one, npart_b, nbase_a, nbase_b = before_second(
-        me, rounded_b, nsib_b, (new_a, new_b), (rest_a, rest_b), new_lo, new_hi, kernels, growth, death, chunks
+    new_one, npart_a, npart_b, nbase_a, nbase_b = before_second(
+        me, npart_a, nsib_a, rounded_b, nsib_b, (new_a, new_b), (rest_a, rest_b), new_lo, new_hi, kernels, growth,
+        death, chunks,
     )
     two_a = second_node(me, nfar_a, nfarsib_a, npart_a, nbase_a, new_a, kernels, death, chunks[0], xcount)
     nfar_b = after(nfar_b, two_a)

time: 51.5 us -> 51.6 us (level)
  starting transfers between devices: 14.4 us -> 16.6 us
  local copies, waits for them, and re-layouts: 1.59 us -> 0.04 us
    ppermute x2, starting transfers between devices: 5.14 us -> 7.76 us  [faces(): lax.ppermute(head, 'gx', [((i + 1) % gcount, i) for i in range(gcount)])]
    ppermute x4, waiting for transfers between devices: 7.15 us -> 5.52 us  [to_far(): return lax.ppermute(v, 'trait', [(i, i ^ 2) for i in range(traits)])]
    unnamed x16 -> x12, local copies, waits for them, and re-layouts: 1.59 us -> 0.04 us
    ppermute x2, starting transfers between devices: 2.92 us -> 1.49 us  [faces(): lax.ppermute(tail, 'gx', [(i, (i + 1) % gcount) for i in range(gcount)])]
    ppermute x8, starting transfers between devices: 0.36 us -> 1.04 us  [to_sibling(): return lax.ppermute(v, 'trait', [(i, i ^ 1) for i in range(traits)])]
    ppermute x2, waiting for transfers between devices: 8.28 us -> 8.9 us  [faces(): lax.ppermute(tail, 'gx', [(i, (i + 1) % gcount) for i in range(gcount)])]
    pallas_call x9 -> x10, Pallas kernels: 15 us -> 15.1 us  [call(): pl.pallas_call(body, out_shape=outs, in_specs=specs, out_specs=out_specs...]
where the time goes in v2:
time: 51.6 us; the launch traced here: 51.4 us
  waiting for transfers between devices  18.9 us (37%)
  starting transfers between devices  16.6 us (32%)
  Pallas kernels  15.1 us (29%)
  between operations  0.8 us (2%)
    pallas_call x10, Pallas kernels, call(): pl.pallas_call(body, out_shape=outs, in_specs=specs, out_specs=out_specs...  15.1 us
    ppermute x2, waiting for transfers between devices, faces(): lax.ppermute(tail, 'gx', [(i, (i + 1) % gcount) for i in range(gcount)])  8.9 us
    ppermute x2, starting transfers between devices, faces(): lax.ppermute(head, 'gx', [((i + 1) % gcount, i) for i in range(gcount)])  7.76 us
    ppermute x4, starting transfers between devices, to_far(): return lax.ppermute(v, 'trait', [(i, i ^ 2) for i in range(traits)])  6.27 us
    ppermute x4, waiting for transfers between devices, to_far(): return lax.ppermute(v, 'trait', [(i, i ^ 2) for i in range(traits)])  5.52 us
    ppermute x8, waiting for transfers between devices, to_sibling(): return lax.ppermute(v, 'trait', [(i, i ^ 1) for i in range(traits)])  2.39 us
    ppermute x2, waiting for transfers between devices, faces(): lax.ppermute(head, 'gx', [((i + 1) % gcount, i) for i in range(gcount)])  2.05 us
    ppermute x2, starting transfers between devices, faces(): lax.ppermute(tail, 'gx', [(i, (i + 1) % gcount) for i in range(gcount)])  1.49 us
  transfers between devices with their start and end apart: 16, of which 9 were waited for; matrix products, arithmetic and copies ran while one was open for 0% of the time, Pallas kernels for 22%

profile of v2, /device:TPU:0, one launch (start us, length us, event | category | flops | bytes accessed | tf_op | source)
XLA Modules:
  0.0 51.4 jit_solution(2846443649160656130)
XLA Ops:
  0.6 2.4 %round_chunk.2 = (bf16[2,640,256]{2,1,0:T(8,128)(2,1)}, bf16[2,128,256]{2,1,0:T(8,128)(2,1)}, bf16[2,128,256]{2,1,0:T(8,128)(2,1)}) custom-call(f32[8,128,256]{2,1,0:T(8,128)} %refs_4_.5, f32[8,128,256]{2,1,0:T(8,128)} %refs_5_.3), custom_call_target="tpu_custom_call" | custom-call | tf_op jit(solution)/shard_map/round_chunk/pallas_call | solution.py:37
  3.1 0.0 copy-start
  3.1 0.0 copy-start.1
  3.1 0.0 copy-start.5
  3.1 3.0 %collective-permute-start = (bf16[2,640,256]{2,1,0:T(8,128)(2,1)}, bf16[2,640,256]{2,1,0:T(8,128)(2,1)}, u32[]{:S(2)}, u32[]{:S(2)}) collective-permute-start(bf16[2,640,256]{2,1,0:T(8,128)(2,1)} %get-tuple-element.42.refs_0_), channel_id=1, source_target_pairs={{0,2},{1,3},{2,0},{3,1},{4,6},{5,7},{6,4},{7,5},{8,10},{9,11},{10,... | collective-permute-start | bytes 1966088 | tf_op jit(solution)/shard_map/ppermute | solution.py:325
  6.2 1.3 %round_chunk.3.refs_1_ = bf16[2,384,256]{2,1,0:T(8,128)(2,1)S(1)} custom-call(f32[8,128,256]{2,1,0:T(8,128)} %refs_4_.5, f32[8,128,256]{2,1,0:T(8,128)} %refs_5_.3), custom_call_target="tpu_custom_call" | custom-call | tf_op jit(solution)/shard_map/round_chunk/pallas_call | solution.py:37
  7.4 0.1 collective-permute-start.4
  7.5 0.5 collective-permute-start.5
  8.0 1.5 %collective-permute-start.1 = (bf16[2,128,256]{2,1,0:T(8,128)(2,1)}, bf16[2,128,256]{2,1,0:T(8,128)(2,1)}, u32[]{:S(2)}, u32[]{:S(2)}) collective-permute-start(bf16[2,128,256]{2,1,0:T(8,128)(2,1)} %get-tuple-element.37), channel_id=1, source_target_pairs={{0,4},{4,8},{8,12},{12,16},{16,20},{20,24},{24,28},{28,0},{1,5},{5... | collective-permute-start | bytes 393224 | tf_op jit(solution)/shard_map/ppermute | solution.py:328
  9.5 3.2 %collective-permute-start.2 = (bf16[2,128,256]{2,1,0:T(8,128)(2,1)}, bf16[2,128,256]{2,1,0:T(8,128)(2,1)}, u32[]{:S(2)}, u32[]{:S(2)}) collective-permute-start(bf16[2,128,256]{2,1,0:T(8,128)(2,1)} %get-tuple-element.38), channel_id=1, source_target_pairs={{4,0},{8,4},{12,8},{16,12},{20,16},{24,20},{28,24},{0,28},{5,1},{9... | collective-permute-start | bytes 393224 | tf_op jit(solution)/shard_map/ppermute | solution.py:329
  12.7 4.0 %collective-permute-done.1.refs_4_ = bf16[2,128,256]{2,1,0:T(8,128)(2,1)} collective-permute-done((bf16[2,128,256]{2,1,0:T(8,128)(2,1)}, bf16[2,128,256]{2,1,0:T(8,128)(2,1)}, u32[]{:S(2)}, u32[]{:S(2)}) %collective-permute-start.1) | collective-permute-done | bytes 131104 | tf_op jit(solution)/shard_map/ppermute | solution.py:328
  16.7 0.5 %collective-permute-start.7 = (bf16[2,384,256]{2,1,0:T(8,128)(2,1)S(1)}, bf16[2,384,256]{2,1,0:T(8,128)(2,1)S(1)}, u32[]{:S(2)}, u32[]{:S(2)}) collective-permute-start(bf16[2,384,256]{2,1,0:T(8,128)(2,1)S(1)} %round_chunk.3.refs_1_), channel_id=1, source_target_pairs={{0,2},{1,3},{2,0},{3,1},{4,6},{5,7},{6,4},{7,5},{8,10},{9,11},{10,... | collective-permute-start | bytes 1179656 | tf_op jit(solution)/shard_map/ppermute | solution.py:325
  17.2 0.6 %collective-permute-done.2.refs_5_ = bf16[2,128,256]{2,1,0:T(8,128)(2,1)} collective-permute-done((bf16[2,128,256]{2,1,0:T(8,128)(2,1)}, bf16[2,128,256]{2,1,0:T(8,128)(2,1)}, u32[]{:S(2)}, u32[]{:S(2)}) %collective-permute-start.2) | collective-permute-done | bytes 131104 | tf_op jit(solution)/shard_map/ppermute | solution.py:329
  17.8 0.0 copy-done
  17.8 2.6 %before_first.1 = (f32[2,1280,256]{2,1,0:T(8,128)S(1)}, f32[2,768,256]{2,1,0:T(8,128)S(1)}, f32[2,5,128,256]{3,2,1,0:T(8,128)S(1)}, f32[2,3,128,256]{3,2,1,0:T(8,128)S(1)}) custom-call(s32[1]{0:T(128)} %bitcast.me_ref, bf16[2,640,256]{2,1,0:T(8,128)(2,1)} %get-tuple-element.42.refs_0_, bf16[2,384,256]{2,1,0:T(8,128)(2,1)S(1)} %round_chunk.3.refs_1_, ...), custom_call_target="tpu_custom_call" | custom-call | tf_op jit(solution)/shard_map/before_first/pallas_call | solution.py:37
  20.4 1.6 %collective-permute-done.refs_0_ = bf16[2,640,256]{2,1,0:T(8,128)(2,1)} collective-permute-done((bf16[2,640,256]{2,1,0:T(8,128)(2,1)}, bf16[2,640,256]{2,1,0:T(8,128)(2,1)}, u32[]{:S(2)}, u32[]{:S(2)}) %collective-permute-start) | collective-permute-done | bytes 655392 | tf_op jit(solution)/shard_map/ppermute | solution.py:325
  22.0 0.0 collective-permute-start.3
  22.0 0.0 collective-permute-done.5.refs_3_
  22.0 0.0 collective-permute-done.4.refs_2_
  22.0 0.0 copy-start.3
  22.1 0.0 copy-start.4
  22.1 2.0 %sibling_part.1 = (f32[2,1280,256]{2,1,0:T(8,128)S(1)}, f32[2,768,256]{2,1,0:T(8,128)S(1)}) custom-call(s32[1]{0:T(128)} %bitcast.me_ref, f32[2,1280,256]{2,1,0:T(8,128)S(1)} %get-tuple-element.39.refs_0_, f32[2,768,256]{2,1,0:T(8,128)S(1)} %get-tuple-element.41.refs_1_, bf16[2,640,256]{2,1,0:T(8,128)(2,1)} %collective-permute-done.4.refs_2_, ...), custom_call_target="tpu_custom_call" | custom-call | flops 20000000000 | tf_op jit(solution)/shard_map/sibling_part/pallas_call | solution.py:37
  24.1 0.3 collective-permute-done.3.refs_1_
  24.3 2.5 %first_node.2 = (f32[5,128,256]{2,1,0:T(8,128)S(1)}, bf16[1,640,256]{2,1,0:T(8,128)(2,1)S(1)}, f32[5,128,256]{2,1,0:T(8,128)S(1)}, bf16[1,128,256]{2,1,0:T(8,128)(2,1)S(1)}, bf16[1,128,256]{2,1,0:T(8,128)(2,1)S(1)}) custom-call(s32[1]{0:T(128)} %bitcast.me_ref, bf16[2,640,256]{2,1,0:T(8,128)(2,1)} %collective-permute-done.refs_0_, ...), custom_call_target="tpu_custom_call" | custom-call | tf_op jit(solution)/shard_map/first_node/pallas_call | solution.py:37
  26.9 2.1 %collective-permute-start.13 = (bf16[1,640,256]{2,1,0:T(8,128)(2,1)S(1)}, bf16[1,640,256]{2,1,0:T(8,128)(2,1)S(1)}, u32[]{:S(2)}, u32[]{:S(2)}) collective-permute-start(bf16[1,640,256]{2,1,0:T(8,128)(2,1)S(1)} %get-tuple-element.45.own_ref), channel_id=1, source_target_pairs={{0,2},{1,3},{2,0},{3,1},{4,6},{5,7},{6,4},{7,5},{8,10},{9,11},{10,... | collective-permute-start | bytes 983048 | tf_op jit(solution)/shard_map/ppermute | solution.py:325
  29.0 0.0 collective-permute-start.6
  29.0 4.5 %collective-permute-start.10 = (bf16[1,128,256]{2,1,0:T(8,128)(2,1)S(1)}, bf16[1,128,256]{2,1,0:T(8,128)(2,1)S(1)}, u32[]{:S(2)}, u32[]{:S(2)}) collective-permute-start(bf16[1,128,256]{2,1,0:T(8,128)(2,1)S(1)} %get-tuple-element.49), channel_id=1, source_target_pairs={{4,0},{8,4},{12,8},{16,12},{20,16},{24,20},{28,24},{0,28},{5,1},{9... | collective-permute-start | bytes 196616 | tf_op jit(solution)/shard_map/ppermute | solution.py:329
  33.5 0.0 collective-permute-start.9
  33.5 0.0 collective-permute-done.7.refs_0_
  33.5 0.2 collective-permute-start.8
  33.8 0.3 own_part.1.owned_ref
  34.1 1.5 %collective-permute-done.10.refs_5_ = bf16[1,128,256]{2,1,0:T(8,128)(2,1)S(1)} collective-permute-done((bf16[1,128,256]{2,1,0:T(8,128)(2,1)S(1)}, bf16[1,128,256]{2,1,0:T(8,128)(2,1)S(1)}, u32[]{:S(2)}, u32[]{:S(2)}) %collective-permute-start.10) | collective-permute-done | bytes 65568 | tf_op jit(solution)/shard_map/ppermute | solution.py:329
  35.5 4.9 %collective-permute-done.9.refs_4_ = bf16[1,128,256]{2,1,0:T(8,128)(2,1)S(1)} collective-permute-done((bf16[1,128,256]{2,1,0:T(8,128)(2,1)S(1)}, bf16[1,128,256]{2,1,0:T(8,128)(2,1)S(1)}, u32[]{:S(2)}, u32[]{:S(2)}) %collective-permute-start.9) | collective-permute-done | bytes 65568 | tf_op jit(solution)/shard_map/ppermute | solution.py:328
  40.5 0.0 collective-permute-done.8.refs_1_
  40.5 0.9 %first_node.3 = (f32[3,128,256]{2,1,0:T(8,128)S(1)}, bf16[1,384,256]{2,1,0:T(8,128)(2,1)S(1)}, f32[3,128,256]{2,1,0:T(8,128)S(1)}) custom-call(s32[1]{0:T(128)} %bitcast.me_ref, bf16[2,384,256]{2,1,0:T(8,128)(2,1)S(1)} %collective-permute-done.7.refs_0_, bf16[2,384,256]{2,1,0:T(8,128)(2,1)S(1)} %collective-permute-done.8.refs_1_, ...), custom_call_target="tpu_custom_call" | custom-call | tf_op jit(solution)/shard_map/first_node/pallas_call | solution.py:37
  41.4 0.1 collective-permute-start.11
  41.5 0.6 %collective-permute-start.12 = (bf16[1,384,256]{2,1,0:T(8,128)(2,1)S(1)}, bf16[1,384,256]{2,1,0:T(8,128)(2,1)S(1)}, u32[]{:S(2)}, u32[]{:S(2)}) collective-permute-start(bf16[1,384,256]{2,1,0:T(8,128)(2,1)S(1)} %get-tuple-element.52.own_ref), channel_id=1, source_target_pairs={{0,2},{1,3},{2,0},{3,1},{4,6},{5,7},{6,4},{7,5},{8,10},{9,11},{10,... | collective-permute-start | bytes 589832 | tf_op jit(solution)/shard_map/ppermute | solution.py:325
  42.0 0.0 collective-permute-done.13.far_ref
  42.0 0.2 collective-permute-start.14
  42.2 0.0 collective-permute-done.6.sib_a_ref
  42.2 0.7 %collective-permute-done.11.sib_ref = bf16[1,384,256]{2,1,0:T(8,128)(2,1)S(1)} collective-permute-done((bf16[1,384,256]{2,1,0:T(8,128)(2,1)S(1)}, bf16[1,384,256]{2,1,0:T(8,128)(2,1)S(1)}, u32[]{:S(2)}, u32[]{:S(2)}) %collective-permute-start.11) | collective-permute-done | bytes 196640 | tf_op jit(solution)/shard_map/ppermute | solution.py:322
  42.9 1.4 %before_second.1 = (f32[8,128,256]{2,1,0:T(8,128)}, f32[2,640,256]{2,1,0:T(8,128)S(1)}, f32[2,384,256]{2,1,0:T(8,128)S(1)}, f32[5,128,256]{2,1,0:T(8,128)S(1)}, f32[3,128,256]{2,1,0:T(8,128)S(1)}) custom-call(s32[1]{0:T(128)} %bitcast.me_ref, f32[2,640,256]{2,1,0:T(8,128)S(1)} %own_part.1.owned_ref, ...), custom_call_target="tpu_custom_call" | custom-call | flops 20000000000 | tf_op jit(solution)/shard_map/before_second/pallas_call | solution.py:37
  44.3 0.0 collective-permute-done.14.farsib_ref
  44.3 0.6 %second_node.2.refs_0_ = f32[5,128,256]{2,1,0:T(8,128)S(1)} custom-call(s32[1]{0:T(128)} %bitcast.me_ref, bf16[1,640,256]{2,1,0:T(8,128)(2,1)S(1)} %collective-permute-done.13.far_ref, bf16[1,640,256]{2,1,0:T(8,128)(2,1)S(1)} %collective-permute-done.14.farsib_ref, f32[2,640,256]{2,1,0:T(8,128)S(1)} %get-tuple-element.59.part_ref, ...), custom_call_target="tpu_custom_call" | custom-call | tf_op jit(solution)/shard_map/second_node/pallas_call | solution.py:37
  44.9 3.9 %collective-permute-done.12.far_ref = bf16[1,384,256]{2,1,0:T(8,128)(2,1)S(1)} collective-permute-done((bf16[1,384,256]{2,1,0:T(8,128)(2,1)S(1)}, bf16[1,384,256]{2,1,0:T(8,128)(2,1)S(1)}, u32[]{:S(2)}, u32[]{:S(2)}) %collective-permute-start.12) | collective-permute-done | bytes 196640 | tf_op jit(solution)/shard_map/ppermute | solution.py:325
  48.8 0.0 collective-permute-start.15
  48.8 1.4 %collective-permute-done.15.farsib_ref = bf16[1,384,256]{2,1,0:T(8,128)(2,1)S(1)} collective-permute-done((bf16[1,384,256]{2,1,0:T(8,128)(2,1)S(1)}, bf16[1,384,256]{2,1,0:T(8,128)(2,1)S(1)}, u32[]{:S(2)}, u32[]{:S(2)}) %collective-permute-start.15) | collective-permute-done | bytes 196640 | tf_op jit(solution)/shard_map/ppermute | solution.py:322
  50.2 1.1 %second_node.3 = f32[8,128,256]{2,1,0:T(8,128)} custom-call(s32[1]{0:T(128)} %bitcast.me_ref, bf16[1,384,256]{2,1,0:T(8,128)(2,1)S(1)} %collective-permute-done.12.far_ref, bf16[1,384,256]{2,1,0:T(8,128)(2,1)S(1)} %collective-permute-done.15.farsib_ref, f32[2,384,256]{2,1,0:T(8,128)S(1)} %get-tuple-element.62.part_ref, ...), custom_call_target="tpu_custom_call" | custom-call | tf_op jit(solution)/shard_map/second_node/pallas_call | solution.py:37
  (6 shorter events, 0.0 us)
Async XLA Ops:
  0.6 17.2 %copy-start.2 = (bf16[2,1024,256]{2,1,0:T(8,128)(2,1)S(1)}, bf16[2,1024,256]{2,1,0:T(8,128)(2,1)}, u32[]{:S(2)}) copy-start(bf16[2,1024,256]{2,1,0:T(8,128)(2,1)} %k_ref.5) | copy-start | bytes 3145732
  3.1 14.7 %copy-start = (f32[8,128,256]{2,1,0:T(8,128)S(1)}, f32[8,128,256]{2,1,0:T(8,128)}, u32[]{:S(2)}) copy-start(f32[8,128,256]{2,1,0:T(8,128)} %refs_4_.5) | copy-start | bytes 3145732
  3.1 14.7 %copy-start.1 = (f32[8,128,256]{2,1,0:T(8,128)S(1)}, f32[8,128,256]{2,1,0:T(8,128)}, u32[]{:S(2)}) copy-start(f32[8,128,256]{2,1,0:T(8,128)} %refs_5_.3) | copy-start | bytes 3145732
  3.1 14.7 %copy-start.5 = (f32[256]{0:T(256)S(1)}, f32[256]{0:T(256)}, u32[]{:S(2)}) copy-start(f32[256]{0:T(256)} %param.10) | copy-start | bytes 3076
  3.1 18.9 %collective-permute-start = (bf16[2,640,256]{2,1,0:T(8,128)(2,1)}, bf16[2,640,256]{2,1,0:T(8,128)(2,1)}, u32[]{:S(2)}, u32[]{:S(2)}) collective-permute-start(bf16[2,640,256]{2,1,0:T(8,128)(2,1)} %get-tuple-element.42.refs_0_), channel_id=1, source_target_pairs={{0,2},{1,3},{2,0},{3,1},{4,6},{5,7},{6,4},{7,5},{8,10},{9,11},{10,... | collective-permute-start | bytes 1966088 | tf_op jit(solution)/shard_map/ppermute | solution.py:325
  7.4 14.6 %collective-permute-start.4 = (bf16[2,640,256]{2,1,0:T(8,128)(2,1)}, bf16[2,640,256]{2,1,0:T(8,128)(2,1)}, u32[]{:S(2)}, u32[]{:S(2)}) collective-permute-start(bf16[2,640,256]{2,1,0:T(8,128)(2,1)} %get-tuple-element.42.refs_0_), channel_id=1, source_target_pairs={{0,1},{1,0},{2,3},{3,2},{4,5},{5,4},{6,7},{7,6},{8,9},{9,8},{10,11... | collective-permute-start | bytes 1966088 | tf_op jit(solution)/shard_map/ppermute | solution.py:322
  7.5 14.5 %collective-permute-start.5 = (bf16[2,384,256]{2,1,0:T(8,128)(2,1)S(1)}, bf16[2,384,256]{2,1,0:T(8,128)(2,1)}, u32[]{:S(2)}, u32[]{:S(2)}) collective-permute-start(bf16[2,384,256]{2,1,0:T(8,128)(2,1)S(1)} %round_chunk.3.refs_1_), channel_id=1, source_target_pairs={{0,1},{1,0},{2,3},{3,2},{4,5},{5,4},{6,7},{7,6},{8,9},{9,8},{10,11... | collective-permute-start | bytes 1179656 | tf_op jit(solution)/shard_map/ppermute | solution.py:322
  8.0 8.7 %collective-permute-start.1 = (bf16[2,128,256]{2,1,0:T(8,128)(2,1)}, bf16[2,128,256]{2,1,0:T(8,128)(2,1)}, u32[]{:S(2)}, u32[]{:S(2)}) collective-permute-start(bf16[2,128,256]{2,1,0:T(8,128)(2,1)} %get-tuple-element.37), channel_id=1, source_target_pairs={{0,4},{4,8},{8,12},{12,16},{16,20},{20,24},{24,28},{28,0},{1,5},{5... | collective-permute-start | bytes 393224 | tf_op jit(solution)/shard_map/ppermute | solution.py:328
  9.5 8.3 %collective-permute-start.2 = (bf16[2,128,256]{2,1,0:T(8,128)(2,1)}, bf16[2,128,256]{2,1,0:T(8,128)(2,1)}, u32[]{:S(2)}, u32[]{:S(2)}) collective-permute-start(bf16[2,128,256]{2,1,0:T(8,128)(2,1)} %get-tuple-element.38), channel_id=1, source_target_pairs={{4,0},{8,4},{12,8},{16,12},{20,16},{24,20},{28,24},{0,28},{5,1},{9... | collective-permute-start | bytes 393224 | tf_op jit(solution)/shard_map/ppermute | solution.py:329
  16.7 16.8 %collective-permute-start.7 = (bf16[2,384,256]{2,1,0:T(8,128)(2,1)S(1)}, bf16[2,384,256]{2,1,0:T(8,128)(2,1)S(1)}, u32[]{:S(2)}, u32[]{:S(2)}) collective-permute-start(bf16[2,384,256]{2,1,0:T(8,128)(2,1)S(1)} %round_chunk.3.refs_1_), channel_id=1, source_target_pairs={{0,2},{1,3},{2,0},{3,1},{4,6},{5,7},{6,4},{7,5},{8,10},{9,11},{10,... | collective-permute-start | bytes 1179656 | tf_op jit(solution)/shard_map/ppermute | solution.py:325
  22.0 2.3 %collective-permute-start.3 = (bf16[2,640,256]{2,1,0:T(8,128)(2,1)}, bf16[2,640,256]{2,1,0:T(8,128)(2,1)S(1)}, u32[]{:S(2)}, u32[]{:S(2)}) collective-permute-start(bf16[2,640,256]{2,1,0:T(8,128)(2,1)} %collective-permute-done.refs_0_), channel_id=1, source_target_pairs={{0,1},{1,0},{2,3},{3,2},{4,5},{5,4},{6,7},{7,6},{8,9},{9,8},{10,11... | collective-permute-start | bytes 1966088 | tf_op jit(solution)/shard_map/ppermute | solution.py:322
  22.0 2.3 %copy-start.3 = (f32[8,128,256]{2,1,0:T(8,128)S(1)}, f32[8,128,256]{2,1,0:T(8,128)}, u32[]{:S(2)}) copy-start(f32[8,128,256]{2,1,0:T(8,128)} %refs_6_.6) | copy-start | bytes 3145732
  22.1 2.3 %copy-start.4 = (f32[256]{0:T(256)S(1)}, f32[256]{0:T(256)}, u32[]{:S(2)}) copy-start(f32[256]{0:T(256)} %param.11) | copy-start | bytes 3076
  26.9 15.2 %collective-permute-start.13 = (bf16[1,640,256]{2,1,0:T(8,128)(2,1)S(1)}, bf16[1,640,256]{2,1,0:T(8,128)(2,1)S(1)}, u32[]{:S(2)}, u32[]{:S(2)}) collective-permute-start(bf16[1,640,256]{2,1,0:T(8,128)(2,1)S(1)} %get-tuple-element.45.own_ref), channel_id=1, source_target_pairs={{0,2},{1,3},{2,0},{3,1},{4,6},{5,7},{6,4},{7,5},{8,10},{9,11},{10,... | collective-permute-start | bytes 983048 | tf_op jit(solution)/shard_map/ppermute | solution.py:325
  29.0 13.2 %collective-permute-start.6 = (bf16[1,640,256]{2,1,0:T(8,128)(2,1)S(1)}, bf16[1,640,256]{2,1,0:T(8,128)(2,1)S(1)}, u32[]{:S(2)}, u32[]{:S(2)}) collective-permute-start(bf16[1,640,256]{2,1,0:T(8,128)(2,1)S(1)} %get-tuple-element.45.own_ref), channel_id=1, source_target_pairs={{0,1},{1,0},{2,3},{3,2},{4,5},{5,4},{6,7},{7,6},{8,9},{9,8},{10,11... | collective-permute-start | bytes 983048 | tf_op jit(solution)/shard_map/ppermute | solution.py:322
  29.0 6.5 %collective-permute-start.10 = (bf16[1,128,256]{2,1,0:T(8,128)(2,1)S(1)}, bf16[1,128,256]{2,1,0:T(8,128)(2,1)S(1)}, u32[]{:S(2)}, u32[]{:S(2)}) collective-permute-start(bf16[1,128,256]{2,1,0:T(8,128)(2,1)S(1)} %get-tuple-element.49), channel_id=1, source_target_pairs={{4,0},{8,4},{12,8},{16,12},{20,16},{24,20},{28,24},{0,28},{5,1},{9... | collective-permute-start | bytes 196616 | tf_op jit(solution)/shard_map/ppermute | solution.py:329
  33.5 7.0 %collective-permute-start.9 = (bf16[1,128,256]{2,1,0:T(8,128)(2,1)S(1)}, bf16[1,128,256]{2,1,0:T(8,128)(2,1)S(1)}, u32[]{:S(2)}, u32[]{:S(2)}) collective-permute-start(bf16[1,128,256]{2,1,0:T(8,128)(2,1)S(1)} %get-tuple-element.48), channel_id=1, source_target_pairs={{0,4},{4,8},{8,12},{12,16},{16,20},{20,24},{24,28},{28,0},{1,5},{5... | collective-permute-start | bytes 196616 | tf_op jit(solution)/shard_map/ppermute | solution.py:328
  33.5 7.0 %collective-permute-start.8 = (bf16[2,384,256]{2,1,0:T(8,128)(2,1)S(1)}, bf16[2,384,256]{2,1,0:T(8,128)(2,1)S(1)}, u32[]{:S(2)}, u32[]{:S(2)}) collective-permute-start(bf16[2,384,256]{2,1,0:T(8,128)(2,1)S(1)} %collective-permute-done.7.refs_0_), channel_id=1, source_target_pairs={{0,1},{1,0},{2,3},{3,2},{4,5},{5,4},{6,7},{7,6},{8,9},{9,8},{10,11... | collective-permute-start | bytes 1179656 | tf_op jit(solution)/shard_map/ppermute | solution.py:322
  41.4 1.5 %collective-permute-start.11 = (bf16[1,384,256]{2,1,0:T(8,128)(2,1)S(1)}, bf16[1,384,256]{2,1,0:T(8,128)(2,1)S(1)}, u32[]{:S(2)}, u32[]{:S(2)}) collective-permute-start(bf16[1,384,256]{2,1,0:T(8,128)(2,1)S(1)} %get-tuple-element.52.own_ref), channel_id=1, source_target_pairs={{0,1},{1,0},{2,3},{3,2},{4,5},{5,4},{6,7},{7,6},{8,9},{9,8},{10,11... | collective-permute-start | bytes 589832 | tf_op jit(solution)/shard_map/ppermute | solution.py:322
  41.5 7.3 %collective-permute-start.12 = (bf16[1,384,256]{2,1,0:T(8,128)(2,1)S(1)}, bf16[1,384,256]{2,1,0:T(8,128)(2,1)S(1)}, u32[]{:S(2)}, u32[]{:S(2)}) collective-permute-start(bf16[1,384,256]{2,1,0:T(8,128)(2,1)S(1)} %get-tuple-element.52.own_ref), channel_id=1, source_target_pairs={{0,2},{1,3},{2,0},{3,1},{4,6},{5,7},{6,4},{7,5},{8,10},{9,11},{10,... | collective-permute-start | bytes 589832 | tf_op jit(solution)/shard_map/ppermute | solution.py:325
  42.0 2.2 %collective-permute-start.14 = (bf16[1,640,256]{2,1,0:T(8,128)(2,1)S(1)}, bf16[1,640,256]{2,1,0:T(8,128)(2,1)S(1)}, u32[]{:S(2)}, u32[]{:S(2)}) collective-permute-start(bf16[1,640,256]{2,1,0:T(8,128)(2,1)S(1)} %collective-permute-done.13.far_ref), channel_id=1, source_target_pairs={{0,1},{1,0},{2,3},{3,2},{4,5},{5,4},{6,7},{7,6},{8,9},{9,8},{10,11... | collective-permute-start | bytes 983048 | tf_op jit(solution)/shard_map/ppermute | solution.py:322
  48.8 1.4 %collective-permute-start.15 = (bf16[1,384,256]{2,1,0:T(8,128)(2,1)S(1)}, bf16[1,384,256]{2,1,0:T(8,128)(2,1)S(1)}, u32[]{:S(2)}, u32[]{:S(2)}) collective-permute-start(bf16[1,384,256]{2,1,0:T(8,128)(2,1)S(1)} %collective-permute-done.12.far_ref), channel_id=1, source_target_pairs={{0,1},{1,0},{2,3},{3,2},{4,5},{5,4},{6,7},{7,6},{8,9},{9,8},{10,11... | collective-permute-start | bytes 589832 | tf_op jit(solution)/shard_map/ppermute | solution.py:322

commit v3 on v1

v3 whole, which is shorter than its diff:
```python
import jax
import jax.numpy as jnp
from jax import lax
from jax.experimental import pallas as pl
from jax.experimental.pallas import tpu as pltpu
from jax.sharding import PartitionSpec as P

DIFFUSION = 0.25
STEP_SIZE = 0.5
FIRST = STEP_SIZE / 3.0
SECOND = 2.0 * STEP_SIZE / 3.0
F32 = jnp.float32
BF16 = jnp.bfloat16
VMEM_LIMIT = 20 * 1024 * 1024
SPEC = pl.BlockSpec(memory_space=pltpu.VMEM)
ANYWHERE = pl.BlockSpec(memory_space=pl.ANY)
FROM_HBM = pl.BlockSpec(memory_space=pltpu.HBM)


def chunks_of(xcount):
    last = max(1, 3 * xcount // 8)
    start = (xcount - last + 1) // 2
    middle = list(range(start, start + last))
    return [x for x in range(xcount) if x not in middle], middle


def after(value, *others):
    return lax.optimization_barrier((value, *others))[0]


def call(body, name, args, outs, scratch=(), specs=None, out_specs=None, gflop=0.0, alias=None):
    specs = specs or [SPEC] * len(args)
    space = {id(SPEC): pltpu.VMEM, id(FROM_HBM): pltpu.HBM}
    args = [
        pltpu.with_memory_space_constraint(a, space[id(s)]) if id(s) in space else a for a, s in zip(args, specs)
    ]
    return pl.pallas_call(
        body,
        out_shape=outs,
        in_specs=specs,
        out_specs=out_specs or [SPEC] * len(outs),
        scratch_shapes=list(scratch),
        compiler_params=pltpu.CompilerParams(vmem_limit_bytes=VMEM_LIMIT),
        cost_estimate=pl.CostEstimate(flops=int(gflop * 1e9), bytes_accessed=0, transcendentals=0),
        input_output_aliases=alias or {},
        name=name,
    )(*args)


def round_chunk(fields, cells, with_faces):
    xcount, ycount, owned = fields[0].shape
    count = len(fields)

    def body(*refs):
        field_refs = refs[:count]
        out = refs[count]
        held, sems = refs[-2:]
        copies = []
        for f in range(count):
            for i, x in enumerate(cells):
                copies.append(pltpu.make_async_copy(field_refs[f].at[x], held.at[f, i], sems.at[f, i]))
                copies[-1].start()
        for f in range(count):
            for i, x in enumerate(cells):
                copies[f * len(cells) + i].wait()
                value = held[f, i].astype(BF16)
                out[f, i * ycount:(i + 1) * ycount, :] = value
                if with_faces and x == 0:
                    refs[count + 1][f] = value
                if with_faces and x == xcount - 1:
                    refs[count + 2][f] = value

    outs = [pltpu.VMEM((count, len(cells) * ycount, owned), BF16)]
    if with_faces:
        outs += [pltpu.VMEM((count, ycount, owned), BF16)] * 2
    return call(
        body, "round_chunk", fields, outs,
        scratch=[pltpu.VMEM((count, len(cells), ycount, owned), F32), pltpu.SemaphoreType.DMA((count, len(cells)))],
        specs=[FROM_HBM] * count, gflop=0.0,
    )


def blocks_dot(blocks, kernels_ref, k, owners):
    depth = blocks[0].shape[-1]
    lhs = jnp.concatenate(blocks, axis=-1)
    rhs = jnp.concatenate(
        [kernels_ref[k, pl.ds(pl.multiple_of(o * depth, depth), depth), :] for o in owners], axis=0
    )
    return jnp.dot(lhs, rhs, preferred_element_type=F32)


def along_y(core):
    return DIFFUSION * (pltpu.roll(core, 1, 0) + pltpu.roll(core, core.shape[0] - 1, 0)) - 2.0 * core


def before_first(one, two, lo, hi, growth, cells, gflop):
    xcount, ycount, owned = one.shape
    ends = [] if lo is None else [lo, hi]

    def body(one_ref, two_ref, g_ref, *refs):
        end_refs, base_ref = refs[:-1], refs[-1]
        growth = g_ref[...]
        for f, ref in enumerate((one_ref, two_ref)):
            for i, x in enumerate(cells):
                core = ref[x]
                before = ref[x - 1] if x > 0 else end_refs[0][f].astype(F32)
                behind = ref[x + 1] if x < xcount - 1 else end_refs[1][f].astype(F32)
                base_ref[f, i] = DIFFUSION * (before + behind) + along_y(core) + core * growth

    args = [one, two, growth, *ends]
    return call(
        body, "before_first", args, [pltpu.VMEM((2, len(cells), ycount, owned), F32)], gflop=gflop
    )[0]


def first_node(me, blocks, base, one, two, initial, kernels, death, cells, with_faces):
    xcount, ycount, owned = one.shape
    rows = len(cells) * ycount
    count = len(blocks)

    def body(me_ref, *refs):
        block_refs = refs[:count]
        base_ref, one_ref, two_ref, init_ref, k_ref, d_ref = refs[count:count + 6]
        refs = refs[count + 6:]
        new_ref, rounded_ref, rest_ref = refs[:3]
        sums = refs[-1]
        me = me_ref[0]
        values = [r[...].reshape(2 * rows, owned) for r in block_refs]
        for k in range(2):
            sums[k] = blocks_dot(values, k_ref, k, [me ^ j for j in range(count)]).astype(BF16)
        death = d_ref[...]
        inv_one = 1.0 / (1.0 + FIRST * death)
        inv_two = 1.0 / (1.0 + SECOND * death)
        for i, x in enumerate(cells):
            cores = (one_ref[x], two_ref[x])
            e = []
            for f in range(2):
                at = pl.ds(f * rows + i * ycount, ycount)
                e.append(base_ref[f, i] - cores[f] * sums[0, at, :].astype(F32) + sums[1, at, :].astype(F32))
            full_one = e[0] - death * cores[0]
            full_two = e[1] - death * cores[1]
            new = (
                init_ref[x]
                + FIRST * death * cores[0]
                + STEP_SIZE * (5.0 / 12.0 * full_one - 1.0 / 12.0 * full_two)
            ) * inv_one
            new_ref[i] = new
            rounded = new.astype(BF16)
            rounded_ref[0, i * ycount:(i + 1) * ycount, :] = rounded
            if with_faces and x == 0:
                refs[3][0] = rounded
            if with_faces and x == xcount - 1:
                refs[4][0] = rounded
            rest_ref[i] = (
                new - SECOND * e[0] + SECOND * death * cores[1] + STEP_SIZE / 3.0 * (full_one + full_two)
            ) * inv_two

    outs = [
        pltpu.VMEM((len(cells), ycount, owned), F32),
        pltpu.VMEM((1, rows, owned), BF16),
        pltpu.VMEM((len(cells), ycount, owned), F32),
    ]
    if with_faces:
        outs += [pltpu.VMEM((1, ycount, owned), BF16)] * 2
    args = [me, *blocks, base, one, two, initial, kernels, death]
    return call(
        body, "first_node", args, outs, scratch=[pltpu.VMEM((2, 2 * rows, owned), BF16)],
        specs=[pl.BlockSpec(memory_space=pltpu.SMEM)] + [SPEC] * (len(args) - 1), gflop=0.0,
    )


def before_second(news, rests, growth, death, chunks, c, whole, gflop):
    _, ycount, owned = news[0].shape
    xcount = sum(len(cells) for cells in chunks)
    count = len(news)
    place = {x: (n, i) for n, cells in enumerate(chunks[:count]) for i, x in enumerate(cells)}

    def body(*refs):
        new_refs, rest_ref, g_ref, d_ref = refs[:count], refs[count], refs[count + 1], refs[count + 2]
        refs = refs[count + 3:]
        base_ref = refs[0]
        copies = []
        if whole:
            whole_ref, sems = refs[1:]
            copies = [
                pltpu.make_async_copy(new_refs[n].at[i], whole_ref.at[x], sems.at[x]) for x, (n, i) in place.items()
            ]
        for copy in copies:
            copy.start()
        growth = g_ref[...]
        factor = SECOND / (1.0 + SECOND * d_ref[...])
        for i, x in enumerate(chunks[c]):
            core = new_refs[c][i]
            e = along_y(core) + core * growth
            for near in (x - 1, x + 1):
                if near in place:
                    e = e + DIFFUSION * new_refs[place[near][0]][place[near][1]]
            base_ref[i] = rest_ref[i] + factor * e
        for copy in copies:
            copy.wait()

    outs = [pltpu.VMEM((len(chunks[c]), ycount, owned), F32)]
    out_specs = [SPEC]
    scratch = []
    if whole:
        outs.append(jax.ShapeDtypeStruct((xcount, ycount, owned), F32))
        out_specs.append(ANYWHERE)
        scratch.append(pltpu.SemaphoreType.DMA((xcount,)))
    return call(
        body, "before_second", [*news, rests[c], growth, death], outs, scratch=scratch, out_specs=out_specs, gflop=gflop
    )


def second_node(me, blocks, base, new, kernels, death, cells, xcount, around=(), begun=None):
    _, ycount, owned = new.shape
    rows = len(cells) * ycount
    count = len(blocks)

    def body(me_ref, *refs):
        block_refs = refs[:count]
        base_ref, new_ref, k_ref, d_ref = refs[count:count + 4]
        around_refs = refs[count + 4:count + 4 + len(around)]
        out_ref, sums, held, sems = refs[-4:]
        me = me_ref[0]
        values = [r[...].reshape(rows, owned) for r in block_refs]
        for k in range(2):
            sums[k] = blocks_dot(values, k_ref, k, [me ^ j for j in range(count)]).astype(BF16)
        factor = SECOND / (1.0 + SECOND * d_ref[...])
        copies = []
        for i, x in enumerate(cells):
            at = pl.ds(i * ycount, ycount)
            e = sums[1, at, :].astype(F32) - new_ref[i] * sums[0, at, :].astype(F32)
            for (cell, _, j), ref in zip(around, around_refs):
                if cell == x:
                    e = e + DIFFUSION * ref[j].astype(F32)
            held[i] = base_ref[i] + factor * e
            copies.append(pltpu.make_async_copy(held.at[i], out_ref.at[x], sems.at[i]))
            copies[-1].start()
        for copy in copies:
            copy.wait()

    args = [me, *blocks, base, new, kernels, death, *[a[1] for a in around]]
    specs = [pl.BlockSpec(memory_space=pltpu.SMEM)] + [SPEC] * (len(args) - 1)
    alias = {}
    if begun is not None:
        alias = {len(args): 0}
        args.append(begun)
        specs.append(FROM_HBM)
    return call(
        body, "second_node", args, [jax.ShapeDtypeStruct((xcount, ycount, owned), F32)],
        scratch=[
            pltpu.VMEM((2, rows, owned), BF16),
            pltpu.VMEM((len(cells), ycount, owned), F32),
            pltpu.SemaphoreType.DMA((len(cells),)),
        ],
        specs=specs, out_specs=[ANYWHERE], gflop=0.0, alias=alias,
    )[0]


def local(initial, section_one, section_two, kernels, growth, death_rate):
    xcount, ycount, owned = section_one.shape
    traits = lax.axis_size("trait")
    gcount = lax.axis_size("gx")
    me = lax.axis_index("trait").reshape(1)
    growth = growth.reshape(1, owned)
    death = death_rate.reshape(1, owned)
    chunks = chunks_of(xcount)

    def to_sibling(v):
        return lax.ppermute(v, "trait", [(i, i ^ 1) for i in range(traits)])

    def to_far(v):
        return lax.ppermute(v, "trait", [(i, i ^ 2) for i in range(traits)])

    def faces(head, tail):
        lo = lax.ppermute(tail, "gx", [(i, (i + 1) % gcount) for i in range(gcount)])
        hi = lax.ppermute(head, "gx", [((i + 1) % gcount, i) for i in range(gcount)])
        return lo, hi

    own_a, head, tail = round_chunk((section_one, section_two), chunks[0], True)
    far_a = to_far(own_a)
    own_b = round_chunk((after(section_one, own_a), section_two), chunks[1], False)[0]
    far_b = to_far(own_b)
    head, tail, kernels = lax.optimization_barrier((head, tail, kernels, own_b))[:3]
    lo, hi = faces(head, tail)
    base_a = before_first(section_one, section_two, lo, hi, growth, chunks[0], 0.0)
    base_b = before_first(section_one, section_two, None, None, growth, chunks[1], 20.0)
    sib_a = to_sibling(after(own_a, own_b))
    sib_b = to_sibling(own_b)
    far_a = after(far_a, base_a)
    farsib_a = to_sibling(far_a)
    new_a, rounded_a, rest_a, new_head, new_tail = first_node(
        me, [own_a, sib_a, far_a, farsib_a], after(base_a, base_b), section_one, section_two, initial, kernels, death,
        chunks[0], True,
    )
    nfar_a = to_far(rounded_a)
    nsib_a = to_sibling(rounded_a)
    nbase_a = before_second((new_a,), (rest_a,), growth, death, chunks, 0, False, 20.0)[0]

    far_b = after(far_b, rounded_a)
    farsib_b = to_sibling(far_b)
    new_b, rounded_b, rest_b = first_node(
        me, [own_b, sib_b, far_b, farsib_b], after(base_b, nbase_a), section_one, section_two, initial, kernels, death,
        chunks[1], False,
    )
    nfar_b = to_far(rounded_b)
    nsib_b = to_sibling(rounded_b)
    new_lo, new_hi = faces(*lax.optimization_barrier((new_head, new_tail, rounded_b))[:2])
    nfar_a = after(nfar_a, rounded_b)
    nfarsib_a = to_sibling(nfar_a)
    nbase_b, new_one = before_second((new_a, new_b), (rest_a, rest_b), growth, death, chunks, 1, True, 20.0)
    around = [(0, new_lo, 0), (xcount - 1, new_hi, 0)]
    around += [(x + d, new_b, i) for i, x in enumerate(chunks[1]) for d in (-1, 1) if x + d in chunks[0]]
    two_a = second_node(
        me, [rounded_a, nsib_a, nfar_a, nfarsib_a], after(nbase_a, nbase_b), new_a, kernels, death, chunks[0], xcount,
        around,
    )
    nfar_b = after(nfar_b, two_a)
    nfarsib_b = to_sibling(nfar_b)
    new_two = second_node(
        me, [rounded_b, nsib_b, nfar_b, nfarsib_b], nbase_b, new_b, kernels, death, chunks[1], xcount, begun=two_a
    )
    return new_one, new_two


def solution(mesh):
    in_specs = (
        P("gx", None, "trait"),
        P("gx", None, "trait"),
        P("gx", None, "trait"),
        P(None, None, "trait"),
        P("trait"),
        P("trait"),
    )
    out_specs = (P("gx", None, "trait"), P("gx", None, "trait"))
    return jax.shard_map(local, mesh=mesh, in_specs=in_specs, out_specs=out_specs, check_vma=False)
```

time: 51.5 us -> 49.8 us (0.967)
  waiting for transfers between devices: 19.3 us -> 14 us
  starting transfers between devices: 14.4 us -> 16.6 us
  local copies, waits for them, and re-layouts: 1.59 us -> 3.46 us
    ppermute x2, waiting for transfers between devices: 8.28 us -> 3.38 us  [faces(): lax.ppermute(tail, 'gx', [(i, (i + 1) % gcount) for i in range(gcount)])]
    ppermute x4, waiting for transfers between devices: 7.15 us -> 4.79 us  [to_far(): return lax.ppermute(v, 'trait', [(i, i ^ 2) for i in range(traits)])]
    ppermute x8, waiting for transfers between devices: 2.1 us -> 4.19 us  [to_sibling(): return lax.ppermute(v, 'trait', [(i, i ^ 1) for i in range(traits)])]
    unnamed x16 -> x22, local copies, waits for them, and re-layouts: 1.59 us -> 3.46 us
    ppermute x2, starting transfers between devices: 5.14 us -> 6.27 us  [faces(): lax.ppermute(head, 'gx', [((i + 1) % gcount, i) for i in range(gcount)])]
    ppermute x8, starting transfers between devices: 0.36 us -> 1.16 us  [to_sibling(): return lax.ppermute(v, 'trait', [(i, i ^ 1) for i in range(traits)])]
    ppermute x2, starting transfers between devices: 2.92 us -> 3.46 us  [faces(): lax.ppermute(tail, 'gx', [(i, (i + 1) % gcount) for i in range(gcount)])]
    pallas_call x9 -> x10, Pallas kernels: 15 us -> 14.6 us  [call(): pl.pallas_call(body, out_shape=outs, in_specs=specs, out_specs=out_specs...]
  transfers between devices with their start and end apart: 16 -> 16, of which waited for: 9 -> 8; matrix products, arithmetic and copies ran while one was open for 0% -> 0% of each run, Pallas kernels for 22% -> 22%
where the time goes in v3:
time: 49.8 us; the launch traced here: 49.5 us
  starting transfers between devices  16.6 us (33%)
  Pallas kernels  14.6 us (29%)
  waiting for transfers between devices  14 us (28%)
  local copies, waits for them, and re-layouts  3.46 us (7%)
  between operations  0.81 us (2%)
    pallas_call x10, Pallas kernels, call(): pl.pallas_call(body, out_shape=outs, in_specs=specs, out_specs=out_specs...  14.6 us
    ppermute x2, starting transfers between devices, faces(): lax.ppermute(head, 'gx', [((i + 1) % gcount, i) for i in range(gcount)])  6.27 us
    ppermute x4, starting transfers between devices, to_far(): return lax.ppermute(v, 'trait', [(i, i ^ 2) for i in range(traits)])  5.71 us
    ppermute x4, waiting for transfers between devices, to_far(): return lax.ppermute(v, 'trait', [(i, i ^ 2) for i in range(traits)])  4.79 us
    ppermute x8, waiting for transfers between devices, to_sibling(): return lax.ppermute(v, 'trait', [(i, i ^ 1) for i in range(traits)])  4.19 us
    ppermute x2, starting transfers between devices, faces(): lax.ppermute(tail, 'gx', [(i, (i + 1) % gcount) for i in range(gcount)])  3.46 us
    unnamed x22, local copies, waits for them, and re-layouts  3.46 us
    ppermute x2, waiting for transfers between devices, faces(): lax.ppermute(tail, 'gx', [(i, (i + 1) % gcount) for i in range(gcount)])  3.38 us
  transfers between devices with their start and end apart: 16, of which 8 were waited for; matrix products, arithmetic and copies ran while one was open for 0% of the time, Pallas kernels for 22%

profile of v3, /device:TPU:0, one launch (start us, length us, event | category | flops | bytes accessed | tf_op | source)
XLA Modules:
  0.0 49.5 jit_solution(3450360481551208063)
XLA Ops:
  0.6 2.3 %round_chunk.2 = (bf16[2,640,256]{2,1,0:T(8,128)(2,1)}, bf16[2,128,256]{2,1,0:T(8,128)(2,1)S(1)}, bf16[2,128,256]{2,1,0:T(8,128)(2,1)S(1)}) custom-call(f32[8,128,256]{2,1,0:T(8,128)} %refs_5_.3, f32[8,128,256]{2,1,0:T(8,128)} %refs_6_.3), custom_call_target="tpu_custom_call" | custom-call | tf_op jit(solution)/shard_map/round_chunk/pallas_call | solution.py:37
  2.9 0.0 copy-start
  2.9 0.0 copy-start.1
  3.0 0.0 copy-start.10
  3.0 3.0 %collective-permute-start.1 = (bf16[2,640,256]{2,1,0:T(8,128)(2,1)}, bf16[2,640,256]{2,1,0:T(8,128)(2,1)}, u32[]{:S(2)}, u32[]{:S(2)}) collective-permute-start(bf16[2,640,256]{2,1,0:T(8,128)(2,1)} %get-tuple-element.31.refs_0_), channel_id=1, source_target_pairs={{0,2},{1,3},{2,0},{3,1},{4,6},{5,7},{6,4},{7,5},{8,10},{9,11},{10,... | collective-permute-start | bytes 1966088 | tf_op jit(solution)/shard_map/ppermute | solution.py:273
  6.0 1.3 %round_chunk.3.refs_0_ = bf16[2,384,256]{2,1,0:T(8,128)(2,1)S(1)} custom-call(f32[8,128,256]{2,1,0:T(8,128)} %refs_5_.3, f32[8,128,256]{2,1,0:T(8,128)} %refs_6_.3), custom_call_target="tpu_custom_call" | custom-call | tf_op jit(solution)/shard_map/round_chunk/pallas_call | solution.py:37
  7.3 1.5 %collective-permute-start.2 = (bf16[2,128,256]{2,1,0:T(8,128)(2,1)S(1)}, bf16[2,128,256]{2,1,0:T(8,128)(2,1)S(1)}, u32[]{:S(2)}, u32[]{:S(2)}) collective-permute-start(bf16[2,128,256]{2,1,0:T(8,128)(2,1)S(1)} %get-tuple-element.34), channel_id=1, source_target_pairs={{0,4},{4,8},{8,12},{12,16},{16,20},{20,24},{24,28},{28,0},{1,5},{5... | collective-permute-start | bytes 393224 | tf_op jit(solution)/shard_map/ppermute | solution.py:276
  8.8 3.2 %collective-permute-start.3 = (bf16[2,128,256]{2,1,0:T(8,128)(2,1)S(1)}, bf16[2,128,256]{2,1,0:T(8,128)(2,1)S(1)}, u32[]{:S(2)}, u32[]{:S(2)}) collective-permute-start(bf16[2,128,256]{2,1,0:T(8,128)(2,1)S(1)} %get-tuple-element.35), channel_id=1, source_target_pairs={{4,0},{8,4},{12,8},{16,12},{20,16},{24,20},{28,24},{0,28},{5,1},{9... | collective-permute-start | bytes 393224 | tf_op jit(solution)/shard_map/ppermute | solution.py:277
  12.0 0.4 collective-permute-start.6
  12.5 0.0 collective-permute-start.5
  12.5 2.7 %collective-permute-done.2.refs_0_ = bf16[2,128,256]{2,1,0:T(8,128)(2,1)S(1)} collective-permute-done((bf16[2,128,256]{2,1,0:T(8,128)(2,1)S(1)}, bf16[2,128,256]{2,1,0:T(8,128)(2,1)S(1)}, u32[]{:S(2)}, u32[]{:S(2)}) %collective-permute-start.2) | collective-permute-done | bytes 131104 | tf_op jit(solution)/shard_map/ppermute | solution.py:276
  15.2 0.0 collective-permute-start
  15.2 1.3 %collective-permute-done.3.refs_1_ = bf16[2,128,256]{2,1,0:T(8,128)(2,1)S(1)} collective-permute-done((bf16[2,128,256]{2,1,0:T(8,128)(2,1)S(1)}, bf16[2,128,256]{2,1,0:T(8,128)(2,1)S(1)}, u32[]{:S(2)}, u32[]{:S(2)}) %collective-permute-start.3) | collective-permute-done | bytes 131104 | tf_op jit(solution)/shard_map/ppermute | solution.py:277
  16.5 0.6 %before_first.2.refs_4_ = f32[2,5,128,256]{3,2,1,0:T(8,128)S(1)} custom-call(f32[8,128,256]{2,1,0:T(8,128)S(1)} %copy-done, f32[8,128,256]{2,1,0:T(8,128)S(1)} %copy-done.1, f32[1,256]{1,0:T(1,128)S(1)} %bitcast.9, bf16[2,128,256]{2,1,0:T(8,128)(2,1)S(1)} %collective-permute-done.2.refs_0_, bf16[2,128,256]{2,1,0:T(8,128)(2,1)S(1)} %collective-permute-done.3.refs_1_), custom_call_target="tpu_custom_call" | custom-call | tf_op jit(solution)/shard_map/before_first/pallas_call | solution.py:37
  17.1 0.0 copy-start.2
  17.1 0.0 copy-start.9
  17.1 4.8 %collective-permute-done.1.refs_2_ = bf16[2,640,256]{2,1,0:T(8,128)(2,1)} collective-permute-done((bf16[2,640,256]{2,1,0:T(8,128)(2,1)}, bf16[2,640,256]{2,1,0:T(8,128)(2,1)}, u32[]{:S(2)}, u32[]{:S(2)}) %collective-permute-start.1) | collective-permute-done | bytes 655392 | tf_op jit(solution)/shard_map/ppermute | solution.py:273
  21.9 0.0 collective-permute-start.4
  21.9 0.3 before_first.3.refs_4_
  22.2 0.0 copy-start.7
  22.2 0.9 %copy-done.7 = f32[2,3,128,256]{3,2,1,0:T(8,128)} copy-done((f32[2,3,128,256]{3,2,1,0:T(8,128)}, f32[2,3,128,256]{3,2,1,0:T(8,128)S(1)}, u32[]{:S(2)}) %copy-start.7) | copy-done | bytes 786456
  23.1 1.2 %collective-permute-done.4.refs_3_ = bf16[2,640,256]{2,1,0:T(8,128)(2,1)} collective-permute-done((bf16[2,640,256]{2,1,0:T(8,128)(2,1)}, bf16[2,640,256]{2,1,0:T(8,128)(2,1)}, u32[]{:S(2)}, u32[]{:S(2)}) %collective-permute-start.4) | collective-permute-done | bytes 655392 | tf_op jit(solution)/shard_map/ppermute | solution.py:270
  24.3 1.3 %copy-done.4 = f32[2,5,128,256]{3,2,1,0:T(8,128)S(1)} copy-done((f32[2,5,128,256]{3,2,1,0:T(8,128)S(1)}, f32[2,5,128,256]{3,2,1,0:T(8,128)}, u32[]{:S(2)}) %copy-start.4) | copy-done | bytes 1310744
  25.6 1.2 %copy-done.5 = f32[8,128,256]{2,1,0:T(8,128)S(1)} copy-done((f32[8,128,256]{2,1,0:T(8,128)S(1)}, f32[8,128,256]{2,1,0:T(8,128)}, u32[]{:S(2)}) %copy-start.5) | copy-done | bytes 1048600
  26.9 3.6 %first_node.2 = (f32[5,128,256]{2,1,0:T(8,128)S(1)}, bf16[1,640,256]{2,1,0:T(8,128)(2,1)S(1)}, f32[5,128,256]{2,1,0:T(8,128)S(1)}, bf16[1,128,256]{2,1,0:T(8,128)(2,1)S(1)}, bf16[1,128,256]{2,1,0:T(8,128)(2,1)S(1)}) custom-call(s32[1]{0:T(128)} %bitcast.me_ref, bf16[2,640,256]{2,1,0:T(8,128)(2,1)} %get-tuple-element.31.refs_0_, ...), custom_call_target="tpu_custom_call" | custom-call | tf_op jit(solution)/shard_map/first_node/pallas_call | solution.py:37
  30.5 2.1 %collective-permute-start.11 = (bf16[1,640,256]{2,1,0:T(8,128)(2,1)S(1)}, bf16[1,640,256]{2,1,0:T(8,128)(2,1)S(1)}, u32[]{:S(2)}, u32[]{:S(2)}) collective-permute-start(bf16[1,640,256]{2,1,0:T(8,128)(2,1)S(1)} %get-tuple-element.40.refs_0_), channel_id=1, source_target_pairs={{0,2},{1,3},{2,0},{3,1},{4,6},{5,7},{6,4},{7,5},{8,10},{9,11},{10,... | collective-permute-start | bytes 983048 | tf_op jit(solution)/shard_map/ppermute | solution.py:273
  32.6 0.0 collective-permute-start.10
  32.6 0.0 collective-permute-done.6.refs_2_
  32.6 0.5 %collective-permute-start.7 = (bf16[2,384,256]{2,1,0:T(8,128)(2,1)}, bf16[2,384,256]{2,1,0:T(8,128)(2,1)S(1)}, u32[]{:S(2)}, u32[]{:S(2)}) collective-permute-start(bf16[2,384,256]{2,1,0:T(8,128)(2,1)} %collective-permute-done.6.refs_2_), channel_id=1, source_target_pairs={{0,1},{1,0},{2,3},{3,2},{4,5},{5,4},{6,7},{7,6},{8,9},{9,8},{10,11... | collective-permute-start | bytes 1179656 | tf_op jit(solution)/shard_map/ppermute | solution.py:270
  33.1 0.3 before_second.2.refs_4_
  33.5 0.0 collective-permute-done.5.refs_1_
  33.5 1.6 %collective-permute-done.7.refs_3_ = bf16[2,384,256]{2,1,0:T(8,128)(2,1)S(1)} collective-permute-done((bf16[2,384,256]{2,1,0:T(8,128)(2,1)}, bf16[2,384,256]{2,1,0:T(8,128)(2,1)S(1)}, u32[]{:S(2)}, u32[]{:S(2)}) %collective-permute-start.7) | collective-permute-done | bytes 393248 | tf_op jit(solution)/shard_map/ppermute | solution.py:270
  35.0 2.3 %first_node.3 = (f32[3,128,256]{2,1,0:T(8,128)S(1)}, bf16[1,384,256]{2,1,0:T(8,128)(2,1)S(1)}, f32[3,128,256]{2,1,0:T(8,128)S(1)}) custom-call(s32[1]{0:T(128)} %bitcast.me_ref, bf16[2,384,256]{2,1,0:T(8,128)(2,1)S(1)} %round_chunk.3.refs_0_, bf16[2,384,256]{2,1,0:T(8,128)(2,1)} %collective-permute-done.5.refs_1_, ...), custom_call_target="tpu_custom_call" | custom-call | tf_op jit(solution)/shard_map/first_node/pallas_call | solution.py:37
  37.4 0.1 collective-permute-start.9
  37.5 1.9 %collective-permute-start.13 = (bf16[1,128,256]{2,1,0:T(8,128)(2,1)S(1)}, bf16[1,128,256]{2,1,0:T(8,128)(2,1)S(1)}, u32[]{:S(2)}, u32[]{:S(2)}) collective-permute-start(bf16[1,128,256]{2,1,0:T(8,128)(2,1)S(1)} %get-tuple-element.53), channel_id=1, source_target_pairs={{0,4},{4,8},{8,12},{12,16},{16,20},{20,24},{24,28},{28,0},{1,5},{5... | collective-permute-start | bytes 196616 | tf_op jit(solution)/shard_map/ppermute | solution.py:276
  39.4 3.0 %collective-permute-start.14 = (bf16[1,128,256]{2,1,0:T(8,128)(2,1)S(1)}, bf16[1,128,256]{2,1,0:T(8,128)(2,1)S(1)}, u32[]{:S(2)}, u32[]{:S(2)}) collective-permute-start(bf16[1,128,256]{2,1,0:T(8,128)(2,1)S(1)} %get-tuple-element.54), channel_id=1, source_target_pairs={{4,0},{8,4},{12,8},{16,12},{20,16},{24,20},{28,24},{0,28},{5,1},{9... | collective-permute-start | bytes 196616 | tf_op jit(solution)/shard_map/ppermute | solution.py:277
  42.5 0.0 collective-permute-done.11.refs_2_
  42.5 0.0 collective-permute-start.12
  42.5 1.0 %before_second.3 = (f32[3,128,256]{2,1,0:T(8,128)S(1)}, f32[8,128,256]{2,1,0:T(8,128)}) custom-call(f32[5,128,256]{2,1,0:T(8,128)S(1)} %get-tuple-element.39.refs_0_.refs_5_, f32[3,128,256]{2,1,0:T(8,128)S(1)} %get-tuple-element.44.refs_1_.refs_10_.refs_11_.refs_5_, f32[3,128,256]{2,1,0:T(8,128)S(1)} %get-tuple-element.45.refs_2_, f32[1,256]{1,0:T(1,128)S(1)} %bitcast.12, ...), custom_call_target="tpu_custom_call" | custom-call | flops 20000000000 | tf_op jit(solution)/shard_map/before_second/pallas_call | solution.py:37
  43.5 0.6 %collective-permute-start.8 = (bf16[1,384,256]{2,1,0:T(8,128)(2,1)S(1)}, bf16[1,384,256]{2,1,0:T(8,128)(2,1)S(1)}, u32[]{:S(2)}, u32[]{:S(2)}) collective-permute-start(bf16[1,384,256]{2,1,0:T(8,128)(2,1)S(1)} %get-tuple-element.47.refs_0_), channel_id=1, source_target_pairs={{0,1},{1,0},{2,3},{3,2},{4,5},{5,4},{6,7},{7,6},{8,9},{9,8},{10,11... | collective-permute-start | bytes 589832 | tf_op jit(solution)/shard_map/ppermute | solution.py:270
  44.1 0.7 %collective-permute-done.13.refs_8_ = bf16[1,128,256]{2,1,0:T(8,128)(2,1)S(1)} collective-permute-done((bf16[1,128,256]{2,1,0:T(8,128)(2,1)S(1)}, bf16[1,128,256]{2,1,0:T(8,128)(2,1)S(1)}, u32[]{:S(2)}, u32[]{:S(2)}) %collective-permute-start.13) | collective-permute-done | bytes 65568 | tf_op jit(solution)/shard_map/ppermute | solution.py:276
  44.8 0.3 collective-permute-done.14.refs_9_
  45.1 0.0 collective-permute-done.12.refs_3_
  45.1 1.6 %second_node.2.refs_8_ = f32[8,128,256]{2,1,0:T(8,128)} custom-call(s32[1]{0:T(128)} %bitcast.me_ref, bf16[1,640,256]{2,1,0:T(8,128)(2,1)S(1)} %get-tuple-element.40.refs_0_, bf16[1,640,256]{2,1,0:T(8,128)(2,1)S(1)} %collective-permute-done.10.refs_1_, bf16[1,640,256]{2,1,0:T(8,128)(2,1)S(1)} %collective-permute-done.11.refs_2_, ...), custom_call_target="tpu_custom_call" | custom-call | tf_op jit(solution)/shard_map/second_node/pallas_call | solution.py:37
  46.7 0.1 collective-permute-start.15
  46.8 0.0 collective-permute-done.8.refs_1_
  46.8 1.4 %collective-permute-done.15.refs_3_ = bf16[1,384,256]{2,1,0:T(8,128)(2,1)S(1)} collective-permute-done((bf16[1,384,256]{2,1,0:T(8,128)(2,1)S(1)}, bf16[1,384,256]{2,1,0:T(8,128)(2,1)S(1)}, u32[]{:S(2)}, u32[]{:S(2)}) %collective-permute-start.15) | collective-permute-done | bytes 196640 | tf_op jit(solution)/shard_map/ppermute | solution.py:270
  48.2 1.3 %second_node.3 = f32[8,128,256]{2,1,0:T(8,128)} custom-call(s32[1]{0:T(128)} %bitcast.me_ref, bf16[1,384,256]{2,1,0:T(8,128)(2,1)S(1)} %get-tuple-element.47.refs_0_, bf16[1,384,256]{2,1,0:T(8,128)(2,1)S(1)} %collective-permute-done.8.refs_1_, bf16[1,384,256]{2,1,0:T(8,128)(2,1)S(1)} %collective-permute-done.9.refs_2_, ...), custom_call_target="tpu_custom_call", output_to_operand_aliasing={{}: (9, {})} | custom-call | tf_op jit(solution)/shard_map/second_node/pallas_call | solution.py:37
  (16 shorter events, 0.0 us)
Async XLA Ops:
  2.9 13.5 %copy-start = (f32[8,128,256]{2,1,0:T(8,128)S(1)}, f32[8,128,256]{2,1,0:T(8,128)}, u32[]{:S(2)}) copy-start(f32[8,128,256]{2,1,0:T(8,128)} %refs_5_.3) | copy-start | bytes 3145732
  2.9 13.5 %copy-start.1 = (f32[8,128,256]{2,1,0:T(8,128)S(1)}, f32[8,128,256]{2,1,0:T(8,128)}, u32[]{:S(2)}) copy-start(f32[8,128,256]{2,1,0:T(8,128)} %refs_6_.3) | copy-start | bytes 3145732
  3.0 13.5 %copy-start.10 = (f32[256]{0:T(256)S(1)}, f32[256]{0:T(256)}, u32[]{:S(2)}) copy-start(f32[256]{0:T(256)} %param.10) | copy-start | bytes 3076
  3.0 18.9 %collective-permute-start.1 = (bf16[2,640,256]{2,1,0:T(8,128)(2,1)}, bf16[2,640,256]{2,1,0:T(8,128)(2,1)}, u32[]{:S(2)}, u32[]{:S(2)}) collective-permute-start(bf16[2,640,256]{2,1,0:T(8,128)(2,1)} %get-tuple-element.31.refs_0_), channel_id=1, source_target_pairs={{0,2},{1,3},{2,0},{3,1},{4,6},{5,7},{6,4},{7,5},{8,10},{9,11},{10,... | collective-permute-start | bytes 1966088 | tf_op jit(solution)/shard_map/ppermute | solution.py:273
  7.3 7.9 %collective-permute-start.2 = (bf16[2,128,256]{2,1,0:T(8,128)(2,1)S(1)}, bf16[2,128,256]{2,1,0:T(8,128)(2,1)S(1)}, u32[]{:S(2)}, u32[]{:S(2)}) collective-permute-start(bf16[2,128,256]{2,1,0:T(8,128)(2,1)S(1)} %get-tuple-element.34), channel_id=1, source_target_pairs={{0,4},{4,8},{8,12},{12,16},{16,20},{20,24},{24,28},{28,0},{1,5},{5... | collective-permute-start | bytes 393224 | tf_op jit(solution)/shard_map/ppermute | solution.py:276
  8.8 7.7 %collective-permute-start.3 = (bf16[2,128,256]{2,1,0:T(8,128)(2,1)S(1)}, bf16[2,128,256]{2,1,0:T(8,128)(2,1)S(1)}, u32[]{:S(2)}, u32[]{:S(2)}) collective-permute-start(bf16[2,128,256]{2,1,0:T(8,128)(2,1)S(1)} %get-tuple-element.35), channel_id=1, source_target_pairs={{4,0},{8,4},{12,8},{16,12},{20,16},{24,20},{28,24},{0,28},{5,1},{9... | collective-permute-start | bytes 393224 | tf_op jit(solution)/shard_map/ppermute | solution.py:277
  12.0 20.6 %collective-permute-start.6 = (bf16[2,384,256]{2,1,0:T(8,128)(2,1)S(1)}, bf16[2,384,256]{2,1,0:T(8,128)(2,1)}, u32[]{:S(2)}, u32[]{:S(2)}) collective-permute-start(bf16[2,384,256]{2,1,0:T(8,128)(2,1)S(1)} %round_chunk.3.refs_0_), channel_id=1, source_target_pairs={{0,2},{1,3},{2,0},{3,1},{4,6},{5,7},{6,4},{7,5},{8,10},{9,11},{10,... | collective-permute-start | bytes 1179656 | tf_op jit(solution)/shard_map/ppermute | solution.py:273
  12.5 21.0 %collective-permute-start.5 = (bf16[2,384,256]{2,1,0:T(8,128)(2,1)S(1)}, bf16[2,384,256]{2,1,0:T(8,128)(2,1)}, u32[]{:S(2)}, u32[]{:S(2)}) collective-permute-start(bf16[2,384,256]{2,1,0:T(8,128)(2,1)S(1)} %round_chunk.3.refs_0_), channel_id=1, source_target_pairs={{0,1},{1,0},{2,3},{3,2},{4,5},{5,4},{6,7},{7,6},{8,9},{9,8},{10,11... | collective-permute-start | bytes 1179656 | tf_op jit(solution)/shard_map/ppermute | solution.py:270
  15.2 7.9 %collective-permute-start = (bf16[2,640,256]{2,1,0:T(8,128)(2,1)}, bf16[2,640,256]{2,1,0:T(8,128)(2,1)}, u32[]{:S(2)}, u32[]{:S(2)}) collective-permute-start(bf16[2,640,256]{2,1,0:T(8,128)(2,1)} %get-tuple-element.31.refs_0_), channel_id=1, source_target_pairs={{0,1},{1,0},{2,3},{3,2},{4,5},{5,4},{6,7},{7,6},{8,9},{9,8},{10,11... | collective-permute-start | bytes 1966088 | tf_op jit(solution)/shard_map/ppermute | solution.py:270
  17.1 5.2 %copy-start.3 = (f32[2,5,128,256]{3,2,1,0:T(8,128)}, f32[2,5,128,256]{3,2,1,0:T(8,128)S(1)}, u32[]{:S(2)}) copy-start(f32[2,5,128,256]{3,2,1,0:T(8,128)S(1)} %before_first.2.refs_4_) | copy-start | bytes 3932164
  17.1 7.3 %copy-start.2 = (bf16[2,1024,256]{2,1,0:T(8,128)(2,1)S(1)}, bf16[2,1024,256]{2,1,0:T(8,128)(2,1)}, u32[]{:S(2)}) copy-start(bf16[2,1024,256]{2,1,0:T(8,128)(2,1)} %refs_6_.5) | copy-start | bytes 3145732
  17.1 7.2 %copy-start.9 = (f32[256]{0:T(256)S(1)}, f32[256]{0:T(256)}, u32[]{:S(2)}) copy-start(f32[256]{0:T(256)} %param.11) | copy-start | bytes 3076
  21.9 2.4 %collective-permute-start.4 = (bf16[2,640,256]{2,1,0:T(8,128)(2,1)}, bf16[2,640,256]{2,1,0:T(8,128)(2,1)}, u32[]{:S(2)}, u32[]{:S(2)}) collective-permute-start(bf16[2,640,256]{2,1,0:T(8,128)(2,1)} %collective-permute-done.1.refs_2_), channel_id=1, source_target_pairs={{0,1},{1,0},{2,3},{3,2},{4,5},{5,4},{6,7},{7,6},{8,9},{9,8},{10,11... | collective-permute-start | bytes 1966088 | tf_op jit(solution)/shard_map/ppermute | solution.py:270
  22.2 0.9 %copy-start.7 = (f32[2,3,128,256]{3,2,1,0:T(8,128)}, f32[2,3,128,256]{3,2,1,0:T(8,128)S(1)}, u32[]{:S(2)}) copy-start(f32[2,3,128,256]{3,2,1,0:T(8,128)S(1)} %before_first.3.refs_4_) | copy-start | bytes 2359300
  24.3 1.3 %copy-start.4 = (f32[2,5,128,256]{3,2,1,0:T(8,128)S(1)}, f32[2,5,128,256]{3,2,1,0:T(8,128)}, u32[]{:S(2)}) copy-start(f32[2,5,128,256]{3,2,1,0:T(8,128)} %copy-done.3) | copy-start | bytes 3932164
  25.6 1.2 %copy-start.5 = (f32[8,128,256]{2,1,0:T(8,128)S(1)}, f32[8,128,256]{2,1,0:T(8,128)}, u32[]{:S(2)}) copy-start(f32[8,128,256]{2,1,0:T(8,128)} %refs_7_.3) | copy-start | bytes 3145732
  30.5 12.0 %collective-permute-start.11 = (bf16[1,640,256]{2,1,0:T(8,128)(2,1)S(1)}, bf16[1,640,256]{2,1,0:T(8,128)(2,1)S(1)}, u32[]{:S(2)}, u32[]{:S(2)}) collective-permute-start(bf16[1,640,256]{2,1,0:T(8,128)(2,1)S(1)} %get-tuple-element.40.refs_0_), channel_id=1, source_target_pairs={{0,2},{1,3},{2,0},{3,1},{4,6},{5,7},{6,4},{7,5},{8,10},{9,11},{10,... | collective-permute-start | bytes 983048 | tf_op jit(solution)/shard_map/ppermute | solution.py:273
  32.6 10.9 %collective-permute-start.10 = (bf16[1,640,256]{2,1,0:T(8,128)(2,1)S(1)}, bf16[1,640,256]{2,1,0:T(8,128)(2,1)S(1)}, u32[]{:S(2)}, u32[]{:S(2)}) collective-permute-start(bf16[1,640,256]{2,1,0:T(8,128)(2,1)S(1)} %get-tuple-element.40.refs_0_), channel_id=1, source_target_pairs={{0,1},{1,0},{2,3},{3,2},{4,5},{5,4},{6,7},{7,6},{8,9},{9,8},{10,11... | collective-permute-start | bytes 983048 | tf_op jit(solution)/shard_map/ppermute | solution.py:270
  32.6 2.4 %collective-permute-start.7 = (bf16[2,384,256]{2,1,0:T(8,128)(2,1)}, bf16[2,384,256]{2,1,0:T(8,128)(2,1)S(1)}, u32[]{:S(2)}, u32[]{:S(2)}) collective-permute-start(bf16[2,384,256]{2,1,0:T(8,128)(2,1)} %collective-permute-done.6.refs_2_), channel_id=1, source_target_pairs={{0,1},{1,0},{2,3},{3,2},{4,5},{5,4},{6,7},{7,6},{8,9},{9,8},{10,11... | collective-permute-start | bytes 1179656 | tf_op jit(solution)/shard_map/ppermute | solution.py:270
  33.1 1.9 %copy-start.6 = (f32[8,128,256]{2,1,0:T(8,128)S(1)}, f32[8,128,256]{2,1,0:T(8,128)}, u32[]{:S(2)}) copy-start(f32[8,128,256]{2,1,0:T(8,128)} %refs_7_.3) | copy-start | bytes 3145732
  33.1 1.9 %copy-start.8 = (f32[2,3,128,256]{3,2,1,0:T(8,128)S(1)}, f32[2,3,128,256]{3,2,1,0:T(8,128)}, u32[]{:S(2)}) copy-start(f32[2,3,128,256]{3,2,1,0:T(8,128)} %copy-done.7) | copy-start | bytes 2359300
  37.4 9.3 %collective-permute-start.9 = (bf16[1,384,256]{2,1,0:T(8,128)(2,1)S(1)}, bf16[1,384,256]{2,1,0:T(8,128)(2,1)S(1)}, u32[]{:S(2)}, u32[]{:S(2)}) collective-permute-start(bf16[1,384,256]{2,1,0:T(8,128)(2,1)S(1)} %get-tuple-element.47.refs_0_), channel_id=1, source_target_pairs={{0,2},{1,3},{2,0},{3,1},{4,6},{5,7},{6,4},{7,5},{8,10},{9,11},{10,... | collective-permute-start | bytes 589832 | tf_op jit(solution)/shard_map/ppermute | solution.py:273
  37.5 7.3 %collective-permute-start.13 = (bf16[1,128,256]{2,1,0:T(8,128)(2,1)S(1)}, bf16[1,128,256]{2,1,0:T(8,128)(2,1)S(1)}, u32[]{:S(2)}, u32[]{:S(2)}) collective-permute-start(bf16[1,128,256]{2,1,0:T(8,128)(2,1)S(1)} %get-tuple-element.53), channel_id=1, source_target_pairs={{0,4},{4,8},{8,12},{12,16},{16,20},{20,24},{24,28},{28,0},{1,5},{5... | collective-permute-start | bytes 196616 | tf_op jit(solution)/shard_map/ppermute | solution.py:276
  39.4 5.7 %collective-permute-start.14 = (bf16[1,128,256]{2,1,0:T(8,128)(2,1)S(1)}, bf16[1,128,256]{2,1,0:T(8,128)(2,1)S(1)}, u32[]{:S(2)}, u32[]{:S(2)}) collective-permute-start(bf16[1,128,256]{2,1,0:T(8,128)(2,1)S(1)} %get-tuple-element.54), channel_id=1, source_target_pairs={{4,0},{8,4},{12,8},{16,12},{20,16},{24,20},{28,24},{0,28},{5,1},{9... | collective-permute-start | bytes 196616 | tf_op jit(solution)/shard_map/ppermute | solution.py:277
  42.5 2.6 %collective-permute-start.12 = (bf16[1,640,256]{2,1,0:T(8,128)(2,1)S(1)}, bf16[1,640,256]{2,1,0:T(8,128)(2,1)S(1)}, u32[]{:S(2)}, u32[]{:S(2)}) collective-permute-start(bf16[1,640,256]{2,1,0:T(8,128)(2,1)S(1)} %collective-permute-done.11.refs_2_), channel_id=1, source_target_pairs={{0,1},{1,0},{2,3},{3,2},{4,5},{5,4},{6,7},{7,6},{8,9},{9,8},{10,11... | collective-permute-start | bytes 983048 | tf_op jit(solution)/shard_map/ppermute | solution.py:270
  43.5 3.3 %collective-permute-start.8 = (bf16[1,384,256]{2,1,0:T(8,128)(2,1)S(1)}, bf16[1,384,256]{2,1,0:T(8,128)(2,1)S(1)}, u32[]{:S(2)}, u32[]{:S(2)}) collective-permute-start(bf16[1,384,256]{2,1,0:T(8,128)(2,1)S(1)} %get-tuple-element.47.refs_0_), channel_id=1, source_target_pairs={{0,1},{1,0},{2,3},{3,2},{4,5},{5,4},{6,7},{7,6},{8,9},{9,8},{10,11... | collective-permute-start | bytes 589832 | tf_op jit(solution)/shard_map/ppermute | solution.py:270
  46.7 1.5 %collective-permute-start.15 = (bf16[1,384,256]{2,1,0:T(8,128)(2,1)S(1)}, bf16[1,384,256]{2,1,0:T(8,128)(2,1)S(1)}, u32[]{:S(2)}, u32[]{:S(2)}) collective-permute-start(bf16[1,384,256]{2,1,0:T(8,128)(2,1)S(1)} %collective-permute-done.9.refs_2_), channel_id=1, source_target_pairs={{0,1},{1,0},{2,3},{3,2},{4,5},{5,4},{6,7},{7,6},{8,9},{9,8},{10,11... | collective-permute-start | bytes 589832 | tf_op jit(solution)/shard_map/ppermute | solution.py:270

commit v4 on v3

--- a/solution.py
+++ b/solution.py
@@ -113,18 +113,18 @@
     )[0]
 
 
-def first_node(me, blocks, base, one, two, initial, kernels, death, cells, with_faces):
+def first_node(blocks, base, one, two, initial, kernels, death, cells, with_faces):
     xcount, ycount, owned = one.shape
     rows = len(cells) * ycount
     count = len(blocks)
 
-    def body(me_ref, *refs):
+    def body(*refs):
         block_refs = refs[:count]
         base_ref, one_ref, two_ref, init_ref, k_ref, d_ref = refs[count:count + 6]
         refs = refs[count + 6:]
         new_ref, rounded_ref, rest_ref = refs[:3]
         sums = refs[-1]
-        me = me_ref[0]
+        me = lax.axis_index("trait")
         values = [r[...].reshape(2 * rows, owned) for r in block_refs]
         for k in range(2):
             sums[k] = blocks_dot(values, k_ref, k, [me ^ j for j in range(count)]).astype(BF16)
@@ -162,10 +162,10 @@
     ]
     if with_faces:
         outs += [pltpu.VMEM((1, ycount, owned), BF16)] * 2
-    args = [me, *blocks, base, one, two, initial, kernels, death]
+    args = [*blocks, base, one, two, initial, kernels, death]
     return call(
         body, "first_node", args, outs, scratch=[pltpu.VMEM((2, 2 * rows, owned), BF16)],
-        specs=[pl.BlockSpec(memory_space=pltpu.SMEM)] + [SPEC] * (len(args) - 1), gflop=0.0,
+        gflop=0.0,
     )
 
 
@@ -211,17 +211,17 @@
     )
 
 
-def second_node(me, blocks, base, new, kernels, death, cells, xcount, around=(), begun=None):
+def second_node(blocks, base, new, kernels, death, cells, xcount, around=(), begun=None):
     _, ycount, owned = new.shape
     rows = len(cells) * ycount
     count = len(blocks)
 
-    def body(me_ref, *refs):
+    def body(*refs):
         block_refs = refs[:count]
         base_ref, new_ref, k_ref, d_ref = refs[count:count + 4]
         around_refs = refs[count + 4:count + 4 + len(around)]
         out_ref, sums, held, sems = refs[-4:]
-        me = me_ref[0]
+        me = lax.axis_index("trait")
         values = [r[...].reshape(rows, owned) for r in block_refs]
         for k in range(2):
             sums[k] = blocks_dot(values, k_ref, k, [me ^ j for j in range(count)]).astype(BF16)
@@ -239,8 +239,8 @@
         for copy in copies:
             copy.wait()
 
-    args = [me, *blocks, base, new, kernels, death, *[a[1] for a in around]]
-    specs = [pl.BlockSpec(memory_space=pltpu.SMEM)] + [SPEC] * (len(args) - 1)
+    args = [*blocks, base, new, kernels, death, *[a[1] for a in around]]
+    specs = [SPEC] * len(args)
     alias = {}
     if begun is not None:
         alias = {len(args): 0}
@@ -261,7 +261,6 @@
     xcount, ycount, owned = section_one.shape
     traits = lax.axis_size("trait")
     gcount = lax.axis_size("gx")
-    me = lax.axis_index("trait").reshape(1)
     growth = growth.reshape(1, owned)
     death = death_rate.reshape(1, owned)
     chunks = chunks_of(xcount)
@@ -290,7 +289,7 @@
     far_a = after(far_a, base_a)
     farsib_a = to_sibling(far_a)
     new_a, rounded_a, rest_a, new_head, new_tail = first_node(
-        me, [own_a, sib_a, far_a, farsib_a], after(base_a, base_b), section_one, section_two, initial, kernels, death,
+        [own_a, sib_a, far_a, farsib_a], after(base_a, base_b), section_one, section_two, initial, kernels, death,
         chunks[0], True,
     )
     nfar_a = to_far(rounded_a)
@@ -300,7 +299,7 @@
     far_b = after(far_b, rounded_a)
     farsib_b = to_sibling(far_b)
     new_b, rounded_b, rest_b = first_node(
-        me, [own_b, sib_b, far_b, farsib_b], after(base_b, nbase_a), section_one, section_two, initial, kernels, death,
+        [own_b, sib_b, far_b, farsib_b], after(base_b, nbase_a), section_one, section_two, initial, kernels, death,
         chunks[1], False,
     )
     nfar_b = to_far(rounded_b)
@@ -312,13 +311,13 @@
     around = [(0, new_lo, 0), (xcount - 1, new_hi, 0)]
     around += [(x + d, new_b, i) for i, x in enumerate(chunks[1]) for d in (-1, 1) if x + d in chunks[0]]
     two_a = second_node(
-        me, [rounded_a, nsib_a, nfar_a, nfarsib_a], after(nbase_a, nbase_b), new_a, kernels, death, chunks[0], xcount,
+        [rounded_a, nsib_a, nfar_a, nfarsib_a], after(nbase_a, nbase_b), new_a, kernels, death, chunks[0], xcount,
         around,
     )
     nfar_b = after(nfar_b, two_a)
     nfarsib_b = to_sibling(nfar_b)
     new_two = second_node(
-        me, [rounded_b, nsib_b, nfar_b, nfarsib_b], nbase_b, new_b, kernels, death, chunks[1], xcount, begun=two_a
+        [rounded_b, nsib_b, nfar_b, nfarsib_b], nbase_b, new_b, kernels, death, chunks[1], xcount, begun=two_a
     )
     return new_one, new_two
 

time: 49.8 us -> 45.1 us (0.906)
  Pallas kernels: 14.6 us -> 11.1 us
  local copies, waits for them, and re-layouts: 3.46 us -> 0.04 us
  waiting for transfers between devices: 14 us -> 15.5 us
  starting transfers between devices: 16.6 us -> 17.5 us
    pallas_call x10, Pallas kernels: 14.6 us -> 11.1 us  [call(): pl.pallas_call(body, out_shape=outs, in_specs=specs, out_specs=out_specs...]
    unnamed x22 -> x12, local copies, waits for them, and re-layouts: 3.46 us -> 0.04 us
    ppermute x4, starting transfers between devices: 5.71 us -> 7.38 us  [to_far(): return lax.ppermute(v, 'trait', [(i, i ^ 2) for i in range(traits)])]
    ppermute x4, waiting for transfers between devices: 4.79 us -> 6.11 us  [to_far(): return lax.ppermute(v, 'trait', [(i, i ^ 2) for i in range(traits)])]
    ppermute x8, starting transfers between devices: 1.16 us -> 0.66 us  [to_sibling(): return lax.ppermute(v, 'trait', [(i, i ^ 1) for i in range(traits)])]
  transfers between devices with their start and end apart: 16 -> 16, of which waited for: 8 -> 9; matrix products, arithmetic and copies ran while one was open for 0% -> 0% of each run, Pallas kernels for 22% -> 19%
where the time goes in v4:
time: 45.1 us; the launch traced here: 44.9 us
  starting transfers between devices  17.5 us (39%)
  waiting for transfers between devices  15.5 us (34%)
  Pallas kernels  11.1 us (25%)
  between operations  0.8 us (2%)
    pallas_call x10, Pallas kernels, call(): pl.pallas_call(body, out_shape=outs, in_specs=specs, out_specs=out_specs...  11.1 us
    ppermute x4, starting transfers between devices, to_far(): return lax.ppermute(v, 'trait', [(i, i ^ 2) for i in range(traits)])  7.38 us
    ppermute x2, starting transfers between devices, faces(): lax.ppermute(head, 'gx', [((i + 1) % gcount, i) for i in range(gcount)])  6.46 us
    ppermute x4, waiting for transfers between devices, to_far(): return lax.ppermute(v, 'trait', [(i, i ^ 2) for i in range(traits)])  6.11 us
    ppermute x8, waiting for transfers between devices, to_sibling(): return lax.ppermute(v, 'trait', [(i, i ^ 1) for i in range(traits)])  4.55 us
    ppermute x2, waiting for transfers between devices, faces(): lax.ppermute(tail, 'gx', [(i, (i + 1) % gcount) for i in range(gcount)])  3.38 us
    ppermute x2, starting transfers between devices, faces(): lax.ppermute(tail, 'gx', [(i, (i + 1) % gcount) for i in range(gcount)])  3.03 us
    ppermute x2, waiting for transfers between devices, faces(): lax.ppermute(head, 'gx', [((i + 1) % gcount, i) for i in range(gcount)])  1.44 us
  transfers between devices with their start and end apart: 16, of which 9 were waited for; matrix products, arithmetic and copies ran while one was open for 0% of the time, Pallas kernels for 19%

profile of v4, /device:TPU:0, one launch (start us, length us, event | category | flops | bytes accessed | tf_op | source)
XLA Modules:
  0.0 44.9 jit_solution(17812304902889997239)
XLA Ops:
  0.6 1.5 %round_chunk.2 = (bf16[2,640,256]{2,1,0:T(8,128)(2,1)S(1)}, bf16[2,128,256]{2,1,0:T(8,128)(2,1)S(1)}, bf16[2,128,256]{2,1,0:T(8,128)(2,1)S(1)}) custom-call(f32[8,128,256]{2,1,0:T(8,128)} %refs_5_.3, f32[8,128,256]{2,1,0:T(8,128)} %refs_6_.3), custom_call_target="tpu_custom_call" | custom-call | tf_op jit(solution)/shard_map/round_chunk/pallas_call | solution.py:37
  2.1 0.0 copy-start
  2.1 0.0 copy-start.1
  2.1 0.0 copy-start.5
  2.1 3.0 %collective-permute-start.1 = (bf16[2,640,256]{2,1,0:T(8,128)(2,1)S(1)}, bf16[2,640,256]{2,1,0:T(8,128)(2,1)S(1)}, u32[]{:S(2)}, u32[]{:S(2)}) collective-permute-start(bf16[2,640,256]{2,1,0:T(8,128)(2,1)S(1)} %get-tuple-element.31.refs_0_), channel_id=1, source_target_pairs={{0,2},{1,3},{2,0},{3,1},{4,6},{5,7},{6,4},{7,5},{8,10},{9,11},{10,... | collective-permute-start | bytes 1966088 | tf_op jit(solution)/shard_map/ppermute | solution.py:272
  5.2 1.3 %round_chunk.3.refs_0_ = bf16[2,384,256]{2,1,0:T(8,128)(2,1)S(1)} custom-call(f32[8,128,256]{2,1,0:T(8,128)} %refs_5_.3, f32[8,128,256]{2,1,0:T(8,128)} %refs_6_.3), custom_call_target="tpu_custom_call" | custom-call | tf_op jit(solution)/shard_map/round_chunk/pallas_call | solution.py:37
  6.4 1.5 %collective-permute-start.2 = (bf16[2,128,256]{2,1,0:T(8,128)(2,1)S(1)}, bf16[2,128,256]{2,1,0:T(8,128)(2,1)S(1)}, u32[]{:S(2)}, u32[]{:S(2)}) collective-permute-start(bf16[2,128,256]{2,1,0:T(8,128)(2,1)S(1)} %get-tuple-element.34), channel_id=1, source_target_pairs={{0,4},{4,8},{8,12},{12,16},{16,20},{20,24},{24,28},{28,0},{1,5},{5... | collective-permute-start | bytes 393224 | tf_op jit(solution)/shard_map/ppermute | solution.py:275
  8.0 3.2 %collective-permute-start.3 = (bf16[2,128,256]{2,1,0:T(8,128)(2,1)S(1)}, bf16[2,128,256]{2,1,0:T(8,128)(2,1)S(1)}, u32[]{:S(2)}, u32[]{:S(2)}) collective-permute-start(bf16[2,128,256]{2,1,0:T(8,128)(2,1)S(1)} %get-tuple-element.35), channel_id=1, source_target_pairs={{4,0},{8,4},{12,8},{16,12},{20,16},{24,20},{28,24},{0,28},{5,1},{9... | collective-permute-start | bytes 393224 | tf_op jit(solution)/shard_map/ppermute | solution.py:276
  11.2 0.4 collective-permute-start.6
  11.6 0.0 collective-permute-start.5
  11.6 2.7 %collective-permute-done.2.refs_0_ = bf16[2,128,256]{2,1,0:T(8,128)(2,1)S(1)} collective-permute-done((bf16[2,128,256]{2,1,0:T(8,128)(2,1)S(1)}, bf16[2,128,256]{2,1,0:T(8,128)(2,1)S(1)}, u32[]{:S(2)}, u32[]{:S(2)}) %collective-permute-start.2) | collective-permute-done | bytes 131104 | tf_op jit(solution)/shard_map/ppermute | solution.py:275
  14.3 0.0 collective-permute-start
  14.3 1.3 %collective-permute-done.3.refs_1_ = bf16[2,128,256]{2,1,0:T(8,128)(2,1)S(1)} collective-permute-done((bf16[2,128,256]{2,1,0:T(8,128)(2,1)S(1)}, bf16[2,128,256]{2,1,0:T(8,128)(2,1)S(1)}, u32[]{:S(2)}, u32[]{:S(2)}) %collective-permute-start.3) | collective-permute-done | bytes 131104 | tf_op jit(solution)/shard_map/ppermute | solution.py:276
  15.6 0.6 %before_first.2.refs_4_ = f32[2,5,128,256]{3,2,1,0:T(8,128)S(1)} custom-call(f32[8,128,256]{2,1,0:T(8,128)S(1)} %copy-done, f32[8,128,256]{2,1,0:T(8,128)S(1)} %copy-done.1, f32[1,256]{1,0:T(1,128)S(1)} %bitcast.8, bf16[2,128,256]{2,1,0:T(8,128)(2,1)S(1)} %collective-permute-done.2.refs_0_, bf16[2,128,256]{2,1,0:T(8,128)(2,1)S(1)} %collective-permute-done.3.refs_1_), custom_call_target="tpu_custom_call" | custom-call | tf_op jit(solution)/shard_map/before_first/pallas_call | solution.py:37
  16.2 0.0 copy-start.2
  16.2 0.0 copy-start.3
  16.3 0.0 copy-start.4
  16.3 4.5 %collective-permute-done.1.refs_2_ = bf16[2,640,256]{2,1,0:T(8,128)(2,1)S(1)} collective-permute-done((bf16[2,640,256]{2,1,0:T(8,128)(2,1)S(1)}, bf16[2,640,256]{2,1,0:T(8,128)(2,1)S(1)}, u32[]{:S(2)}, u32[]{:S(2)}) %collective-permute-start.1) | collective-permute-done | bytes 655392 | tf_op jit(solution)/shard_map/ppermute | solution.py:272
  20.7 0.0 collective-permute-start.4
  20.7 0.3 before_first.3.refs_4_
  21.1 0.0 collective-permute-done.refs_1_
  21.1 1.7 %collective-permute-done.4.refs_3_ = bf16[2,640,256]{2,1,0:T(8,128)(2,1)S(1)} collective-permute-done((bf16[2,640,256]{2,1,0:T(8,128)(2,1)S(1)}, bf16[2,640,256]{2,1,0:T(8,128)(2,1)S(1)}, u32[]{:S(2)}, u32[]{:S(2)}) %collective-permute-start.4) | collective-permute-done | bytes 655392 | tf_op jit(solution)/shard_map/ppermute | solution.py:269
  22.8 2.0 %first_node.2 = (f32[5,128,256]{2,1,0:T(8,128)S(1)}, bf16[1,640,256]{2,1,0:T(8,128)(2,1)S(1)}, f32[5,128,256]{2,1,0:T(8,128)S(1)}, bf16[1,128,256]{2,1,0:T(8,128)(2,1)S(1)}, bf16[1,128,256]{2,1,0:T(8,128)(2,1)S(1)}) custom-call(bf16[2,640,256]{2,1,0:T(8,128)(2,1)S(1)} %get-tuple-element.31.refs_0_, bf16[2,640,256]{2,1,0:T(8,128)(2,1)S(1)} %collective-permute-done.refs_1_, ...), custom_call_target="tpu_custom_call" | custom-call | tf_op jit(solution)/shard_map/first_node/pallas_call | solution.py:37
  24.9 2.1 %collective-permute-start.11 = (bf16[1,640,256]{2,1,0:T(8,128)(2,1)S(1)}, bf16[1,640,256]{2,1,0:T(8,128)(2,1)S(1)}, u32[]{:S(2)}, u32[]{:S(2)}) collective-permute-start(bf16[1,640,256]{2,1,0:T(8,128)(2,1)S(1)} %get-tuple-element.40.refs_0_), channel_id=1, source_target_pairs={{0,2},{1,3},{2,0},{3,1},{4,6},{5,7},{6,4},{7,5},{8,10},{9,11},{10,... | collective-permute-start | bytes 983048 | tf_op jit(solution)/shard_map/ppermute | solution.py:272
  27.0 0.0 collective-permute-start.10
  27.0 1.6 %collective-permute-done.6.refs_2_ = bf16[2,384,256]{2,1,0:T(8,128)(2,1)S(1)} collective-permute-done((bf16[2,384,256]{2,1,0:T(8,128)(2,1)S(1)}, bf16[2,384,256]{2,1,0:T(8,128)(2,1)S(1)}, u32[]{:S(2)}, u32[]{:S(2)}) %collective-permute-start.6) | collective-permute-done | bytes 393248 | tf_op jit(solution)/shard_map/ppermute | solution.py:272
  28.6 0.0 collective-permute-start.7
  28.6 0.3 before_second.2.refs_4_
  29.0 0.0 collective-permute-done.5.refs_1_
  29.0 1.4 %collective-permute-done.7.refs_3_ = bf16[2,384,256]{2,1,0:T(8,128)(2,1)S(1)} collective-permute-done((bf16[2,384,256]{2,1,0:T(8,128)(2,1)S(1)}, bf16[2,384,256]{2,1,0:T(8,128)(2,1)S(1)}, u32[]{:S(2)}, u32[]{:S(2)}) %collective-permute-start.7) | collective-permute-done | bytes 393248 | tf_op jit(solution)/shard_map/ppermute | solution.py:269
  30.3 1.2 %first_node.3 = (f32[3,128,256]{2,1,0:T(8,128)S(1)}, bf16[1,384,256]{2,1,0:T(8,128)(2,1)S(1)}, f32[3,128,256]{2,1,0:T(8,128)S(1)}) custom-call(bf16[2,384,256]{2,1,0:T(8,128)(2,1)S(1)} %round_chunk.3.refs_0_, bf16[2,384,256]{2,1,0:T(8,128)(2,1)S(1)} %collective-permute-done.5.refs_1_, bf16[2,384,256]{2,1,0:T(8,128)(2,1)S(1)} %collective-permute-done.6.refs_2_, ...), custom_call_target="tpu_custom_call" | custom-call | tf_op jit(solution)/shard_map/first_node/pallas_call | solution.py:37
  31.6 1.8 %collective-permute-start.9 = (bf16[1,384,256]{2,1,0:T(8,128)(2,1)S(1)}, bf16[1,384,256]{2,1,0:T(8,128)(2,1)S(1)}, u32[]{:S(2)}, u32[]{:S(2)}) collective-permute-start(bf16[1,384,256]{2,1,0:T(8,128)(2,1)S(1)} %get-tuple-element.47.refs_0_), channel_id=1, source_target_pairs={{0,2},{1,3},{2,0},{3,1},{4,6},{5,7},{6,4},{7,5},{8,10},{9,11},{10,... | collective-permute-start | bytes 589832 | tf_op jit(solution)/shard_map/ppermute | solution.py:272
  33.4 1.5 %collective-permute-start.13 = (bf16[1,128,256]{2,1,0:T(8,128)(2,1)S(1)}, bf16[1,128,256]{2,1,0:T(8,128)(2,1)S(1)}, u32[]{:S(2)}, u32[]{:S(2)}) collective-permute-start(bf16[1,128,256]{2,1,0:T(8,128)(2,1)S(1)} %get-tuple-element.53), channel_id=1, source_target_pairs={{0,4},{4,8},{8,12},{12,16},{16,20},{20,24},{24,28},{28,0},{1,5},{5... | collective-permute-start | bytes 196616 | tf_op jit(solution)/shard_map/ppermute | solution.py:275
  34.9 3.2 %collective-permute-start.14 = (bf16[1,128,256]{2,1,0:T(8,128)(2,1)S(1)}, bf16[1,128,256]{2,1,0:T(8,128)(2,1)S(1)}, u32[]{:S(2)}, u32[]{:S(2)}) collective-permute-start(bf16[1,128,256]{2,1,0:T(8,128)(2,1)S(1)} %get-tuple-element.54), channel_id=1, source_target_pairs={{4,0},{8,4},{12,8},{16,12},{20,16},{24,20},{28,24},{0,28},{5,1},{9... | collective-permute-start | bytes 196616 | tf_op jit(solution)/shard_map/ppermute | solution.py:276
  38.1 0.0 collective-permute-done.11.refs_2_
  38.1 0.0 collective-permute-start.12
  38.1 1.0 %before_second.3 = (f32[3,128,256]{2,1,0:T(8,128)S(1)}, f32[8,128,256]{2,1,0:T(8,128)}) custom-call(f32[5,128,256]{2,1,0:T(8,128)S(1)} %get-tuple-element.39.refs_0_.refs_5_, f32[3,128,256]{2,1,0:T(8,128)S(1)} %get-tuple-element.44.refs_1_.refs_10_.refs_11_.refs_5_, f32[3,128,256]{2,1,0:T(8,128)S(1)} %get-tuple-element.45.refs_2_, f32[1,256]{1,0:T(1,128)S(1)} %bitcast.11, ...), custom_call_target="tpu_custom_call" | custom-call | flops 20000000000 | tf_op jit(solution)/shard_map/before_second/pallas_call | solution.py:37
  39.1 0.0 collective-permute-done.10.refs_1_
  39.2 0.6 %collective-permute-start.8 = (bf16[1,384,256]{2,1,0:T(8,128)(2,1)S(1)}, bf16[1,384,256]{2,1,0:T(8,128)(2,1)S(1)}, u32[]{:S(2)}, u32[]{:S(2)}) collective-permute-start(bf16[1,384,256]{2,1,0:T(8,128)(2,1)S(1)} %get-tuple-element.47.refs_0_), channel_id=1, source_target_pairs={{0,1},{1,0},{2,3},{3,2},{4,5},{5,4},{6,7},{7,6},{8,9},{9,8},{10,11... | collective-permute-start | bytes 589832 | tf_op jit(solution)/shard_map/ppermute | solution.py:269
  39.7 0.7 %collective-permute-done.13.refs_8_ = bf16[1,128,256]{2,1,0:T(8,128)(2,1)S(1)} collective-permute-done((bf16[1,128,256]{2,1,0:T(8,128)(2,1)S(1)}, bf16[1,128,256]{2,1,0:T(8,128)(2,1)S(1)}, u32[]{:S(2)}, u32[]{:S(2)}) %collective-permute-start.13) | collective-permute-done | bytes 65568 | tf_op jit(solution)/shard_map/ppermute | solution.py:275
  40.4 0.1 collective-permute-done.14.refs_9_
  40.5 0.0 collective-permute-done.12.refs_3_
  40.5 1.6 %second_node.2.refs_8_ = f32[8,128,256]{2,1,0:T(8,128)} custom-call(bf16[1,640,256]{2,1,0:T(8,128)(2,1)S(1)} %get-tuple-element.40.refs_0_, bf16[1,640,256]{2,1,0:T(8,128)(2,1)S(1)} %collective-permute-done.10.refs_1_, bf16[1,640,256]{2,1,0:T(8,128)(2,1)S(1)} %collective-permute-done.11.refs_2_, bf16[1,640,256]{2,1,0:T(8,128)(2,1)S(1)} %collective-permute-done.12.refs_3_, ...), custom_call_target="tpu_custom_call" | custom-call | tf_op jit(solution)/shard_map/second_node/pallas_call | solution.py:37
  42.1 0.0 collective-permute-done.9.refs_2_
  42.2 0.1 collective-permute-start.15
  42.2 0.0 collective-permute-done.8.refs_1_
  42.2 1.4 %collective-permute-done.15.refs_3_ = bf16[1,384,256]{2,1,0:T(8,128)(2,1)S(1)} collective-permute-done((bf16[1,384,256]{2,1,0:T(8,128)(2,1)S(1)}, bf16[1,384,256]{2,1,0:T(8,128)(2,1)S(1)}, u32[]{:S(2)}, u32[]{:S(2)}) %collective-permute-start.15) | collective-permute-done | bytes 196640 | tf_op jit(solution)/shard_map/ppermute | solution.py:269
  43.7 1.3 %second_node.3 = f32[8,128,256]{2,1,0:T(8,128)} custom-call(bf16[1,384,256]{2,1,0:T(8,128)(2,1)S(1)} %get-tuple-element.47.refs_0_, bf16[1,384,256]{2,1,0:T(8,128)(2,1)S(1)} %collective-permute-done.8.refs_1_, bf16[1,384,256]{2,1,0:T(8,128)(2,1)S(1)} %collective-permute-done.9.refs_2_, ...), custom_call_target="tpu_custom_call", output_to_operand_aliasing={{}: (8, {})} | custom-call | tf_op jit(solution)/shard_map/second_node/pallas_call | solution.py:37
  (6 shorter events, 0.0 us)
Async XLA Ops:
  2.1 13.5 %copy-start = (f32[8,128,256]{2,1,0:T(8,128)S(1)}, f32[8,128,256]{2,1,0:T(8,128)}, u32[]{:S(2)}) copy-start(f32[8,128,256]{2,1,0:T(8,128)} %refs_5_.3) | copy-start | bytes 3145732
  2.1 13.5 %copy-start.1 = (f32[8,128,256]{2,1,0:T(8,128)S(1)}, f32[8,128,256]{2,1,0:T(8,128)}, u32[]{:S(2)}) copy-start(f32[8,128,256]{2,1,0:T(8,128)} %refs_6_.3) | copy-start | bytes 3145732
  2.1 13.5 %copy-start.5 = (f32[256]{0:T(256)S(1)}, f32[256]{0:T(256)}, u32[]{:S(2)}) copy-start(f32[256]{0:T(256)} %param.10) | copy-start | bytes 3076
  2.1 18.6 %collective-permute-start.1 = (bf16[2,640,256]{2,1,0:T(8,128)(2,1)S(1)}, bf16[2,640,256]{2,1,0:T(8,128)(2,1)S(1)}, u32[]{:S(2)}, u32[]{:S(2)}) collective-permute-start(bf16[2,640,256]{2,1,0:T(8,128)(2,1)S(1)} %get-tuple-element.31.refs_0_), channel_id=1, source_target_pairs={{0,2},{1,3},{2,0},{3,1},{4,6},{5,7},{6,4},{7,5},{8,10},{9,11},{10,... | collective-permute-start | bytes 1966088 | tf_op jit(solution)/shard_map/ppermute | solution.py:272
  6.4 7.9 %collective-permute-start.2 = (bf16[2,128,256]{2,1,0:T(8,128)(2,1)S(1)}, bf16[2,128,256]{2,1,0:T(8,128)(2,1)S(1)}, u32[]{:S(2)}, u32[]{:S(2)}) collective-permute-start(bf16[2,128,256]{2,1,0:T(8,128)(2,1)S(1)} %get-tuple-element.34), channel_id=1, source_target_pairs={{0,4},{4,8},{8,12},{12,16},{16,20},{20,24},{24,28},{28,0},{1,5},{5... | collective-permute-start | bytes 393224 | tf_op jit(solution)/shard_map/ppermute | solution.py:275
  8.0 7.7 %collective-permute-start.3 = (bf16[2,128,256]{2,1,0:T(8,128)(2,1)S(1)}, bf16[2,128,256]{2,1,0:T(8,128)(2,1)S(1)}, u32[]{:S(2)}, u32[]{:S(2)}) collective-permute-start(bf16[2,128,256]{2,1,0:T(8,128)(2,1)S(1)} %get-tuple-element.35), channel_id=1, source_target_pairs={{4,0},{8,4},{12,8},{16,12},{20,16},{24,20},{28,24},{0,28},{5,1},{9... | collective-permute-start | bytes 393224 | tf_op jit(solution)/shard_map/ppermute | solution.py:276
  11.2 17.4 %collective-permute-start.6 = (bf16[2,384,256]{2,1,0:T(8,128)(2,1)S(1)}, bf16[2,384,256]{2,1,0:T(8,128)(2,1)S(1)}, u32[]{:S(2)}, u32[]{:S(2)}) collective-permute-start(bf16[2,384,256]{2,1,0:T(8,128)(2,1)S(1)} %round_chunk.3.refs_0_), channel_id=1, source_target_pairs={{0,2},{1,3},{2,0},{3,1},{4,6},{5,7},{6,4},{7,5},{8,10},{9,11},{10,... | collective-permute-start | bytes 1179656 | tf_op jit(solution)/shard_map/ppermute | solution.py:272
  11.6 17.3 %collective-permute-start.5 = (bf16[2,384,256]{2,1,0:T(8,128)(2,1)S(1)}, bf16[2,384,256]{2,1,0:T(8,128)(2,1)S(1)}, u32[]{:S(2)}, u32[]{:S(2)}) collective-permute-start(bf16[2,384,256]{2,1,0:T(8,128)(2,1)S(1)} %round_chunk.3.refs_0_), channel_id=1, source_target_pairs={{0,1},{1,0},{2,3},{3,2},{4,5},{5,4},{6,7},{7,6},{8,9},{9,8},{10,11... | collective-permute-start | bytes 1179656 | tf_op jit(solution)/shard_map/ppermute | solution.py:269
  14.3 6.7 %collective-permute-start = (bf16[2,640,256]{2,1,0:T(8,128)(2,1)S(1)}, bf16[2,640,256]{2,1,0:T(8,128)(2,1)S(1)}, u32[]{:S(2)}, u32[]{:S(2)}) collective-permute-start(bf16[2,640,256]{2,1,0:T(8,128)(2,1)S(1)} %get-tuple-element.31.refs_0_), channel_id=1, source_target_pairs={{0,1},{1,0},{2,3},{3,2},{4,5},{5,4},{6,7},{7,6},{8,9},{9,8},{10,11... | collective-permute-start | bytes 1966088 | tf_op jit(solution)/shard_map/ppermute | solution.py:269
  16.2 6.6 %copy-start.2 = (bf16[2,1024,256]{2,1,0:T(8,128)(2,1)S(1)}, bf16[2,1024,256]{2,1,0:T(8,128)(2,1)}, u32[]{:S(2)}) copy-start(bf16[2,1024,256]{2,1,0:T(8,128)(2,1)} %refs_6_.5) | copy-start | bytes 3145732
  16.2 6.6 %copy-start.3 = (f32[8,128,256]{2,1,0:T(8,128)S(1)}, f32[8,128,256]{2,1,0:T(8,128)}, u32[]{:S(2)}) copy-start(f32[8,128,256]{2,1,0:T(8,128)} %refs_7_.3) | copy-start | bytes 3145732
  16.3 6.6 %copy-start.4 = (f32[256]{0:T(256)S(1)}, f32[256]{0:T(256)}, u32[]{:S(2)}) copy-start(f32[256]{0:T(256)} %param.11) | copy-start | bytes 3076
  20.7 2.1 %collective-permute-start.4 = (bf16[2,640,256]{2,1,0:T(8,128)(2,1)S(1)}, bf16[2,640,256]{2,1,0:T(8,128)(2,1)S(1)}, u32[]{:S(2)}, u32[]{:S(2)}) collective-permute-start(bf16[2,640,256]{2,1,0:T(8,128)(2,1)S(1)} %collective-permute-done.1.refs_2_), channel_id=1, source_target_pairs={{0,1},{1,0},{2,3},{3,2},{4,5},{5,4},{6,7},{7,6},{8,9},{9,8},{10,11... | collective-permute-start | bytes 1966088 | tf_op jit(solution)/shard_map/ppermute | solution.py:269
  24.9 13.2 %collective-permute-start.11 = (bf16[1,640,256]{2,1,0:T(8,128)(2,1)S(1)}, bf16[1,640,256]{2,1,0:T(8,128)(2,1)S(1)}, u32[]{:S(2)}, u32[]{:S(2)}) collective-permute-start(bf16[1,640,256]{2,1,0:T(8,128)(2,1)S(1)} %get-tuple-element.40.refs_0_), channel_id=1, source_target_pairs={{0,2},{1,3},{2,0},{3,1},{4,6},{5,7},{6,4},{7,5},{8,10},{9,11},{10,... | collective-permute-start | bytes 983048 | tf_op jit(solution)/shard_map/ppermute | solution.py:272
  27.0 12.2 %collective-permute-start.10 = (bf16[1,640,256]{2,1,0:T(8,128)(2,1)S(1)}, bf16[1,640,256]{2,1,0:T(8,128)(2,1)S(1)}, u32[]{:S(2)}, u32[]{:S(2)}) collective-permute-start(bf16[1,640,256]{2,1,0:T(8,128)(2,1)S(1)} %get-tuple-element.40.refs_0_), channel_id=1, source_target_pairs={{0,1},{1,0},{2,3},{3,2},{4,5},{5,4},{6,7},{7,6},{8,9},{9,8},{10,11... | collective-permute-start | bytes 983048 | tf_op jit(solution)/shard_map/ppermute | solution.py:269
  28.6 1.7 %collective-permute-start.7 = (bf16[2,384,256]{2,1,0:T(8,128)(2,1)S(1)}, bf16[2,384,256]{2,1,0:T(8,128)(2,1)S(1)}, u32[]{:S(2)}, u32[]{:S(2)}) collective-permute-start(bf16[2,384,256]{2,1,0:T(8,128)(2,1)S(1)} %collective-permute-done.6.refs_2_), channel_id=1, source_target_pairs={{0,1},{1,0},{2,3},{3,2},{4,5},{5,4},{6,7},{7,6},{8,9},{9,8},{10,11... | collective-permute-start | bytes 1179656 | tf_op jit(solution)/shard_map/ppermute | solution.py:269
  31.6 10.6 %collective-permute-start.9 = (bf16[1,384,256]{2,1,0:T(8,128)(2,1)S(1)}, bf16[1,384,256]{2,1,0:T(8,128)(2,1)S(1)}, u32[]{:S(2)}, u32[]{:S(2)}) collective-permute-start(bf16[1,384,256]{2,1,0:T(8,128)(2,1)S(1)} %get-tuple-element.47.refs_0_), channel_id=1, source_target_pairs={{0,2},{1,3},{2,0},{3,1},{4,6},{5,7},{6,4},{7,5},{8,10},{9,11},{10,... | collective-permute-start | bytes 589832 | tf_op jit(solution)/shard_map/ppermute | solution.py:272
  33.4 7.0 %collective-permute-start.13 = (bf16[1,128,256]{2,1,0:T(8,128)(2,1)S(1)}, bf16[1,128,256]{2,1,0:T(8,128)(2,1)S(1)}, u32[]{:S(2)}, u32[]{:S(2)}) collective-permute-start(bf16[1,128,256]{2,1,0:T(8,128)(2,1)S(1)} %get-tuple-element.53), channel_id=1, source_target_pairs={{0,4},{4,8},{8,12},{12,16},{16,20},{20,24},{24,28},{28,0},{1,5},{5... | collective-permute-start | bytes 196616 | tf_op jit(solution)/shard_map/ppermute | solution.py:275
  34.9 5.7 %collective-permute-start.14 = (bf16[1,128,256]{2,1,0:T(8,128)(2,1)S(1)}, bf16[1,128,256]{2,1,0:T(8,128)(2,1)S(1)}, u32[]{:S(2)}, u32[]{:S(2)}) collective-permute-start(bf16[1,128,256]{2,1,0:T(8,128)(2,1)S(1)} %get-tuple-element.54), channel_id=1, source_target_pairs={{4,0},{8,4},{12,8},{16,12},{20,16},{24,20},{28,24},{0,28},{5,1},{9... | collective-permute-start | bytes 196616 | tf_op jit(solution)/shard_map/ppermute | solution.py:276
  38.1 2.4 %collective-permute-start.12 = (bf16[1,640,256]{2,1,0:T(8,128)(2,1)S(1)}, bf16[1,640,256]{2,1,0:T(8,128)(2,1)S(1)}, u32[]{:S(2)}, u32[]{:S(2)}) collective-permute-start(bf16[1,640,256]{2,1,0:T(8,128)(2,1)S(1)} %collective-permute-done.11.refs_2_), channel_id=1, source_target_pairs={{0,1},{1,0},{2,3},{3,2},{4,5},{5,4},{6,7},{7,6},{8,9},{9,8},{10,11... | collective-permute-start | bytes 983048 | tf_op jit(solution)/shard_map/ppermute | solution.py:269
  39.2 3.1 %collective-permute-start.8 = (bf16[1,384,256]{2,1,0:T(8,128)(2,1)S(1)}, bf16[1,384,256]{2,1,0:T(8,128)(2,1)S(1)}, u32[]{:S(2)}, u32[]{:S(2)}) collective-permute-start(bf16[1,384,256]{2,1,0:T(8,128)(2,1)S(1)} %get-tuple-element.47.refs_0_), channel_id=1, source_target_pairs={{0,1},{1,0},{2,3},{3,2},{4,5},{5,4},{6,7},{7,6},{8,9},{9,8},{10,11... | collective-permute-start | bytes 589832 | tf_op jit(solution)/shard_map/ppermute | solution.py:269
  42.2 1.5 %collective-permute-start.15 = (bf16[1,384,256]{2,1,0:T(8,128)(2,1)S(1)}, bf16[1,384,256]{2,1,0:T(8,128)(2,1)S(1)}, u32[]{:S(2)}, u32[]{:S(2)}) collective-permute-start(bf16[1,384,256]{2,1,0:T(8,128)(2,1)S(1)} %collective-permute-done.9.refs_2_), channel_id=1, source_target_pairs={{0,1},{1,0},{2,3},{3,2},{4,5},{5,4},{6,7},{7,6},{8,9},{9,8},{10,11... | collective-permute-start | bytes 589832 | tf_op jit(solution)/shard_map/ppermute | solution.py:269
